TPU v7x, 128 devices: a whole 4x4x4 slice. The times are simulated.
128 devices in a mesh: space: 16 (over y_lo, x, core), mem: 8 (over y_hi, z).
Axes of the slice: x: 4, y: 4 (y_hi: 2, y_lo: 2; y = y_hi * 2 + y_lo), z: 4, core: 2. Of those that a mesh axis runs over, the one named last changes fastest.
Arguments:
- prior_ensemble: bfloat16 [64, 80, 256, 128], P('mem', None, 'space'), may hold values from -6 to 6
- initial_kernel_taps: bfloat16 [9, 80, 80], replicated, may hold values from -0.21875 to 0.21875
- latter_kernel_taps: bfloat16 [9, 80, 80], replicated, may hold values from -0.21875 to 0.21875
- observed_cells: int32 [16, 1024], P('space'), may hold values from 0 to 491519
- observed_count: int32 [16], P('space'), may hold values from 512 to 1024, as said below
- local_radius: int32 [16], P('space'), may hold values from 8 to 32
- observed_value: float32 [16, 1024], P('space'), may hold values from -6 to 6
- error_variance: float32 [16, 1024], P('space'), may hold values from 5.12 to 51.2
Outputs:
- analysis: bfloat16 [64, 80, 256, 128], P('mem', None, 'space')
Inputs may be any that keep to these rules, and one draw needn't show every extreme that they name: observed_count reaches 1024 on some tile of every draw.
All inputs are finite; a program needn't handle non-finite values.
Results may differ from a plain program's by a relative error of at most 0.0064.
Values may be sent and summed in bfloat16 or wider, within the bound.
No kernel may reach another device: no remote copies, remote signals or barrier semaphores. Data moves between devices by JAX's collectives and lax.ppermute only.
A program may use at most 320 MiB of HBM per device.

v0:
```python
import jax
import jax.numpy as jnp
from jax import lax
from jax.experimental import pallas as pl
from jax.experimental.pallas import tpu as pltpu
from jax.sharding import PartitionSpec as P

NS_ITERS = 4
STEP_SIZE = 0.5
HALO = 4


def gelu(x):
    c = 0.7978845608028654
    return 0.5 * x * (1.0 + jnp.tanh(c * (x + 0.044715 * (x * x * x))))


def shifted_sum(p, lane):
    below = pltpu.roll(p[0:80], 1, axis=1)
    above = pltpu.roll(p[160:240], 127, axis=1)
    return p[80:160] + jnp.where(lane == 0, 0.0, below) + jnp.where(lane == 127, 0.0, above)


def conv_columns(source, taps, columns, emit):
    lane = lax.broadcasted_iota(jnp.int32, (80, 128), 1)
    for k in range(0, columns, 2):
        window = jnp.concatenate(
            [source[pl.ds(80 * k, 240), :], source[pl.ds(80 * (k + 1), 240), :]], axis=1
        )
        partial = jnp.dot(taps, window, preferred_element_type=jnp.float32)
        emit(k, shifted_sum(partial[:, :128], lane))
        emit(k + 1, shifted_sum(partial[:, 128:], lane))


def forecast_kernel(
    rows, shifts, own, left, right, first_taps, second_taps, out, picked, v, h, s, rate, fields
):
    m = pl.program_id(0)
    v[0:320, :] = left[0].reshape(320, 128)
    v[320:1600, :] = own[0].reshape(1280, 128)
    v[1600:1920, :] = right[0].reshape(320, 128)
    taps_a = first_taps[...]
    taps_b = second_taps[...]

    def put_hidden(x, value):
        h[pl.ds(80 * x, 80), :] = gelu(value).astype(jnp.bfloat16)

    def put_section(x, value):
        base = v[pl.ds(80 * (x + 2), 80), :].astype(jnp.float32)
        s[pl.ds(80 * x, 80), :] = (base + STEP_SIZE * value).astype(jnp.bfloat16)
        if 2 <= x < 18:
            rate[pl.ds(80 * (x - 2), 80), :] = base + 0.5 * STEP_SIZE * value

    def put_forecast(x, value):
        cells = rate[pl.ds(80 * x, 80), :] + 0.5 * STEP_SIZE * value
        cells = cells.astype(jnp.bfloat16).astype(jnp.float32)
        fields[pl.ds(640 * x + m, 80, stride=8), :] = cells

    conv_columns(v, taps_a, 22, put_hidden)
    conv_columns(h, taps_b, 20, put_section)
    conv_columns(s, taps_a, 18, put_hidden)
    conv_columns(h, taps_b, 16, put_forecast)

    @pl.when(m == pl.num_programs(0) - 1)
    def _():
        out[...] = fields[...].astype(jnp.bfloat16).reshape(out.shape)
        lane = lax.broadcasted_iota(jnp.int32, (8, 128), 1)

        def block(b, carry):
            acc = jnp.zeros((8, 128), jnp.float32)
            for j in range(128):
                row = pl.multiple_of(rows[b * 128 + j], 8)
                cell = pltpu.roll(fields[pl.ds(row, 8), :], shifts[b * 128 + j], axis=1)
                acc = jnp.where(lane == j, cell, acc)
            picked[pl.ds(pl.multiple_of(b * 8, 8), 8), :] = acc
            return carry

        lax.fori_loop(0, picked.shape[0] // 8, block, 0)


def forecast(rows, shifts, own, left, right, first_taps, second_taps):
    members = own.shape[0]
    whole = lambda shape: pl.BlockSpec(shape, lambda i: (0,) * len(shape))
    slots = rows.shape[0]
    return pl.pallas_call(
        forecast_kernel,
        grid=(members,),
        in_specs=[
            pl.BlockSpec(memory_space=pltpu.SMEM),
            pl.BlockSpec(memory_space=pltpu.SMEM),
            pl.BlockSpec((1, 16, 80, 128), lambda i: (i, 0, 0, 0)),
            pl.BlockSpec((1, HALO, 80, 128), lambda i: (i, 0, 0, 0)),
            pl.BlockSpec((1, HALO, 80, 128), lambda i: (i, 0, 0, 0)),
            whole((240, 240)),
            whole((240, 240)),
        ],
        out_specs=[whole((16, 80, 8, 128)), whole((slots // 16, 128))],
        out_shape=[
            jax.ShapeDtypeStruct((16, 80, 8, 128), jnp.bfloat16),
            jax.ShapeDtypeStruct((slots // 16, 128), jnp.float32),
        ],
        scratch_shapes=[
            pltpu.VMEM((1920, 128), jnp.bfloat16),
            pltpu.VMEM((1760, 128), jnp.bfloat16),
            pltpu.VMEM((1600, 128), jnp.bfloat16),
            pltpu.VMEM((1280, 128), jnp.float32),
            pltpu.VMEM((16 * 80 * 8, 128), jnp.float32),
        ],
        compiler_params=pltpu.CompilerParams(vmem_limit_bytes=40 << 20),
        cost_estimate=pl.CostEstimate(
            flops=16_000_000_000, bytes_accessed=8_000_000, transcendentals=4_000_000
        ),
    )(rows, shifts, own, left, right, first_taps, second_taps)


def mix_kernel(parts, weights, out):
    w = weights[...]
    depth = parts.shape[2]
    for x in range(2):
        for k in range(0, depth, 8):
            centers = []
            halves = []
            for half in range(2):
                stack = []
                for q in range(4):
                    c = k + 4 * half + q
                    cells = parts[:, x, c].astype(jnp.float32)
                    center = jnp.sum(jnp.sum(cells, axis=0), axis=0, keepdims=True) * (1.0 / 64.0)
                    centers.append(center)
                    stack.append((cells.reshape(64, 128) - center).astype(jnp.bfloat16))
                halves.append(jnp.concatenate(stack, axis=0))
            mixed = jnp.dot(
                w, jnp.concatenate(halves, axis=1), preferred_element_type=jnp.float32
            )
            for half in range(2):
                for q in range(4):
                    c = k + 4 * half + q
                    value = mixed[64 * q : 64 * q + 64, 128 * half : 128 * half + 128]
                    value = value + centers[4 * half + q]
                    out[:, x, c] = value.astype(jnp.bfloat16).reshape(8, 8, 128)


def mix(parts, weights):
    depth = 16
    spec = pl.BlockSpec((8, 2, depth, 8, 128), lambda i: (0, 0, i, 0, 0))
    return pl.pallas_call(
        mix_kernel,
        grid=(80 // depth,),
        in_specs=[spec, pl.BlockSpec((256, 256), lambda i: (0, 0))],
        out_specs=spec,
        out_shape=jax.ShapeDtypeStruct((8, 2, 80, 8, 128), jnp.bfloat16),
        compiler_params=pltpu.CompilerParams(vmem_limit_bytes=40 << 20),
        cost_estimate=pl.CostEstimate(
            flops=700_000_000, bytes_accessed=5_300_000, transcendentals=0
        ),
    )(parts, weights)


def taps_matrix(taps):
    return taps.reshape(3, 3, 80, 80).transpose(1, 2, 0, 3).reshape(240, 240)


def ring(cells, step):
    count = lax.axis_size("space")
    return lax.ppermute(cells, "space", [(i, (i + step) % count) for i in range(count)])


def ensemble_transform(member_obs, weight, observed):
    members = member_obs.shape[0]
    model_obs = member_obs.astype(jnp.float32)
    center = jnp.mean(model_obs, axis=0)
    spread = model_obs - center
    weighted = spread * weight[None, :]
    gram_matrix = jnp.dot(weighted, spread.T, precision=lax.Precision.HIGHEST)
    right_side = jnp.dot(weighted, observed - center, precision=lax.Precision.HIGHEST)
    identity_mat = jnp.eye(members, dtype=jnp.float32)
    system = (members - 1.0) * identity_mat + gram_matrix
    norm_bound = members - 1.0 + jnp.sqrt(jnp.sum(gram_matrix * gram_matrix))
    iterate = system / norm_bound
    root_inv = identity_mat
    for sweep_index in range(NS_ITERS):
        factor = 1.5 * identity_mat - 0.5 * jnp.dot(
            root_inv, iterate, precision=lax.Precision.HIGHEST
        )
        iterate = jnp.dot(iterate, factor, precision=lax.Precision.HIGHEST)
        root_inv = jnp.dot(factor, root_inv, precision=lax.Precision.HIGHEST)
    inverse = jnp.dot(root_inv, root_inv, precision=lax.Precision.HIGHEST) / norm_bound
    shift_weights = jnp.dot(inverse, right_side, precision=lax.Precision.HIGHEST)
    return (shift_weights[:, None] + jnp.sqrt((members - 1.0) / norm_bound) * root_inv).astype(
        jnp.bfloat16
    )


def observation_weight(cells, live_count, radius, variance):
    lon = cells // 128 % 48
    distance = lon.astype(jnp.float32) - (16 + 0.5 * 15)
    scaled = distance / radius.astype(jnp.float32)
    taper = jnp.exp(-0.5 * scaled * scaled)
    slot_ids = jnp.arange(cells.shape[0], dtype=jnp.int32)
    return jnp.where(slot_ids < live_count, taper / variance, jnp.float32(0.0))


def per_device(
    prior_ensemble,
    initial_kernel_taps,
    latter_kernel_taps,
    observed_cells,
    observed_count,
    local_radius,
    observed_value,
    error_variance,
):
    own = jnp.swapaxes(prior_ensemble, 1, 2)
    left = ring(own[:, 16 - HALO :], 1)
    right = ring(own[:, :HALO], -1)
    cells = observed_cells[0]
    left_cells = ring(cells, 1)
    right_cells = ring(cells, -1)

    lists = jnp.stack([left_cells, cells, right_cells])
    lon = lists // 128 % 48
    here = lon // 16 == jnp.array([2, 1, 0], jnp.int32)[:, None]
    rows = jnp.where(here, (lon % 16 * 80 + lists // 6144) * 8, 0).reshape(-1)
    slot = jnp.arange(cells.shape[0], dtype=jnp.int32)
    shifts = ((slot - lists) & 127).reshape(-1)

    fields, picked = forecast(
        rows,
        shifts,
        own,
        left,
        right,
        taps_matrix(initial_kernel_taps),
        taps_matrix(latter_kernel_taps),
    )
    picked = picked.astype(jnp.bfloat16).reshape(3, 8, 8, 128)
    from_left = ring(picked[2], 1)
    from_right = ring(picked[0], -1)
    part = (cells // 128 % 48 // 16).reshape(8, 1, 128)
    obs = jnp.where(part == 0, from_left, jnp.where(part == 1, picked[1], from_right))
    everyone = lax.all_to_all(
        jnp.broadcast_to(obs[None], (8, 8, 8, 128)), "mem", split_axis=0, concat_axis=0, tiled=True
    )
    member_obs = everyone.reshape(8, 8, 8, 128).transpose(0, 2, 1, 3).reshape(64, 1024)
    weight = observation_weight(cells, observed_count[0], local_radius[0], error_variance[0])
    transform = ensemble_transform(member_obs, weight, observed_value[0])
    blocks = (
        jnp.eye(4, dtype=jnp.bfloat16)[:, None, :, None] * transform.T[None, :, None, :]
    ).reshape(256, 256)

    parts = lax.all_to_all(
        fields.reshape(8, 2, 80, 8, 128), "mem", split_axis=0, concat_axis=0, tiled=True
    )
    mixed = mix(parts, blocks)
    back = lax.all_to_all(mixed, "mem", split_axis=0, concat_axis=0, tiled=True)
    return back.reshape(16, 80, 8, 128).transpose(2, 1, 0, 3)


def solution(mesh):
    return jax.shard_map(
        per_device,
        mesh=mesh,
        in_specs=(
            P("mem", None, "space", None),
            P(),
            P(),
            P("space", None),
            P("space"),
            P("space"),
            P("space", None),
            P("space", None),
        ),
        out_specs=P("mem", None, "space", None),
        check_vma=False,
    )
```

profile of v0, /device:TPU:6, one launch (start us, length us, event | category | flops | bytes accessed | tf_op | source)
XLA Modules:
  0.0 147.2 jit_solution(11178822750486227665)
XLA Ops:
  0.0 2.4 %copy.30 = bf16[8,80,16,128]{3,1,2,0:T(8,128)(2,1)S(1)} copy(bf16[8,80,16,128]{3,2,1,0:T(8,128)(2,1)} %param.9) | data formatting | bytes 5242880 | tf_op args[0]
  2.5 1.2 fusion.47
  3.6 1.7 %collective-permute-start.3 = (bf16[8,4,80,128]{3,2,1,0:T(8,128)(2,1)}, bf16[8,4,80,128]{3,2,1,0:T(8,128)(2,1)}, u32[]{:S(2)}, u32[]{:S(2)}) collective-permute-start(bf16[8,4,80,128]{3,2,1,0:T(8,128)(2,1)} %get-tuple-element.11), channel_id=1, source_target_pairs={{0,120},{8,0},{16,8},{24,16},{32,24},{40,32},{48,40},{56,48},{64,5... | collective-permute-start | bytes 1966088 | tf_op jit(solution)/shard_map/ppermute | solution.py:165
  5.4 1.7 %collective-permute-start.1 = (s32[1024]{0:T(1024)S(1)}, s32[1024]{0:T(1024)S(1)}, u32[]{:S(2)}, u32[]{:S(2)}) collective-permute-start(s32[1024]{0:T(1024)S(1)} %bitcast.104), channel_id=1, source_target_pairs={{0,120},{8,0},{16,8},{24,16},{32,24},{40,32},{48,40},{56,48},{64,5... | collective-permute-start | bytes 12296 | tf_op jit(solution)/shard_map/ppermute | solution.py:165
  8.4 0.8 copy.32
  9.2 1.1 reshape.168.first_taps
  10.4 1.7 %copy.31 = bf16[3,3,80,80]{3,0,2,1:T(4,128)(2,1)} copy(bf16[3,3,80,80]{3,2,1,0:T(8,128)(2,1)} %bitcast.102) | data formatting | bytes 230400 | tf_op jit(solution)/shard_map/reshape | solution.py:160
  12.1 1.1 reshape.170.second_taps
  13.2 0.7 collective-permute-done
  14.5 0.7 pad_add_fusion
  15.8 0.8 subtract_and_fusion
  16.6 25.4 %shard_map.91 = (bf16[16,80,8,128]{3,2,1,0:T(8,128)(2,1)S(1)}, f32[192,128]{1,0:T(8,128)S(1)}) custom-call(s32[3072]{0:T(1024)S(1)} %get-tuple-element.16.rows, s32[3072]{0:T(1024)S(1)} %get-tuple-element.15.shifts, bf16[8,16,80,128]{3,2,1,0:T(8,128)(2,1)S(1)} %bitcast.96, bf16[8,4,80,128]{3,2,1,0:T(8,128)(2,1)S(1)} %collective-permute-done.2.left, ...), custom_call_target="tpu_custom_call" | custom-call | flops 16000000000 | bytes 8000000 | tf_op jit(solution)/shard_map/pallas_call | solution.py:85
  42.0 1.5 %copy-done = bf16[16,80,8,128]{3,2,1,0:T(8,128)(2,1)} copy-done((bf16[16,80,8,128]{3,2,1,0:T(8,128)(2,1)}, bf16[16,80,8,128]{3,2,1,0:T(8,128)(2,1)S(1)}, u32[]{:S(2)}) %copy-start) | copy-done | bytes 2621464
  43.5 3.8 %collective-permute-start.4 = (bf16[8,8,128]{2,1,0:T(8,128)(2,1)S(1)}, bf16[8,8,128]{2,1,0:T(8,128)(2,1)S(1)}, u32[]{:S(2)}, u32[]{:S(2)}) collective-permute-start(bf16[8,8,128]{2,1,0:T(8,128)(2,1)S(1)} %get-tuple-element.14), channel_id=1, source_target_pairs={{0,8},{8,16},{16,24},{24,32},{32,40},{40,48},{48,56},{56,64},{64,7... | collective-permute-start | bytes 49160 | tf_op jit(solution)/shard_map/ppermute | solution.py:165
  48.6 0.7 collective-permute-done.5
  50.0 7.7 %all-to-all-start.1 = ((bf16[8,8,8,128]{3,2,1,0:T(8,128)(2,1)}), bf16[8,8,8,128]{3,2,1,0:T(8,128)(2,1)S(1)}, u32[]{:S(2)}, u32[]{:S(2)}) async-start(bf16[8,8,8,128]{3,2,1,0:T(8,128)(2,1)} %broadcast_in_dim.34), calls=%async_computation.1 | async-start | bytes 262144 | tf_op jit(solution)/shard_map/all_to_all | solution.py:241
  57.7 0.7 compare_select_fusion
  58.5 7.3 %all-to-all-done.1 = bf16[8,8,8,128]{3,2,1,0:T(8,128)(2,1)S(1)} async-done(((bf16[8,8,8,128]{3,2,1,0:T(8,128)(2,1)}), bf16[8,8,8,128]{3,2,1,0:T(8,128)(2,1)S(1)}, u32[]{:S(2)}, u32[]{:S(2)}) %all-to-all-start.1) | async-done | bytes 131104 | tf_op jit(solution)/shard_map/all_to_all | solution.py:241
  65.8 3.8 %all-to-all-start = ((bf16[8,2,80,8,128]{4,3,2,1,0:T(8,128)(2,1)}), bf16[8,2,80,8,128]{4,3,2,1,0:T(8,128)(2,1)S(1)}, u32[]{:S(2)}, u32[]{:S(2)}) async-start(bf16[8,2,80,8,128]{4,3,2,1,0:T(8,128)(2,1)} %bitcast.97), calls=%async_computation | async-start | bytes 5242880 | tf_op jit(solution)/shard_map/all_to_all | solution.py:251
  69.6 1.1 multiply_reduce_fusion
  74.6 27.5 %all-to-all-done.parts = bf16[8,2,80,8,128]{4,3,2,1,0:T(8,128)(2,1)S(1)} async-done(((bf16[8,2,80,8,128]{4,3,2,1,0:T(8,128)(2,1)}), bf16[8,2,80,8,128]{4,3,2,1,0:T(8,128)(2,1)S(1)}, u32[]{:S(2)}, u32[]{:S(2)}) %all-to-all-start) | async-done | bytes 2621472 | tf_op jit(solution)/shard_map/all_to_all | solution.py:251
  102.1 2.4 %shard_map.92 = bf16[8,2,80,8,128]{4,3,2,1,0:T(8,128)(2,1)S(1)} custom-call(bf16[8,2,80,8,128]{4,3,2,1,0:T(8,128)(2,1)S(1)} %all-to-all-done.parts, bf16[256,256]{1,0:T(8,128)(2,1)S(1)} %mul.121.weights), custom_call_target="tpu_custom_call" | custom-call | flops 700000000 | bytes 5300000 | tf_op jit(solution)/shard_map/pallas_call | solution.py:146
  104.5 39.6 %all_to_all.15 = bf16[8,2,80,8,128]{4,3,2,1,0:T(8,128)(2,1)S(1)} all-to-all(bf16[8,2,80,8,128]{4,3,2,1,0:T(8,128)(2,1)S(1)} %shard_map.92), channel_id=1, replica_groups=mesh['space'=16,'mem'=8] {'mem'}, dimensions={0} | all-to-all | bytes 5242880 | tf_op jit(solution)/shard_map/all_to_all | solution.py:255
  144.1 3.2 %copy.29 = bf16[16,80,8,128]{3,0,1,2:T(8,128)(2,1)} copy(bf16[16,80,8,128]{3,2,1,0:T(8,128)(2,1)S(1)} %bitcast.98) | data formatting | bytes 5242880 | tf_op jit(solution)/shard_map/reshape | solution.py:256
  (56 shorter events, 6.3 us)
Async XLA Ops:
  2.4 3.0 %copy-start.2 = (s32[1,1024]{1,0:T(1,128)S(1)}, s32[1,1024]{1,0:T(1,128)}, u32[]{:S(2)}) copy-start(s32[1,1024]{1,0:T(1,128)} %param.12) | copy-start | bytes 12292
  2.4 5.3 %copy-start.7 = (s32[3]{0:T(128)S(1)}, s32[3]{0:T(128)}, u32[]{:S(2)}) copy-start(s32[3]{0:T(128)} %constant.109.clone) | copy-start | bytes 40
  2.4 6.0 %copy-start.1 = (bf16[9,80,80]{2,1,0:T(8,128)(2,1)S(1)}, bf16[9,80,80]{2,1,0:T(8,128)(2,1)}, u32[]{:S(2)}) copy-start(bf16[9,80,80]{2,1,0:T(8,128)(2,1)} %param.10) | copy-start | bytes 345604
  3.6 12.9 %collective-permute-start.2 = (bf16[8,4,80,128]{3,2,1,0:T(8,128)(2,1)}, bf16[8,4,80,128]{3,2,1,0:T(8,128)(2,1)S(1)}, u32[]{:S(2)}, u32[]{:S(2)}) collective-permute-start(bf16[8,4,80,128]{3,2,1,0:T(8,128)(2,1)} %get-tuple-element.12), channel_id=1, source_target_pairs={{0,8},{8,16},{16,24},{24,32},{32,40},{40,48},{48,56},{56,64},{64,7... | collective-permute-start | bytes 1966088 | tf_op jit(solution)/shard_map/ppermute | solution.py:165
  3.6 12.9 %collective-permute-start.3 = (bf16[8,4,80,128]{3,2,1,0:T(8,128)(2,1)}, bf16[8,4,80,128]{3,2,1,0:T(8,128)(2,1)}, u32[]{:S(2)}, u32[]{:S(2)}) collective-permute-start(bf16[8,4,80,128]{3,2,1,0:T(8,128)(2,1)} %get-tuple-element.11), channel_id=1, source_target_pairs={{0,120},{8,0},{16,8},{24,16},{32,24},{40,32},{48,40},{56,48},{64,5... | collective-permute-start | bytes 1966088 | tf_op jit(solution)/shard_map/ppermute | solution.py:165
  5.4 8.5 %collective-permute-start = (s32[1024]{0:T(1024)S(1)}, s32[1024]{0:T(1024)S(1)}, u32[]{:S(2)}, u32[]{:S(2)}) collective-permute-start(s32[1024]{0:T(1024)S(1)} %bitcast.103), channel_id=1, source_target_pairs={{0,8},{8,16},{16,24},{24,32},{32,40},{40,48},{48,56},{56,64},{64,7... | collective-permute-start | bytes 12296 | tf_op jit(solution)/shard_map/ppermute | solution.py:165
  5.4 8.5 %collective-permute-start.1 = (s32[1024]{0:T(1024)S(1)}, s32[1024]{0:T(1024)S(1)}, u32[]{:S(2)}, u32[]{:S(2)}) collective-permute-start(s32[1024]{0:T(1024)S(1)} %bitcast.104), channel_id=1, source_target_pairs={{0,120},{8,0},{16,8},{24,16},{32,24},{40,32},{48,40},{56,48},{64,5... | collective-permute-start | bytes 12296 | tf_op jit(solution)/shard_map/ppermute | solution.py:165
  13.9 0.6 copy-start.5
  13.9 0.6 copy-start.6
  16.6 30.7 %copy-start.3 = (s32[8,128]{1,0:T(8,128)S(1)}, s32[8,128]{1,0:T(8,128)}, u32[]{:S(2)}) copy-start(s32[8,128]{1,0:T(8,128)} %get-tuple-element.10) | copy-start | bytes 12292
  16.6 32.8 %copy-start.4 = (pred[8,128]{1,0:T(8,128)(4,1)S(1)}, pred[8,128]{1,0:T(8,128)(4,1)}, u32[]{:S(2)}) copy-start(pred[8,128]{1,0:T(8,128)(4,1)} %get-tuple-element.9) | copy-start | bytes 3076
  42.0 1.5 %copy-start = (bf16[16,80,8,128]{3,2,1,0:T(8,128)(2,1)}, bf16[16,80,8,128]{3,2,1,0:T(8,128)(2,1)S(1)}, u32[]{:S(2)}) copy-start(bf16[16,80,8,128]{3,2,1,0:T(8,128)(2,1)S(1)} %get-tuple-element.7) | copy-start | bytes 7864324
  43.5 5.2 %collective-permute-start.4 = (bf16[8,8,128]{2,1,0:T(8,128)(2,1)S(1)}, bf16[8,8,128]{2,1,0:T(8,128)(2,1)S(1)}, u32[]{:S(2)}, u32[]{:S(2)}) collective-permute-start(bf16[8,8,128]{2,1,0:T(8,128)(2,1)S(1)} %get-tuple-element.14), channel_id=1, source_target_pairs={{0,8},{8,16},{16,24},{24,32},{32,40},{40,48},{48,56},{56,64},{64,7... | collective-permute-start | bytes 49160 | tf_op jit(solution)/shard_map/ppermute | solution.py:165
  47.3 2.1 %collective-permute-start.5 = (bf16[8,8,128]{2,1,0:T(8,128)(2,1)S(1)}, bf16[8,8,128]{2,1,0:T(8,128)(2,1)S(1)}, u32[]{:S(2)}, u32[]{:S(2)}) collective-permute-start(bf16[8,8,128]{2,1,0:T(8,128)(2,1)S(1)} %get-tuple-element.13), channel_id=1, source_target_pairs={{0,120},{8,0},{16,8},{24,16},{32,24},{40,32},{48,40},{56,48},{64,5... | collective-permute-start | bytes 49160 | tf_op jit(solution)/shard_map/ppermute | solution.py:165
  50.0 15.7 %all-to-all-start.1 = ((bf16[8,8,8,128]{3,2,1,0:T(8,128)(2,1)}), bf16[8,8,8,128]{3,2,1,0:T(8,128)(2,1)S(1)}, u32[]{:S(2)}, u32[]{:S(2)}) async-start(bf16[8,8,8,128]{3,2,1,0:T(8,128)(2,1)} %broadcast_in_dim.34), calls=%async_computation.1 | async-start | bytes 262144 | tf_op jit(solution)/shard_map/all_to_all | solution.py:241
  65.8 7.7 %copy-start.8 = (f32[1,1024]{1,0:T(1,128)S(1)}, f32[1,1024]{1,0:T(1,128)}, u32[]{:S(2)}) copy-start(f32[1,1024]{1,0:T(1,128)} %param.15) | copy-start | bytes 12292
  65.8 36.3 %all-to-all-start = ((bf16[8,2,80,8,128]{4,3,2,1,0:T(8,128)(2,1)}), bf16[8,2,80,8,128]{4,3,2,1,0:T(8,128)(2,1)S(1)}, u32[]{:S(2)}, u32[]{:S(2)}) async-start(bf16[8,2,80,8,128]{4,3,2,1,0:T(8,128)(2,1)} %bitcast.97), calls=%async_computation | async-start | bytes 5242880 | tf_op jit(solution)/shard_map/all_to_all | solution.py:251
where the time goes:
time: 148 us; the launch traced here: 147 us
  blocking collectives  39.6 us (27%)
  waiting for transfers between devices  36.2 us (24%)
  Pallas kernels  27.8 us (19%)
  starting transfers between devices  18.7 us (13%)
  local copies, waits for them, and re-layouts  15.9 us (11%)
  matrix products  3.47 us (2%)
  other arithmetic  3.15 us (2%)
  between operations  2.42 us (2%)
    all_to_all x1, blocking collectives, per_device(): back = lax.all_to_all(mixed, 'mem', split_axis=0, concat_axis=0, tiled=True)  39.6 us
    all_to_all x1, waiting for transfers between devices, per_device(): lax.all_to_all(fields.reshape(8, 2, 80, 8, 128), 'mem', split_axis=0, con...  27.5 us
    pallas_call x1, Pallas kernels, forecast(): pl.pallas_call(forecast_kernel, grid=(members,), in_specs=[pl.BlockSpec(m...  25.4 us
    all_to_all x1, starting transfers between devices, per_device(): lax.all_to_all(jnp.broadcast_to(obs[None], (8, 8, 8, 128)), 'mem', split_...  7.66 us
    ppermute x6, starting transfers between devices, ring(): lax.ppermute(cells, 'space', [(i, (i + step) % count) for i in range(coun...  7.33 us
    all_to_all x1, waiting for transfers between devices, per_device(): lax.all_to_all(jnp.broadcast_to(obs[None], (8, 8, 8, 128)), 'mem', split_...  7.32 us
    reshape x4, local copies, waits for them, and re-layouts, taps_matrix(): return taps.reshape(3, 3, 80, 80).transpose(1, 2, 0, 3).reshape(240, 240)  4.73 us
    unnamed x19, local copies, waits for them, and re-layouts  4.52 us
  transfers between devices with their start and end apart: 8, of which 4 were waited for; matrix products, arithmetic and copies ran while one was open for 9% of the time, Pallas kernels for 0%

commit v1 on v0

v1 whole, which is shorter than its diff:
```python
import jax
import jax.numpy as jnp
from jax import lax
from jax.experimental import pallas as pl
from jax.experimental.pallas import tpu as pltpu
from jax.sharding import PartitionSpec as P

NS_ITERS = 4
STEP_SIZE = 0.5
HALO = 4
CH = 80
COLUMNS = (4, 5, 6, 7, 8, 9, 10, 11, 0, 1, 2, 3, 12, 13, 14, 15)


def vmem_params():
    return pltpu.CompilerParams(vmem_limit_bytes=40 << 20)


def gelu(x):
    c = 0.7978845608028654
    return 0.5 * x * (1.0 + jnp.tanh(c * (x + 0.044715 * (x * x * x))))


def shifted_sum(p, lane):
    below = pltpu.roll(p[0:80], 1, axis=1)
    above = pltpu.roll(p[160:240], 127, axis=1)
    return p[80:160] + jnp.where(lane == 0, 0.0, below) + jnp.where(lane == 127, 0.0, above)


def conv_columns(source, first, taps, columns, emit):
    lane = lax.broadcasted_iota(jnp.int32, (CH, 128), 1)
    for k in range(0, columns, 2):
        at = CH * (first + k)
        window = jnp.concatenate(
            [source[pl.ds(at, 3 * CH), :], source[pl.ds(at + CH, 3 * CH), :]], axis=1
        )
        partial = jnp.dot(taps, window, preferred_element_type=jnp.float32)
        emit(k, shifted_sum(partial[:, :128], lane))
        emit(k + 1, shifted_sum(partial[:, 128:], lane))


def build_taps(taps, matrix):
    for b in range(3):
        row = jnp.concatenate([taps[3 * a + b].astype(jnp.float32) for a in range(3)], axis=1)
        matrix[pl.ds(CH * b, CH), :] = row.astype(jnp.bfloat16)


def inner_kernel(own, first_taps, second_taps, out, halves, rates, taps_a, taps_b, h, s, g, rate, fields):
    m = pl.program_id(0)

    @pl.when(m == 0)
    def _():
        build_taps(first_taps, taps_a)
        build_taps(second_taps, taps_b)

    a = taps_a[...]
    b = taps_b[...]
    v = own.at[0]

    def put_first(k, value):
        h[pl.ds(CH * k, CH), :] = gelu(value).astype(jnp.bfloat16)

    def put_section(k, value):
        base = v[pl.ds(CH * (k + 2), CH), :].astype(jnp.float32)
        s[pl.ds(CH * k, CH), :] = (base + STEP_SIZE * value).astype(jnp.bfloat16)
        rate[pl.ds(CH * k, CH), :] = base + 0.5 * STEP_SIZE * value

    def put_second(k, value):
        g[pl.ds(CH * k, CH), :] = gelu(value).astype(jnp.bfloat16)

    def put_forecast(k, value):
        cells = rate[pl.ds(CH * (k + 2), CH), :] + 0.5 * STEP_SIZE * value
        fields[pl.ds(8 * CH * k + m, CH, stride=8), :] = cells

    conv_columns(v, 0, a, 14, put_first)
    conv_columns(h, 0, b, 12, put_section)
    conv_columns(s, 0, a, 10, put_second)
    conv_columns(g, 0, b, 8, put_forecast)
    for k, (ref, left, right) in enumerate(((h, 0, 12), (s, 0, 10), (g, 0, 8))):
        halves[0, pl.ds(2 * CH * k, 2 * CH), :] = ref[pl.ds(CH * left, 2 * CH), :]
        halves[0, pl.ds(2 * CH * (k + 3), 2 * CH), :] = ref[pl.ds(CH * right, 2 * CH), :]
    rates[0, pl.ds(0, 2 * CH), :] = rate[pl.ds(0, 2 * CH), :]
    rates[0, pl.ds(2 * CH, 2 * CH), :] = rate[pl.ds(10 * CH, 2 * CH), :]

    @pl.when(m == pl.num_programs(0) - 1)
    def _():
        out[...] = fields[...].astype(jnp.bfloat16).reshape(out.shape)


def edge_kernel(
    inner, cells, first, second, left, right, low, high, halves, rates, out, rows, shifts,
    v, h, s, g, rate, fields,
):
    m = pl.program_id(0)
    a = first[...]
    b = second[...]

    @pl.when(m == 0)
    def _():
        slot = lax.broadcasted_iota(jnp.int32, (8, 128), 1)
        for k in range(3):
            cell = cells[k]
            strip = cell >> 7
            channel = (strip * 43691) >> 21
            lon = strip - 48 * channel - 16 * (2 - k)
            column = jnp.where(lon < 4, lon + 8, jnp.where(lon < 12, lon - 4, lon))
            here = (lon >= 0) & (lon < 16)
            rows[k] = jnp.where(here, column * CH + channel, 0)
            shifts[k] = (slot - cell) & 127

    for side, (x, y) in enumerate(((left, low), (high, right))):
        v[pl.ds(8 * CH * side, 4 * CH), :] = x[0]
        v[pl.ds(8 * CH * side + 4 * CH, 4 * CH), :] = y[0]
    for k, ref in enumerate((h, s, g)):
        ref[pl.ds(4 * CH, 2 * CH), :] = halves[0, pl.ds(2 * CH * k, 2 * CH), :]
        ref[pl.ds(6 * CH, 2 * CH), :] = halves[0, pl.ds(2 * CH * (k + 3), 2 * CH), :]

    def hidden(ref, at):
        def put(k, value):
            ref[pl.ds(CH * (at + k), CH), :] = gelu(value).astype(jnp.bfloat16)

        return put

    def section_left(k, value):
        base = v[pl.ds(CH * (k + 2), CH), :].astype(jnp.float32)
        s[pl.ds(CH * k, CH), :] = (base + STEP_SIZE * value).astype(jnp.bfloat16)
        if k >= 2:
            rate[pl.ds(CH * (k - 2), CH), :] = base + 0.5 * STEP_SIZE * value

    def section_right(k, value):
        base = v[pl.ds(CH * (k + 10), CH), :].astype(jnp.float32)
        s[pl.ds(CH * (8 + k), CH), :] = (base + STEP_SIZE * value).astype(jnp.bfloat16)
        if k < 2:
            rate[pl.ds(CH * (k + 2), CH), :] = base + 0.5 * STEP_SIZE * value

    def forecast_left(k, value):
        start = rate[pl.ds(CH * k, CH), :] if k < 2 else rates[0, pl.ds(CH * (k - 2), CH), :]
        fields[pl.ds(8 * CH * k + m, CH, stride=8), :] = start + 0.5 * STEP_SIZE * value

    def forecast_right(k, value):
        start = rates[0, pl.ds(CH * (k + 2), CH), :] if k < 2 else rate[pl.ds(CH * k, CH), :]
        fields[pl.ds(8 * CH * (k + 4) + m, CH, stride=8), :] = start + 0.5 * STEP_SIZE * value

    conv_columns(v, 0, a, 4, hidden(h, 0))
    conv_columns(v, 10, a, 4, hidden(h, 8))
    conv_columns(h, 0, b, 4, section_left)
    conv_columns(h, 6, b, 4, section_right)
    conv_columns(s, 0, a, 4, hidden(g, 0))
    conv_columns(s, 6, a, 4, hidden(g, 8))
    conv_columns(g, 0, b, 4, forecast_left)
    conv_columns(g, 6, b, 4, forecast_right)

    @pl.when(m == pl.num_programs(0) - 1)
    def _():
        out[...] = fields[...].astype(jnp.bfloat16).reshape(out.shape)


def whole(shape):
    return pl.BlockSpec(shape, lambda i: (0,) * len(shape))


def member(shape, at=0):
    return pl.BlockSpec((1,) + shape, lambda i: (i, at) + (0,) * (len(shape) - 1))


def inner_forecast(own, first_taps, second_taps):
    members = own.shape[0]
    bf16, f32 = jnp.bfloat16, jnp.float32
    return pl.pallas_call(
        inner_kernel,
        grid=(members,),
        in_specs=[member((16 * CH, 128)), whole((9, CH, CH)), whole((9, CH, CH))],
        out_specs=[
            whole((8, CH, 8, 128)),
            member((12 * CH, 128)),
            member((4 * CH, 128)),
            whole((3 * CH, 3 * CH)),
            whole((3 * CH, 3 * CH)),
        ],
        out_shape=[
            jax.ShapeDtypeStruct((16, CH, 8, 128), bf16),
            jax.ShapeDtypeStruct((members, 12 * CH, 128), bf16),
            jax.ShapeDtypeStruct((members, 4 * CH, 128), f32),
            jax.ShapeDtypeStruct((3 * CH, 3 * CH), bf16),
            jax.ShapeDtypeStruct((3 * CH, 3 * CH), bf16),
        ],
        scratch_shapes=[
            pltpu.VMEM((14 * CH, 128), bf16),
            pltpu.VMEM((12 * CH, 128), bf16),
            pltpu.VMEM((10 * CH, 128), bf16),
            pltpu.VMEM((12 * CH, 128), f32),
            pltpu.VMEM((8 * CH * 8, 128), f32),
        ],
        compiler_params=vmem_params(),
        cost_estimate=pl.CostEstimate(
            flops=12_000_000_000, bytes_accessed=8_000_000, transcendentals=2_000_000
        ),
    )(own, first_taps, second_taps)


def edge_forecast(inner, cells, first, second, left, right, own, halves, rates):
    members = own.shape[0]
    bf16, f32 = jnp.bfloat16, jnp.float32
    return pl.pallas_call(
        edge_kernel,
        grid=(members,),
        in_specs=[
            pl.BlockSpec(memory_space=pl.ANY),
            whole((3, 8, 128)),
            whole((3 * CH, 3 * CH)),
            whole((3 * CH, 3 * CH)),
            member((4 * CH, 128)),
            member((4 * CH, 128)),
            member((4 * CH, 128), 0),
            member((4 * CH, 128), 3),
            member((12 * CH, 128)),
            member((4 * CH, 128)),
        ],
        out_specs=[
            pl.BlockSpec((8, CH, 8, 128), lambda i: (1, 0, 0, 0)),
            whole((3, 8, 128)),
            whole((3, 8, 128)),
        ],
        out_shape=[
            jax.ShapeDtypeStruct((16, CH, 8, 128), bf16),
            jax.ShapeDtypeStruct((3, 8, 128), jnp.int32),
            jax.ShapeDtypeStruct((3, 8, 128), jnp.int32),
        ],
        scratch_shapes=[
            pltpu.VMEM((16 * CH, 128), bf16),
            pltpu.VMEM((12 * CH, 128), bf16),
            pltpu.VMEM((12 * CH, 128), bf16),
            pltpu.VMEM((12 * CH, 128), bf16),
            pltpu.VMEM((4 * CH, 128), f32),
            pltpu.VMEM((8 * CH * 8, 128), f32),
        ],
        input_output_aliases={0: 0},
        compiler_params=vmem_params(),
        cost_estimate=pl.CostEstimate(
            flops=9_000_000_000, bytes_accessed=8_000_000, transcendentals=2_000_000
        ),
    )(inner, cells, first, second, left, right, own, own, halves, rates)


def gather_kernel(rows, shifts, fields, picked):
    lane = lax.broadcasted_iota(jnp.int32, (8, 128), 1)

    def block(b, carry):
        acc = jnp.zeros((8, 128), jnp.float32)
        for j in range(128):
            cell = fields[rows[b, j]].astype(jnp.float32)
            acc = jnp.where(lane == j, pltpu.roll(cell, shifts[b, j], axis=1), acc)
        picked[b] = acc.astype(jnp.bfloat16)
        return carry

    lax.fori_loop(0, picked.shape[0], block, 0)


def gather(rows, shifts, fields):
    blocks = rows.shape[0]
    return pl.pallas_call(
        gather_kernel,
        in_specs=[
            pl.BlockSpec(memory_space=pltpu.SMEM),
            pl.BlockSpec(memory_space=pltpu.SMEM),
            pl.BlockSpec(memory_space=pltpu.VMEM),
        ],
        out_specs=pl.BlockSpec(memory_space=pltpu.VMEM),
        out_shape=jax.ShapeDtypeStruct((blocks, 8, 128), jnp.bfloat16),
        compiler_params=vmem_params(),
        cost_estimate=pl.CostEstimate(
            flops=10_000_000, bytes_accessed=3_000_000, transcendentals=0
        ),
    )(rows, shifts, fields)


def transform_kernel(here, pair, ahead, across, behind, cells, numbers, observed, variance, out, stack):
    f32 = jnp.float32
    exact = lax.Precision.HIGHEST
    depth = numbers[0]
    half = numbers[1]
    for z in range(4):
        step = (z - depth) & 3
        for y in range(2):
            other = (y ^ half) & 1
            rows = pl.ds(8 * (4 * y + z), 8)
            for block in range(8):
                lanes = pl.ds(128 * block, 128)

                def take(ref, pick=None):
                    return ref[other, block].astype(f32)

                value = jnp.where(
                    step == 0,
                    jnp.where(other == 0, here[block].astype(f32), pair[block].astype(f32)),
                    jnp.where(step == 1, take(ahead), jnp.where(step == 2, take(across), take(behind))),
                )
                stack[rows, lanes] = value
    model_obs = stack[...]
    center = jnp.sum(model_obs, axis=0, keepdims=True) * (1.0 / 64.0)
    spread = model_obs - center
    cell = cells[...]
    strip = cell >> 7
    lon = strip - 48 * ((strip * 43691) >> 21)
    scaled = (lon.astype(f32) - 23.5) / numbers[3].astype(f32)
    taper = jnp.exp(-0.5 * scaled * scaled)
    slot = lax.broadcasted_iota(jnp.int32, cell.shape, 1)
    weight = jnp.where(slot < numbers[2], taper / variance[...], 0.0)
    weighted = spread * weight

    def product(x, y):
        return jnp.dot(x, y, precision=exact, preferred_element_type=f32)

    gram = lax.dot_general(
        weighted, spread, (((1,), (1,)), ((), ())), precision=exact, preferred_element_type=f32
    )
    right_side = jnp.sum(weighted * (observed[...] - center), axis=1, keepdims=True)
    i = lax.broadcasted_iota(jnp.int32, (64, 64), 0)
    j = lax.broadcasted_iota(jnp.int32, (64, 64), 1)
    eye = jnp.where(i == j, 1.0, 0.0).astype(f32)
    norm = 63.0 + jnp.sqrt(jnp.sum(jnp.sum(gram * gram, axis=1, keepdims=True), axis=0, keepdims=True))
    iterate = (63.0 * eye + gram) / norm
    root = 1.5 * eye - 0.5 * iterate
    iterate = product(iterate, root)
    for sweep in range(1, NS_ITERS):
        factor = 1.5 * eye - 0.5 * product(root, iterate)
        if sweep < NS_ITERS - 1:
            iterate = product(iterate, factor)
        root = product(factor, root)
    wide = jnp.broadcast_to(right_side, (64, 128))
    shift = product(root, product(root, wide)) / norm
    out[...] = (shift[:, :64] + jnp.sqrt(63.0 / norm) * root).astype(jnp.bfloat16)


def transform_of(pieces, cells, numbers, observed, variance):
    vmem = pl.BlockSpec(memory_space=pltpu.VMEM)
    smem = pl.BlockSpec(memory_space=pltpu.SMEM)
    return pl.pallas_call(
        transform_kernel,
        in_specs=[vmem] * 6 + [smem] + [vmem] * 2,
        out_specs=vmem,
        out_shape=jax.ShapeDtypeStruct((64, 64), jnp.bfloat16),
        scratch_shapes=[pltpu.VMEM((64, 1024), jnp.float32)],
        compiler_params=vmem_params(),
        cost_estimate=pl.CostEstimate(
            flops=100_000_000, bytes_accessed=500_000, transcendentals=1000
        ),
    )(*pieces, cells, numbers, observed, variance)


def mix_kernel(parts, weights, out):
    w = weights[...]
    depth = parts.shape[2]
    for x in range(2):
        for k in range(0, depth, 8):
            centers = []
            halves = []
            for half in range(2):
                stack = []
                for q in range(4):
                    c = k + 4 * half + q
                    cells = parts[:, x, c].astype(jnp.float32)
                    center = jnp.sum(jnp.sum(cells, axis=0), axis=0, keepdims=True) * (1.0 / 64.0)
                    centers.append(center)
                    stack.append((cells.reshape(64, 128) - center).astype(jnp.bfloat16))
                halves.append(jnp.concatenate(stack, axis=0))
            mixed = jnp.dot(
                w, jnp.concatenate(halves, axis=1), preferred_element_type=jnp.float32
            )
            for half in range(2):
                for q in range(4):
                    c = k + 4 * half + q
                    value = mixed[64 * q : 64 * q + 64, 128 * half : 128 * half + 128]
                    value = value + centers[4 * half + q]
                    out[:, x, c] = value.astype(jnp.bfloat16).reshape(8, 8, 128)


def mix(parts, weights):
    depth = 16
    spec = pl.BlockSpec((8, 2, depth, 8, 128), lambda i: (0, 0, i, 0, 0))
    return pl.pallas_call(
        mix_kernel,
        grid=(CH // depth,),
        in_specs=[spec, whole((256, 256))],
        out_specs=spec,
        out_shape=jax.ShapeDtypeStruct((8, 2, CH, 8, 128), jnp.bfloat16),
        compiler_params=vmem_params(),
        cost_estimate=pl.CostEstimate(
            flops=700_000_000, bytes_accessed=5_300_000, transcendentals=0
        ),
    )(parts, weights)


def order_kernel(cells, out, scratch):
    depth = cells.shape[1]
    for slot, column in enumerate(COLUMNS):
        for c in range(depth):
            value = cells[slot, c].astype(jnp.float32)
            scratch[pl.ds(128 * c + column, 8, stride=16), :] = value
    for c in range(depth):
        value = scratch[pl.ds(128 * c, 128), :].astype(jnp.bfloat16)
        out[:, c] = value.reshape(8, 16, 128)


def order(cells):
    depth = 16
    return pl.pallas_call(
        order_kernel,
        grid=(CH // depth,),
        in_specs=[pl.BlockSpec((16, depth, 8, 128), lambda i: (0, i, 0, 0))],
        out_specs=pl.BlockSpec((8, depth, 16, 128), lambda i: (0, i, 0, 0)),
        out_shape=jax.ShapeDtypeStruct((8, CH, 16, 128), jnp.bfloat16),
        scratch_shapes=[pltpu.VMEM((depth * 128, 128), jnp.float32)],
        compiler_params=vmem_params(),
        cost_estimate=pl.CostEstimate(
            flops=0, bytes_accessed=5_300_000, transcendentals=0
        ),
    )(cells)


def ring(cells, step):
    count = lax.axis_size("space")
    return lax.ppermute(cells, "space", [(i, (i + step) % count) for i in range(count)])


def depth_ring(cells, step):
    return lax.ppermute(
        cells, "mem", [(4 * y + (z + step) % 4, 4 * y + z) for y in range(2) for z in range(4)]
    )


def per_device(
    prior_ensemble,
    initial_kernel_taps,
    latter_kernel_taps,
    observed_cells,
    observed_count,
    local_radius,
    observed_value,
    error_variance,
):
    members = prior_ensemble.shape[0]
    flat = lambda x: jnp.swapaxes(x, 1, 2).reshape(members, -1, 128)
    left = ring(flat(prior_ensemble[:, :, 16 - HALO :]), 1)
    right = ring(flat(prior_ensemble[:, :, :HALO]), -1)
    cells = observed_cells.reshape(8, 128)
    lists = jnp.stack([ring(cells, 1), cells, ring(cells, -1)])
    own = flat(prior_ensemble)

    inner, halves, rates, first, second = inner_forecast(
        own, initial_kernel_taps, latter_kernel_taps
    )
    fields, rows, shifts = edge_forecast(
        inner, lists, first, second, left, right, own, halves, rates
    )
    parts = lax.all_to_all(
        fields.reshape(8, 2, CH, 8, 128), "mem", split_axis=0, concat_axis=0, tiled=True
    )

    picked = gather(
        rows.reshape(24, 128), shifts.reshape(24, 128), fields.reshape(16 * CH, 8, 128)
    ).reshape(3, 8, 8, 128)
    from_left = ring(picked[2], 1)
    from_right = ring(picked[0], -1)
    part = (cells // 128 % 48 // 16).reshape(8, 1, 128)
    here = jnp.where(part == 0, from_left, jnp.where(part == 1, picked[1], from_right))
    pair = lax.ppermute(here, "mem", [(i, i ^ 4) for i in range(8)])
    both = jnp.stack([here, pair])
    group = lax.axis_index("mem").astype(jnp.int32)
    numbers = jnp.stack([group % 4, group // 4, observed_count[0], local_radius[0]])
    transform = transform_of(
        (here, pair, depth_ring(both, 1), depth_ring(both, 2), depth_ring(both, 3)),
        observed_cells,
        numbers,
        observed_value,
        error_variance,
    )
    blocks = (
        jnp.eye(4, dtype=jnp.bfloat16)[:, None, :, None] * transform.T[None, :, None, :]
    ).reshape(256, 256)
    mixed = mix(parts, blocks)
    back = lax.all_to_all(mixed, "mem", split_axis=0, concat_axis=0, tiled=True)
    return order(back.reshape(16, CH, 8, 128))


def solution(mesh):
    return jax.shard_map(
        per_device,
        mesh=mesh,
        in_specs=(
            P("mem", None, "space", None),
            P(),
            P(),
            P("space", None),
            P("space"),
            P("space"),
            P("space", None),
            P("space", None),
        ),
        out_specs=P("mem", None, "space", None),
        check_vma=False,
    )
```

time: 148 us -> 131 us (0.89)
  waiting for transfers between devices: 36.2 us -> 21.1 us
  Pallas kernels: 27.8 us -> 42.5 us
  local copies, waits for them, and re-layouts: 15.9 us -> 7.1 us
  blocking collectives: 39.6 us -> 35.8 us
  matrix products: 3.47 us -> 0 us
  starting transfers between devices: 18.7 us -> 22 us
  other arithmetic: 3.15 us -> 0.31 us
    all_to_all x2 -> x1, waiting for transfers between devices: 34.8 us -> 0.01 us  [per_device(): lax.all_to_all(fields.reshape(8, 2, CH, 8, 128), 'mem', split_axis=0, con...]
    ppermute x0 -> x4, waiting for transfers between devices: none -> 17.3 us  [the longest x1 13.1 us: per_device(): pair = lax.ppermute(here, 'mem', [(i, i ^ 4) for i in range(8)])]
    pallas_call x2 -> x6, Pallas kernels: 27.8 us -> 42.5 us  [the longest x1 13.3 us: inner_forecast(): pl.pallas_call(inner_kernel, grid=(members,), in_specs=[member((16 * CH,...]
    ppermute x0 -> x4, starting transfers between devices: none -> 8.6 us  [the longest x3 4.38 us: depth_ring(): lax.ppermute(cells, 'mem', [(4 * y + (z + step) % 4, 4 * y + z) for y in...]
    reshape x5 -> x0, local copies, waits for them, and re-layouts: 7.91 us -> none  [the longest x4 4.73 us: taps_matrix(): return taps.reshape(3, 3, 80, 80).transpose(1, 2, 0, 3).reshape(240, 240)]
    all_to_all x1, blocking collectives: 39.6 us -> 35.8 us  [per_device(): back = lax.all_to_all(mixed, 'mem', split_axis=0, concat_axis=0, tiled=True)]
    all_to_all x2 -> x1, starting transfers between devices: 11.4 us -> 7.94 us  [per_device(): lax.all_to_all(fields.reshape(8, 2, CH, 8, 128), 'mem', split_axis=0, con...]
    dot_general x15 -> x0, matrix products: 3.47 us -> none  [the longest x1 1.05 us: ensemble_transform(): gram_matrix = jnp.dot(weighted, spread.T, precision=lax.Precision.HIGHEST)]
  transfers between devices with their start and end apart: 8 -> 11, of which waited for: 4 -> 6; matrix products, arithmetic and copies ran while one was open for 9% -> 3% of each run, Pallas kernels for 0% -> 18%
where the time goes in v1:
time: 131 us; the launch traced here: 130 us
  Pallas kernels  42.5 us (32%)
  blocking collectives  35.8 us (27%)
  starting transfers between devices  22 us (17%)
  waiting for transfers between devices  21.1 us (16%)
  local copies, waits for them, and re-layouts  7.1 us (5%)
  between operations  1.5 us (1%)
    all_to_all x1, blocking collectives, per_device(): back = lax.all_to_all(mixed, 'mem', split_axis=0, concat_axis=0, tiled=True)  35.8 us
    pallas_call x1, Pallas kernels, inner_forecast(): pl.pallas_call(inner_kernel, grid=(members,), in_specs=[member((16 * CH,...  13.3 us
    ppermute x1, waiting for transfers between devices, per_device(): pair = lax.ppermute(here, 'mem', [(i, i ^ 4) for i in range(8)])  13.1 us
    pallas_call x1, Pallas kernels, edge_forecast(): pl.pallas_call(edge_kernel, grid=(members,), in_specs=[pl.BlockSpec(memor...  12.3 us
    all_to_all x1, starting transfers between devices, per_device(): lax.all_to_all(fields.reshape(8, 2, CH, 8, 128), 'mem', split_axis=0, con...  7.94 us
    pallas_call x1, Pallas kernels, gather(): pl.pallas_call(gather_kernel, in_specs=[pl.BlockSpec(memory_space=pltpu.S...  7.46 us
    ppermute x6, starting transfers between devices, ring(): lax.ppermute(cells, 'space', [(i, (i + step) % count) for i in range(coun...  5.43 us
    ppermute x3, starting transfers between devices, depth_ring(): lax.ppermute(cells, 'mem', [(4 * y + (z + step) % 4, 4 * y + z) for y in...  4.38 us
  transfers between devices with their start and end apart: 11, of which 6 were waited for; matrix products, arithmetic and copies ran while one was open for 3% of the time, Pallas kernels for 18%

profile of v1, /device:TPU:6, one launch (start us, length us, event | category | flops | bytes accessed | tf_op | source)
XLA Modules:
  0.0 130.3 jit_solution(6340680308468315223)
XLA Ops:
  0.0 1.7 %collective-permute-start.1 = (s32[8,128]{1,0:T(8,128)}, s32[8,128]{1,0:T(8,128)S(1)}, u32[]{:S(2)}, u32[]{:S(2)}) collective-permute-start(s32[8,128]{1,0:T(8,128)} %bitcast.31), channel_id=1, source_target_pairs={{0,120},{8,0},{16,8},{24,16},{32,24},{40,32},{48,40},{56,48},{64,5... | collective-permute-start | bytes 12296 | tf_op jit(solution)/shard_map/ppermute | solution.py:423
  1.7 2.3 %slice_bitcast_fusion = (bf16[8,4,80,128]{3,1,2,0:T(4,128)(2,1)S(1)}, bf16[8,4,80,128]{3,1,2,0:T(4,128)(2,1)S(1)}) fusion(bf16[8,80,16,128]{3,2,1,0:T(8,128)(2,1)} %param.8), kind=kLoop, calls=%fused_computation | loop fusion | bytes 2621440 | tf_op jit(solution)/shard_map/transpose | solution.py:443
  4.4 1.8 %collective-permute-start.3 = (bf16[8,320,128]{2,1,0:T(8,128)(2,1)S(1)}, bf16[8,320,128]{2,1,0:T(8,128)(2,1)S(1)}, u32[]{:S(2)}, u32[]{:S(2)}) collective-permute-start(bf16[8,320,128]{2,1,0:T(8,128)(2,1)S(1)} %bitcast.39), channel_id=1, source_target_pairs={{0,120},{8,0},{16,8},{24,16},{32,24},{40,32},{48,40},{56,48},{64,5... | collective-permute-start | bytes 1966088 | tf_op jit(solution)/shard_map/ppermute | solution.py:423
  6.2 0.7 copy.10
  7.2 13.3 %shard_map.82 = (bf16[16,80,8,128]{3,2,1,0:T(8,128)(2,1)S(1)}, bf16[8,960,128]{2,1,0:T(8,128)(2,1)S(1)}, f32[8,320,128]{2,1,0:T(8,128)S(1)}, bf16[240,240]{1,0:T(8,128)(2,1)S(1)}, bf16[240,240]{1,0:T(8,128)(2,1)S(1)}) custom-call(bf16[8,1280,128]{2,1,0:T(8,128)(2,1)S(1)} %bitcast.25, bf16[9,80,80]{2,1,0:T(8,128)(2,1)S(1)} %copy-done.3, ...), custom_call_target="tpu_custom_call" | custom-call | flops 12000000000 | bytes 8000000 | tf_op jit(solution)/shard_map/pallas_call | solution.py:169
  20.5 12.3 %shard_map.83 = (bf16[16,80,8,128]{3,2,1,0:T(8,128)(2,1)S(1)}, s32[3,8,128]{2,1,0:T(8,128)S(1)}, s32[3,8,128]{2,1,0:T(8,128)S(1)}) custom-call(bf16[16,80,8,128]{3,2,1,0:T(8,128)(2,1)S(1)} %get-tuple-element.13.inner, s32[3,8,128]{2,1,0:T(8,128)S(1)} %pad_add_fusion.cells, ...), custom_call_target="tpu_custom_call", output_to_operand_aliasing={{0}: (0, {})} | custom-call | flops 8999999488 | bytes 8000000 | tf_op jit(solution)/shard_map/pallas_call | solution.py:204
  32.8 1.5 %copy-done = bf16[16,80,8,128]{3,2,1,0:T(8,128)(2,1)} copy-done((bf16[16,80,8,128]{3,2,1,0:T(8,128)(2,1)}, bf16[16,80,8,128]{3,2,1,0:T(8,128)(2,1)S(1)}, u32[]{:S(2)}) %copy-start) | copy-done | bytes 2621464
  34.3 7.9 %all-to-all-start = ((bf16[8,2,80,8,128]{4,3,2,1,0:T(8,128)(2,1)}), bf16[8,2,80,8,128]{4,3,2,1,0:T(8,128)(2,1)S(1)}, u32[]{:S(2)}, u32[]{:S(2)}) async-start(bf16[8,2,80,8,128]{4,3,2,1,0:T(8,128)(2,1)} %bitcast.22), calls=%async_computation | async-start | bytes 5242880 | tf_op jit(solution)/shard_map/all_to_all | solution.py:456
  42.3 1.8 %copy-done.1 = bf16[16,80,8,128]{3,2,1,0:T(8,128)(2,1)S(1)} copy-done((bf16[16,80,8,128]{3,2,1,0:T(8,128)(2,1)S(1)}, bf16[16,80,8,128]{3,2,1,0:T(8,128)(2,1)}, u32[]{:S(2)}) %copy-start.1) | copy-done | bytes 2621464
  44.1 7.5 %shard_map.84 = bf16[24,8,128]{2,1,0:T(8,128)(2,1)S(1)} custom-call(s32[24,128]{1,0:T(8,128)S(1)} %bitcast.35, s32[24,128]{1,0:T(8,128)S(1)} %bitcast.36, bf16[1280,8,128]{2,1,0:T(8,128)(2,1)S(1)} %bitcast.23), custom_call_target="tpu_custom_call" | custom-call | flops 10000000 | bytes 3000000 | tf_op jit(solution)/shard_map/pallas_call | solution.py:261
  51.6 1.5 %collective-permute-start.4 = (bf16[8,8,128]{2,1,0:T(8,128)(2,1)S(1)}, bf16[8,8,128]{2,1,0:T(8,128)(2,1)S(1)}, u32[]{:S(2)}, u32[]{:S(2)}) collective-permute-start(bf16[8,8,128]{2,1,0:T(8,128)(2,1)S(1)} %get-tuple-element.26), channel_id=1, source_target_pairs={{0,8},{8,16},{16,24},{24,32},{32,40},{40,48},{48,56},{56,64},{64,7... | collective-permute-start | bytes 49160 | tf_op jit(solution)/shard_map/ppermute | solution.py:423
  53.4 1.4 %collective-permute-done.4 = bf16[8,8,128]{2,1,0:T(8,128)(2,1)S(1)} collective-permute-done((bf16[8,8,128]{2,1,0:T(8,128)(2,1)S(1)}, bf16[8,8,128]{2,1,0:T(8,128)(2,1)S(1)}, u32[]{:S(2)}, u32[]{:S(2)}) %collective-permute-start.4) | collective-permute-done | bytes 16416 | tf_op jit(solution)/shard_map/ppermute | solution.py:423
  54.8 2.4 %collective-permute-done.5 = bf16[8,8,128]{2,1,0:T(8,128)(2,1)S(1)} collective-permute-done((bf16[8,8,128]{2,1,0:T(8,128)(2,1)S(1)}, bf16[8,8,128]{2,1,0:T(8,128)(2,1)S(1)}, u32[]{:S(2)}, u32[]{:S(2)}) %collective-permute-start.5) | collective-permute-done | bytes 16416 | tf_op jit(solution)/shard_map/ppermute | solution.py:423
  57.2 4.2 %collective-permute-start.6 = (bf16[8,8,128]{2,1,0:T(8,128)(2,1)S(1)}, bf16[8,8,128]{2,1,0:T(8,128)(2,1)S(1)}, u32[]{:S(2)}, u32[]{:S(2)}) collective-permute-start(bf16[8,8,128]{2,1,0:T(8,128)(2,1)S(1)} %fusion.here), channel_id=1, source_target_pairs={{0,4},{1,5},{2,6},{3,7},{4,0},{5,1},{6,2},{7,3},{8,12},{9,13},{10,... | collective-permute-start | bytes 49160 | tf_op jit(solution)/shard_map/ppermute | solution.py:467
  62.8 13.1 %collective-permute-done.6.pair = bf16[8,8,128]{2,1,0:T(8,128)(2,1)S(1)} collective-permute-done((bf16[8,8,128]{2,1,0:T(8,128)(2,1)S(1)}, bf16[8,8,128]{2,1,0:T(8,128)(2,1)S(1)}, u32[]{:S(2)}, u32[]{:S(2)}) %collective-permute-start.6) | collective-permute-done | bytes 16416 | tf_op jit(solution)/shard_map/ppermute | solution.py:467
  75.8 2.9 %collective-permute-start.7 = (bf16[2,8,8,128]{3,2,1,0:T(8,128)(2,1)S(1)}, bf16[2,8,8,128]{3,2,1,0:T(8,128)(2,1)S(1)}, u32[]{:S(2)}, u32[]{:S(2)}) collective-permute-start(bf16[2,8,8,128]{3,2,1,0:T(8,128)(2,1)S(1)} %pad_maximum_fusion), channel_id=1, source_target_pairs={{1,0},{2,1},{3,2},{0,3},{5,4},{6,5},{7,6},{4,7},{9,8},{10,9},{11,1... | collective-permute-start | bytes 98312 | tf_op jit(solution)/shard_map/ppermute | solution.py:427
  78.7 0.6 collective-permute-start.8
  79.3 0.9 collective-permute-start.9
  80.4 3.7 %collective-permute-done.8.across = bf16[2,8,8,128]{3,2,1,0:T(8,128)(2,1)S(1)} collective-permute-done((bf16[2,8,8,128]{3,2,1,0:T(8,128)(2,1)S(1)}, bf16[2,8,8,128]{3,2,1,0:T(8,128)(2,1)S(1)}, u32[]{:S(2)}, u32[]{:S(2)}) %collective-permute-start.8) | collective-permute-done | bytes 32800 | tf_op jit(solution)/shard_map/ppermute | solution.py:427
  84.1 0.4 collective-permute-done.9.behind
  84.5 2.8 %shard_map.85 = bf16[64,64]{1,0:T(8,128)(2,1)S(1)} custom-call(bf16[8,8,128]{2,1,0:T(8,128)(2,1)S(1)} %fusion.here, bf16[8,8,128]{2,1,0:T(8,128)(2,1)S(1)} %collective-permute-done.6.pair, bf16[2,8,8,128]{3,2,1,0:T(8,128)(2,1)S(1)} %collective-permute-done.7.ahead, bf16[2,8,8,128]{3,2,1,0:T(8,128)(2,1)S(1)} %collective-permute-done.8.across, ...), custom_call_target="tpu_custom_call" | custom-call | flops 100000000 | bytes 500000 | tf_op jit(solution)/shard_map/pallas_call | solution.py:338
  87.8 2.4 %shard_map.86 = bf16[8,2,80,8,128]{4,3,2,1,0:T(8,128)(2,1)S(1)} custom-call(bf16[8,2,80,8,128]{4,3,2,1,0:T(8,128)(2,1)S(1)} %all-to-all-done.parts, bf16[256,256]{1,0:T(8,128)(2,1)S(1)} %mul.20.weights), custom_call_target="tpu_custom_call" | custom-call | flops 700000000 | bytes 5300000 | tf_op jit(solution)/shard_map/pallas_call | solution.py:381
  90.2 35.8 %all_to_all.10 = bf16[8,2,80,8,128]{4,3,2,1,0:T(8,128)(2,1)S(1)} all-to-all(bf16[8,2,80,8,128]{4,3,2,1,0:T(8,128)(2,1)S(1)} %shard_map.86), channel_id=1, replica_groups=mesh['space'=16,'mem'=8] {'mem'}, dimensions={0} | all-to-all | bytes 5242880 | tf_op jit(solution)/shard_map/all_to_all | solution.py:482
  126.0 4.2 %shard_map.87 = bf16[8,80,16,128]{3,2,1,0:T(8,128)(2,1)} custom-call(bf16[16,80,8,128]{3,2,1,0:T(8,128)(2,1)S(1)} %bitcast.24), custom_call_target="tpu_custom_call" | custom-call | bytes 5300000 | tf_op jit(solution)/shard_map/pallas_call | solution.py:407
  (36 shorter events, 1.7 us)
Async XLA Ops:
  0.0 6.2 %copy-start.7 = (bf16[8,80,16,128]{3,2,1,0:T(8,128)(2,1)S(1)}, bf16[8,80,16,128]{3,2,1,0:T(8,128)(2,1)}, u32[]{:S(2)}) copy-start(bf16[8,80,16,128]{3,2,1,0:T(8,128)(2,1)} %param.8) | copy-start | bytes 7864324
  0.0 20.5 %collective-permute-start = (s32[8,128]{1,0:T(8,128)}, s32[8,128]{1,0:T(8,128)S(1)}, u32[]{:S(2)}, u32[]{:S(2)}) collective-permute-start(s32[8,128]{1,0:T(8,128)} %bitcast.30), channel_id=1, source_target_pairs={{0,8},{8,16},{16,24},{24,32},{32,40},{40,48},{48,56},{56,64},{64,7... | collective-permute-start | bytes 12296 | tf_op jit(solution)/shard_map/ppermute | solution.py:423
  0.0 20.5 %collective-permute-start.1 = (s32[8,128]{1,0:T(8,128)}, s32[8,128]{1,0:T(8,128)S(1)}, u32[]{:S(2)}, u32[]{:S(2)}) collective-permute-start(s32[8,128]{1,0:T(8,128)} %bitcast.31), channel_id=1, source_target_pairs={{0,120},{8,0},{16,8},{24,16},{32,24},{40,32},{48,40},{56,48},{64,5... | collective-permute-start | bytes 12296 | tf_op jit(solution)/shard_map/ppermute | solution.py:423
  4.2 16.3 %collective-permute-start.2 = (bf16[8,320,128]{2,1,0:T(8,128)(2,1)S(1)}, bf16[8,320,128]{2,1,0:T(8,128)(2,1)S(1)}, u32[]{:S(2)}, u32[]{:S(2)}) collective-permute-start(bf16[8,320,128]{2,1,0:T(8,128)(2,1)S(1)} %bitcast.38), channel_id=1, source_target_pairs={{0,8},{8,16},{16,24},{24,32},{32,40},{40,48},{48,56},{56,64},{64,7... | collective-permute-start | bytes 1966088 | tf_op jit(solution)/shard_map/ppermute | solution.py:423
  4.4 16.1 %collective-permute-start.3 = (bf16[8,320,128]{2,1,0:T(8,128)(2,1)S(1)}, bf16[8,320,128]{2,1,0:T(8,128)(2,1)S(1)}, u32[]{:S(2)}, u32[]{:S(2)}) collective-permute-start(bf16[8,320,128]{2,1,0:T(8,128)(2,1)S(1)} %bitcast.39), channel_id=1, source_target_pairs={{0,120},{8,0},{16,8},{24,16},{32,24},{40,32},{48,40},{56,48},{64,5... | collective-permute-start | bytes 1966088 | tf_op jit(solution)/shard_map/ppermute | solution.py:423
  6.2 0.9 copy-start.3
  6.2 1.0 copy-start.4
  7.2 13.3 %copy-start.2 = (s32[1,1024]{1,0:T(1,128)S(1)}, s32[1,1024]{1,0:T(1,128)}, u32[]{:S(2)}) copy-start(s32[1,1024]{1,0:T(1,128)} %cells.1) | copy-start | bytes 12292
  32.8 1.5 %copy-start = (bf16[16,80,8,128]{3,2,1,0:T(8,128)(2,1)}, bf16[16,80,8,128]{3,2,1,0:T(8,128)(2,1)S(1)}, u32[]{:S(2)}) copy-start(bf16[16,80,8,128]{3,2,1,0:T(8,128)(2,1)S(1)} %get-tuple-element.18) | copy-start | bytes 7864324
  34.3 53.5 %all-to-all-start = ((bf16[8,2,80,8,128]{4,3,2,1,0:T(8,128)(2,1)}), bf16[8,2,80,8,128]{4,3,2,1,0:T(8,128)(2,1)S(1)}, u32[]{:S(2)}, u32[]{:S(2)}) async-start(bf16[8,2,80,8,128]{4,3,2,1,0:T(8,128)(2,1)} %bitcast.22), calls=%async_computation | async-start | bytes 5242880 | tf_op jit(solution)/shard_map/all_to_all | solution.py:456
  42.3 42.2 %copy-start.5 = (f32[1,1024]{1,0:T(1,128)S(1)}, f32[1,1024]{1,0:T(1,128)}, u32[]{:S(2)}) copy-start(f32[1,1024]{1,0:T(1,128)} %observed.1) | copy-start | bytes 12292
  42.3 42.2 %copy-start.6 = (f32[1,1024]{1,0:T(1,128)S(1)}, f32[1,1024]{1,0:T(1,128)}, u32[]{:S(2)}) copy-start(f32[1,1024]{1,0:T(1,128)} %variance.1) | copy-start | bytes 12292
  42.3 1.8 %copy-start.1 = (bf16[16,80,8,128]{3,2,1,0:T(8,128)(2,1)S(1)}, bf16[16,80,8,128]{3,2,1,0:T(8,128)(2,1)}, u32[]{:S(2)}) copy-start(bf16[16,80,8,128]{3,2,1,0:T(8,128)(2,1)} %copy-done) | copy-start | bytes 7864324
  51.6 3.2 %collective-permute-start.4 = (bf16[8,8,128]{2,1,0:T(8,128)(2,1)S(1)}, bf16[8,8,128]{2,1,0:T(8,128)(2,1)S(1)}, u32[]{:S(2)}, u32[]{:S(2)}) collective-permute-start(bf16[8,8,128]{2,1,0:T(8,128)(2,1)S(1)} %get-tuple-element.26), channel_id=1, source_target_pairs={{0,8},{8,16},{16,24},{24,32},{32,40},{40,48},{48,56},{56,64},{64,7... | collective-permute-start | bytes 49160 | tf_op jit(solution)/shard_map/ppermute | solution.py:423
  53.0 4.2 %collective-permute-start.5 = (bf16[8,8,128]{2,1,0:T(8,128)(2,1)S(1)}, bf16[8,8,128]{2,1,0:T(8,128)(2,1)S(1)}, u32[]{:S(2)}, u32[]{:S(2)}) collective-permute-start(bf16[8,8,128]{2,1,0:T(8,128)(2,1)S(1)} %get-tuple-element.25), channel_id=1, source_target_pairs={{0,120},{8,0},{16,8},{24,16},{32,24},{40,32},{48,40},{56,48},{64,5... | collective-permute-start | bytes 49160 | tf_op jit(solution)/shard_map/ppermute | solution.py:423
  57.2 18.6 %collective-permute-start.6 = (bf16[8,8,128]{2,1,0:T(8,128)(2,1)S(1)}, bf16[8,8,128]{2,1,0:T(8,128)(2,1)S(1)}, u32[]{:S(2)}, u32[]{:S(2)}) collective-permute-start(bf16[8,8,128]{2,1,0:T(8,128)(2,1)S(1)} %fusion.here), channel_id=1, source_target_pairs={{0,4},{1,5},{2,6},{3,7},{4,0},{5,1},{6,2},{7,3},{8,12},{9,13},{10,... | collective-permute-start | bytes 49160 | tf_op jit(solution)/shard_map/ppermute | solution.py:467
  75.8 4.6 %collective-permute-start.7 = (bf16[2,8,8,128]{3,2,1,0:T(8,128)(2,1)S(1)}, bf16[2,8,8,128]{3,2,1,0:T(8,128)(2,1)S(1)}, u32[]{:S(2)}, u32[]{:S(2)}) collective-permute-start(bf16[2,8,8,128]{3,2,1,0:T(8,128)(2,1)S(1)} %pad_maximum_fusion), channel_id=1, source_target_pairs={{1,0},{2,1},{3,2},{0,3},{5,4},{6,5},{7,6},{4,7},{9,8},{10,9},{11,1... | collective-permute-start | bytes 98312 | tf_op jit(solution)/shard_map/ppermute | solution.py:427
  78.7 5.4 %collective-permute-start.8 = (bf16[2,8,8,128]{3,2,1,0:T(8,128)(2,1)S(1)}, bf16[2,8,8,128]{3,2,1,0:T(8,128)(2,1)S(1)}, u32[]{:S(2)}, u32[]{:S(2)}) collective-permute-start(bf16[2,8,8,128]{3,2,1,0:T(8,128)(2,1)S(1)} %pad_maximum_fusion), channel_id=1, source_target_pairs={{2,0},{3,1},{0,2},{1,3},{6,4},{7,5},{4,6},{5,7},{10,8},{11,9},{8,1... | collective-permute-start | bytes 98312 | tf_op jit(solution)/shard_map/ppermute | solution.py:427
  79.3 5.2 %collective-permute-start.9 = (bf16[2,8,8,128]{3,2,1,0:T(8,128)(2,1)S(1)}, bf16[2,8,8,128]{3,2,1,0:T(8,128)(2,1)S(1)}, u32[]{:S(2)}, u32[]{:S(2)}) collective-permute-start(bf16[2,8,8,128]{3,2,1,0:T(8,128)(2,1)S(1)} %pad_maximum_fusion), channel_id=1, source_target_pairs={{3,0},{0,1},{1,2},{2,3},{7,4},{4,5},{5,6},{6,7},{11,8},{8,9},{9,10... | collective-permute-start | bytes 98312 | tf_op jit(solution)/shard_map/ppermute | solution.py:427

commit v2 on v1

v2 whole, which is shorter than its diff:
```python
import jax
import jax.numpy as jnp
from jax import lax
from jax.experimental import pallas as pl
from jax.experimental.pallas import tpu as pltpu
from jax.sharding import PartitionSpec as P

NS_ITERS = 4
STEP_SIZE = 0.5
HALO = 4
CH = 80


def vmem_params():
    return pltpu.CompilerParams(vmem_limit_bytes=40 << 20)


def gelu(x):
    c = 0.7978845608028654
    return 0.5 * x * (1.0 + jnp.tanh(c * (x + 0.044715 * (x * x * x))))


def shifted_sum(p, lane):
    below = pltpu.roll(p[0:80], 1, axis=1)
    above = pltpu.roll(p[160:240], 127, axis=1)
    return p[80:160] + jnp.where(lane == 0, 0.0, below) + jnp.where(lane == 127, 0.0, above)


def conv_columns(source, first, taps, columns, emit):
    lane = lax.broadcasted_iota(jnp.int32, (CH, 128), 1)
    for k in range(0, columns, 2):
        at = CH * (first + k)
        window = jnp.concatenate(
            [source[pl.ds(at, 3 * CH), :], source[pl.ds(at + CH, 3 * CH), :]], axis=1
        )
        partial = jnp.dot(taps, window, preferred_element_type=jnp.float32)
        emit(k, shifted_sum(partial[:, :128], lane))
        emit(k + 1, shifted_sum(partial[:, 128:], lane))


def build_taps(taps, matrix):
    for b in range(3):
        row = jnp.concatenate([taps[3 * a + b].astype(jnp.float32) for a in range(3)], axis=1)
        matrix[pl.ds(CH * b, CH), :] = row.astype(jnp.bfloat16)


def inner_kernel(own, first_taps, second_taps, out, halves, rates, taps_a, taps_b, h, s, g, rate, fields):
    build_taps(first_taps, taps_a)
    build_taps(second_taps, taps_b)
    a = taps_a[...]
    b = taps_b[...]

    def one(m, carry):
        v = own.at[m]

        def put_first(k, value):
            h[pl.ds(CH * k, CH), :] = gelu(value).astype(jnp.bfloat16)

        def put_section(k, value):
            base = v[pl.ds(CH * (k + 2), CH), :].astype(jnp.float32)
            s[pl.ds(CH * k, CH), :] = (base + STEP_SIZE * value).astype(jnp.bfloat16)
            rate[pl.ds(CH * k, CH), :] = base + 0.5 * STEP_SIZE * value

        def put_second(k, value):
            g[pl.ds(CH * k, CH), :] = gelu(value).astype(jnp.bfloat16)

        def put_forecast(k, value):
            cells = rate[pl.ds(CH * (k + 2), CH), :] + 0.5 * STEP_SIZE * value
            fields[pl.ds(8 * CH * k + m, CH, stride=8), :] = cells

        conv_columns(v, 0, a, 14, put_first)
        conv_columns(h, 0, b, 12, put_section)
        conv_columns(s, 0, a, 10, put_second)
        conv_columns(g, 0, b, 8, put_forecast)
        for k, (ref, right) in enumerate(((h, 12), (s, 10), (g, 8))):
            halves[m, pl.ds(2 * CH * k, 2 * CH), :] = ref[pl.ds(0, 2 * CH), :]
            halves[m, pl.ds(2 * CH * (k + 3), 2 * CH), :] = ref[pl.ds(CH * right, 2 * CH), :]
        rates[m, pl.ds(0, 2 * CH), :] = rate[pl.ds(0, 2 * CH), :]
        rates[m, pl.ds(2 * CH, 2 * CH), :] = rate[pl.ds(10 * CH, 2 * CH), :]
        return carry

    lax.fori_loop(0, own.shape[0], one, 0)
    out[...] = fields[...].astype(jnp.bfloat16).reshape(out.shape)


def place_of(channel, lon, lat, part):
    slot = lax.broadcasted_iota(jnp.int32, (8, 128), 1)
    lon = lon - 16 * part
    column = jnp.where(lon < 4, lon + 8, jnp.where(lon < 12, lon - 4, lon))
    here = (lon >= 0) & (lon < 16)
    return jnp.where(here, (column * CH + channel) * 8, 0), (slot - lat) & 127


def edge_kernel(
    inner, cells, first, second, left, right, own, halves, rates, out, picked,
    v, h, s, g, rate, fields, places, rows, turns, sems,
):
    members = own.shape[0]
    a = first[...]
    b = second[...]
    digits = CH * HALO * members
    for k, source in enumerate((left, cells, right)):
        if k == 1:
            cell = source[...]
            strip = cell >> 7
            channel = (strip * 43691) >> 21
            parts = (channel, strip - 48 * channel, cell & 127)
        else:
            block = source[pl.ds(digits, 32), :].astype(jnp.float32).astype(jnp.int32)
            parts = (block[0:8], block[8:16], block[16:24])
        row, turn = place_of(*parts, 2 - k)
        places[0, pl.ds(8 * k, 8), :] = row
        places[1, pl.ds(8 * k, 8), :] = turn
    copies = [
        pltpu.make_async_copy(places.at[0], rows, sems.at[0]),
        pltpu.make_async_copy(places.at[1], turns, sems.at[1]),
    ]
    for copy in copies:
        copy.start()
    fields[pl.ds(0, 64 * CH), :] = inner[...].astype(jnp.float32).reshape(64 * CH, 128)

    def one(m, carry):
        halo = pl.ds(pl.multiple_of(CH * HALO * m, CH * HALO), CH * HALO)
        v[pl.ds(0, 4 * CH), :] = left[halo, :]
        v[pl.ds(4 * CH, 4 * CH), :] = own[m, pl.ds(0, 4 * CH), :]
        v[pl.ds(8 * CH, 4 * CH), :] = own[m, pl.ds(12 * CH, 4 * CH), :]
        v[pl.ds(12 * CH, 4 * CH), :] = right[halo, :]
        for k, ref in enumerate((h, s, g)):
            ref[pl.ds(4 * CH, 2 * CH), :] = halves[m, pl.ds(2 * CH * k, 2 * CH), :]
            ref[pl.ds(6 * CH, 2 * CH), :] = halves[m, pl.ds(2 * CH * (k + 3), 2 * CH), :]

        def hidden(ref, at):
            def put(k, value):
                ref[pl.ds(CH * (at + k), CH), :] = gelu(value).astype(jnp.bfloat16)

            return put

        def section_left(k, value):
            base = v[pl.ds(CH * (k + 2), CH), :].astype(jnp.float32)
            s[pl.ds(CH * k, CH), :] = (base + STEP_SIZE * value).astype(jnp.bfloat16)
            if k >= 2:
                rate[pl.ds(CH * (k - 2), CH), :] = base + 0.5 * STEP_SIZE * value

        def section_right(k, value):
            base = v[pl.ds(CH * (k + 10), CH), :].astype(jnp.float32)
            s[pl.ds(CH * (8 + k), CH), :] = (base + STEP_SIZE * value).astype(jnp.bfloat16)
            if k < 2:
                rate[pl.ds(CH * (k + 2), CH), :] = base + 0.5 * STEP_SIZE * value

        def put_field(column, start, value):
            value = (start + 0.5 * STEP_SIZE * value).astype(jnp.bfloat16).astype(jnp.float32)
            fields[pl.ds(8 * CH * (8 + column) + m, CH, stride=8), :] = value

        def forecast_left(k, value):
            start = rate[pl.ds(CH * k, CH), :] if k < 2 else rates[m, pl.ds(CH * (k - 2), CH), :]
            put_field(k, start, value)

        def forecast_right(k, value):
            start = rates[m, pl.ds(CH * (k + 2), CH), :] if k < 2 else rate[pl.ds(CH * k, CH), :]
            put_field(k + 4, start, value)

        conv_columns(v, 0, a, 4, hidden(h, 0))
        conv_columns(v, 10, a, 4, hidden(h, 8))
        conv_columns(h, 0, b, 4, section_left)
        conv_columns(h, 6, b, 4, section_right)
        conv_columns(s, 0, a, 4, hidden(g, 0))
        conv_columns(s, 6, a, 4, hidden(g, 8))
        conv_columns(g, 0, b, 4, forecast_left)
        conv_columns(g, 6, b, 4, forecast_right)
        return carry

    lax.fori_loop(0, members, one, 0)
    out[...] = fields[pl.ds(64 * CH, 64 * CH), :].astype(jnp.bfloat16).reshape(out.shape)
    for copy in copies:
        copy.wait()
    lane = lax.broadcasted_iota(jnp.int32, (8, 128), 1)

    def block(k, carry):
        acc = jnp.zeros((8, 128), jnp.float32)
        for j in range(128):
            cell = fields[pl.ds(pl.multiple_of(rows[k, j], 8), 8), :]
            acc = jnp.where(lane == j, pltpu.roll(cell, turns[k, j], axis=1), acc)
        picked[k] = acc.astype(jnp.bfloat16)
        return carry

    lax.fori_loop(0, picked.shape[0], block, 0)


def vmem():
    return pl.BlockSpec(memory_space=pltpu.VMEM)


def inner_forecast(own, first_taps, second_taps):
    members = own.shape[0]
    bf16, f32 = jnp.bfloat16, jnp.float32
    return pl.pallas_call(
        inner_kernel,
        in_specs=[vmem()] * 3,
        out_specs=[vmem()] * 5,
        out_shape=[
            jax.ShapeDtypeStruct((8, CH, 8, 128), bf16),
            jax.ShapeDtypeStruct((members, 12 * CH, 128), bf16),
            jax.ShapeDtypeStruct((members, 4 * CH, 128), f32),
            jax.ShapeDtypeStruct((3 * CH, 3 * CH), bf16),
            jax.ShapeDtypeStruct((3 * CH, 3 * CH), bf16),
        ],
        scratch_shapes=[
            pltpu.VMEM((14 * CH, 128), bf16),
            pltpu.VMEM((12 * CH, 128), bf16),
            pltpu.VMEM((10 * CH, 128), bf16),
            pltpu.VMEM((12 * CH, 128), f32),
            pltpu.VMEM((64 * CH, 128), f32),
        ],
        compiler_params=vmem_params(),
        cost_estimate=pl.CostEstimate(
            flops=12_000_000_000, bytes_accessed=8_000_000, transcendentals=2_000_000
        ),
    )(own, first_taps, second_taps)


def edge_forecast(inner, cells, first, second, left, right, own, halves, rates):
    bf16, f32 = jnp.bfloat16, jnp.float32
    return pl.pallas_call(
        edge_kernel,
        in_specs=[vmem()] * 9,
        out_specs=[vmem()] * 2,
        out_shape=[
            jax.ShapeDtypeStruct((8, CH, 8, 128), bf16),
            jax.ShapeDtypeStruct((24, 8, 128), bf16),
        ],
        scratch_shapes=[
            pltpu.VMEM((16 * CH, 128), bf16),
            pltpu.VMEM((12 * CH, 128), bf16),
            pltpu.VMEM((12 * CH, 128), bf16),
            pltpu.VMEM((12 * CH, 128), bf16),
            pltpu.VMEM((4 * CH, 128), f32),
            pltpu.VMEM((128 * CH, 128), f32),
            pltpu.VMEM((2, 24, 128), jnp.int32),
            pltpu.SMEM((24, 128), jnp.int32),
            pltpu.SMEM((24, 128), jnp.int32),
            pltpu.SemaphoreType.DMA((2,)),
        ],
        compiler_params=vmem_params(),
        cost_estimate=pl.CostEstimate(
            flops=9_000_000_000, bytes_accessed=8_000_000, transcendentals=2_000_000
        ),
    )(inner, cells, first, second, left, right, own, halves, rates)


def transform_kernel(here, pair, ahead, across, behind, cells, numbers, observed, variance, out, stack):
    f32 = jnp.float32
    exact = lax.Precision.HIGHEST
    depth = numbers[0]
    half = numbers[1]
    for z in range(4):
        step = (z - depth) & 3
        for y in range(2):
            other = (y ^ half) & 1
            rows = pl.ds(8 * (4 * y + z), 8)
            for block in range(8):
                lanes = pl.ds(128 * block, 128)

                def take(ref, pick=None):
                    return ref[other, block].astype(f32)

                value = jnp.where(
                    step == 0,
                    jnp.where(other == 0, here[block].astype(f32), pair[block].astype(f32)),
                    jnp.where(step == 1, take(ahead), jnp.where(step == 2, take(across), take(behind))),
                )
                stack[rows, lanes] = value
    model_obs = stack[...]
    center = jnp.sum(model_obs, axis=0, keepdims=True) * (1.0 / 64.0)
    spread = model_obs - center
    cell = cells[...]
    strip = cell >> 7
    lon = strip - 48 * ((strip * 43691) >> 21)
    scaled = (lon.astype(f32) - 23.5) / numbers[3].astype(f32)
    taper = jnp.exp(-0.5 * scaled * scaled)
    slot = lax.broadcasted_iota(jnp.int32, cell.shape, 1)
    weight = jnp.where(slot < numbers[2], taper / variance[...], 0.0)
    weighted = spread * weight

    def product(x, y):
        return jnp.dot(x, y, precision=exact, preferred_element_type=f32)

    gram = lax.dot_general(
        weighted, spread, (((1,), (1,)), ((), ())), precision=exact, preferred_element_type=f32
    )
    right_side = jnp.sum(weighted * (observed[...] - center), axis=1, keepdims=True)
    i = lax.broadcasted_iota(jnp.int32, (64, 64), 0)
    j = lax.broadcasted_iota(jnp.int32, (64, 64), 1)
    eye = jnp.where(i == j, 1.0, 0.0).astype(f32)
    norm = 63.0 + jnp.sqrt(jnp.sum(jnp.sum(gram * gram, axis=1, keepdims=True), axis=0, keepdims=True))
    iterate = (63.0 * eye + gram) / norm
    root = 1.5 * eye - 0.5 * iterate
    iterate = product(iterate, root)
    for sweep in range(1, NS_ITERS):
        factor = 1.5 * eye - 0.5 * product(root, iterate)
        if sweep < NS_ITERS - 1:
            iterate = product(iterate, factor)
        root = product(factor, root)
    wide = jnp.broadcast_to(right_side, (64, 128))
    shift = product(root, product(root, wide)) / norm
    transform = (shift[:, :64] + jnp.sqrt(63.0 / norm) * root).astype(jnp.bfloat16)
    i = lax.broadcasted_iota(jnp.int32, (64, 256), 0)
    j = lax.broadcasted_iota(jnp.int32, (64, 256), 1)
    for q in range(4):
        place = jnp.where(j == i + 64 * q, 1.0, 0.0).astype(jnp.bfloat16)
        turned = lax.dot_general(
            transform, place, (((0,), (0,)), ((), ())), preferred_element_type=f32
        )
        out[pl.ds(64 * q, 64), :] = turned.astype(jnp.bfloat16)


def transform_of(pieces, cells, numbers, observed, variance):
    smem = pl.BlockSpec(memory_space=pltpu.SMEM)
    return pl.pallas_call(
        transform_kernel,
        in_specs=[vmem()] * 6 + [smem] + [vmem()] * 2,
        out_specs=vmem(),
        out_shape=jax.ShapeDtypeStruct((256, 256), jnp.bfloat16),
        scratch_shapes=[pltpu.VMEM((64, 1024), jnp.float32)],
        compiler_params=vmem_params(),
        cost_estimate=pl.CostEstimate(
            flops=100_000_000, bytes_accessed=500_000, transcendentals=1000
        ),
    )(*pieces, cells, numbers, observed, variance)


def mix_kernel(inner, edge, weights, out):
    w = weights[...]

    def block(k, carry):
        for x, parts in enumerate((inner, edge)):
            centers = []
            halves = []
            for half in range(2):
                stack = []
                for q in range(4):
                    cells = parts[:, 8 * k + 4 * half + q].astype(jnp.float32)
                    center = jnp.sum(jnp.sum(cells, axis=0), axis=0, keepdims=True) * (1.0 / 64.0)
                    centers.append(center)
                    stack.append((cells.reshape(64, 128) - center).astype(jnp.bfloat16))
                halves.append(jnp.concatenate(stack, axis=0))
            mixed = jnp.dot(
                w, jnp.concatenate(halves, axis=1), preferred_element_type=jnp.float32
            )
            for half in range(2):
                for q in range(4):
                    value = mixed[64 * q : 64 * q + 64, 128 * half : 128 * half + 128]
                    value = value + centers[4 * half + q]
                    out[:, x, 8 * k + 4 * half + q] = value.astype(jnp.bfloat16).reshape(8, 8, 128)
        return carry

    lax.fori_loop(0, CH // 8, block, 0)


def mix(inner, edge, weights):
    return pl.pallas_call(
        mix_kernel,
        in_specs=[vmem()] * 3,
        out_specs=vmem(),
        out_shape=jax.ShapeDtypeStruct((8, 2, CH, 8, 128), jnp.bfloat16),
        compiler_params=vmem_params(),
        cost_estimate=pl.CostEstimate(
            flops=700_000_000, bytes_accessed=5_300_000, transcendentals=0
        ),
    )(inner, edge, weights)


CHUNKS = 5


def order_kernel(cells, out, scratch, sems):
    to = lax.broadcasted_iota(jnp.int32, (128, 128), 0)
    at = lax.broadcasted_iota(jnp.int32, (128, 128), 1)
    source = at >> 4
    side = (at >> 3) & 1
    column = jnp.where(side == 0, source + 4, jnp.where(source < 4, source, source + 8))
    move = jnp.where(to == (at & 7) * 16 + column, 1.0, 0.0).astype(jnp.bfloat16)
    depth = CH // CHUNKS
    copies = []
    for chunk in range(CHUNKS):
        for c in range(depth * chunk, depth * (chunk + 1), 2):
            both = jnp.concatenate(
                [cells[:, c].reshape(128, 128), cells[:, c + 1].reshape(128, 128)], axis=1
            )
            moved = jnp.dot(move, both, preferred_element_type=jnp.float32).astype(jnp.bfloat16)
            scratch[:, c] = moved[:, :128].reshape(8, 16, 128)
            scratch[:, c + 1] = moved[:, 128:].reshape(8, 16, 128)
        rows = pl.ds(depth * chunk, depth)
        copy = pltpu.make_async_copy(scratch.at[:, rows], out.at[:, rows], sems.at[chunk])
        copy.start()
        copies.append(copy)
    for copy in copies:
        copy.wait()


def order(cells):
    return pl.pallas_call(
        order_kernel,
        in_specs=[vmem()],
        out_specs=pl.BlockSpec(memory_space=pl.ANY),
        out_shape=jax.ShapeDtypeStruct((8, CH, 16, 128), jnp.bfloat16),
        scratch_shapes=[
            pltpu.VMEM((8, CH, 16, 128), jnp.bfloat16),
            pltpu.SemaphoreType.DMA((CHUNKS,)),
        ],
        compiler_params=vmem_params(),
        cost_estimate=pl.CostEstimate(
            flops=600_000_000, bytes_accessed=5_300_000, transcendentals=0
        ),
    )(cells)


def ring(cells, step):
    count = lax.axis_size("space")
    return lax.ppermute(cells, "space", [(i, (i + step) % count) for i in range(count)])


def depth_ring(cells, step):
    return lax.ppermute(
        cells, "mem", [(4 * y + (z + step) % 4, 4 * y + z) for y in range(2) for z in range(4)]
    )


def per_device(
    prior_ensemble,
    initial_kernel_taps,
    latter_kernel_taps,
    observed_cells,
    observed_count,
    local_radius,
    observed_value,
    error_variance,
):
    members = prior_ensemble.shape[0]
    bf16 = jnp.bfloat16
    own = jnp.swapaxes(prior_ensemble, 1, 2).reshape(members, 16 * CH, 128)
    cells = observed_cells.reshape(8, 128)
    digits = jnp.stack([cells // 6144, cells // 128 % 48, cells % 128]).reshape(24, 128).astype(bf16)
    digits = jnp.concatenate([digits, jnp.zeros((8, 128), bf16)])
    tail = own[:, (16 - HALO) * CH :].reshape(-1, 128)
    head = own[:, : HALO * CH].reshape(-1, 128)
    left = ring(jnp.concatenate([tail, digits]), 1)
    right = ring(jnp.concatenate([head, digits]), -1)

    inner, halves, rates, first, second = inner_forecast(
        own, initial_kernel_taps, latter_kernel_taps
    )
    inner_parts = lax.all_to_all(inner, "mem", split_axis=0, concat_axis=0, tiled=True)
    edge, picked = edge_forecast(inner, cells, first, second, left, right, own, halves, rates)
    edge_parts = lax.all_to_all(edge, "mem", split_axis=0, concat_axis=0, tiled=True)

    picked = picked.reshape(3, 8, 8, 128)
    from_left = ring(picked[2], 1)
    from_right = ring(picked[0], -1)
    part = (cells // 128 % 48 // 16).reshape(8, 1, 128)
    here = jnp.where(part == 0, from_left, jnp.where(part == 1, picked[1], from_right))
    pair = lax.ppermute(here, "mem", [(i, i ^ 4) for i in range(8)])
    both = jnp.stack([here, pair])
    group = lax.axis_index("mem").astype(jnp.int32)
    numbers = jnp.stack([group % 4, group // 4, observed_count[0], local_radius[0]])
    weights = transform_of(
        (here, pair, depth_ring(both, 1), depth_ring(both, 2), depth_ring(both, 3)),
        observed_cells,
        numbers,
        observed_value,
        error_variance,
    )
    mixed = mix(inner_parts, edge_parts, weights)
    back = lax.all_to_all(mixed, "mem", split_axis=0, concat_axis=0, tiled=True)
    return order(back.reshape(16, CH, 8, 128))


def solution(mesh):
    return jax.shard_map(
        per_device,
        mesh=mesh,
        in_specs=(
            P("mem", None, "space", None),
            P(),
            P(),
            P("space", None),
            P("space"),
            P("space"),
            P("space", None),
            P("space", None),
        ),
        out_specs=P("mem", None, "space", None),
        check_vma=False,
    )
```

time: 131 us -> 135 us (1.031)
  waiting for transfers between devices: 21.1 us -> 14.3 us
  local copies, waits for them, and re-layouts: 7.1 us -> 12.8 us
  starting transfers between devices: 22 us -> 27.6 us
  other arithmetic: 0.31 us -> 2.35 us
  blocking collectives: 35.8 us -> 34.2 us
    all_to_all x1 -> x2, starting transfers between devices: 7.94 us -> 15.4 us  [the longest x1 8.08 us: per_device(): lax.all_to_all(inner, 'mem', split_axis=0, concat_axis=0, tiled=True)]
    unnamed x16 -> x28, local copies, waits for them, and re-layouts: 3.59 us -> 10.2 us
    ppermute x1, waiting for transfers between devices: 13.1 us -> 8.46 us  [per_device(): pair = lax.ppermute(here, 'mem', [(i, i ^ 4) for i in range(8)])]
    ppermute x6 -> x4, waiting for transfers between devices: 3.86 us -> 1.68 us  [ring(): lax.ppermute(cells, 'space', [(i, (i + step) % count) for i in range(coun...]
    ppermute x6 -> x4, starting transfers between devices: 5.43 us -> 3.55 us  [ring(): lax.ppermute(cells, 'space', [(i, (i + step) % count) for i in range(coun...]
    all_to_all x1, blocking collectives: 35.8 us -> 34.2 us  [per_device(): back = lax.all_to_all(mixed, 'mem', split_axis=0, concat_axis=0, tiled=True)]
    concatenate x0 -> x1, other arithmetic: none -> 1.51 us  [per_device(): right = ring(jnp.concatenate([head, digits]), -1)]
    transpose x5 -> x1, local copies, waits for them, and re-layouts: 3.29 us -> 2.42 us  [per_device(): own = jnp.swapaxes(prior_ensemble, 1, 2).reshape(members, 16 * CH, 128)]
  transfers between devices with their start and end apart: 11 -> 10, of which waited for: 6 -> 5; matrix products, arithmetic and copies ran while one was open for 3% -> 0% of each run, Pallas kernels for 18% -> 26%
where the time goes in v2:
time: 135 us; the launch traced here: 134 us
  Pallas kernels  41.8 us (31%)
  blocking collectives  34.2 us (25%)
  starting transfers between devices  27.6 us (20%)
  waiting for transfers between devices  14.3 us (11%)
  local copies, waits for them, and re-layouts  12.8 us (9%)
  other arithmetic  2.35 us (2%)
  between operations  1.45 us (1%)
    all_to_all x1, blocking collectives, per_device(): back = lax.all_to_all(mixed, 'mem', split_axis=0, concat_axis=0, tiled=True)  34.2 us
    pallas_call x1, Pallas kernels, edge_forecast(): pl.pallas_call(edge_kernel, in_specs=[vmem()] * 9, out_specs=[vmem()] * 2...  19.3 us
    pallas_call x1, Pallas kernels, inner_forecast(): pl.pallas_call(inner_kernel, in_specs=[vmem()] * 3, out_specs=[vmem()] *...  13.3 us
    unnamed x28, local copies, waits for them, and re-layouts  10.2 us
    ppermute x1, waiting for transfers between devices, per_device(): pair = lax.ppermute(here, 'mem', [(i, i ^ 4) for i in range(8)])  8.46 us
    all_to_all x1, starting transfers between devices, per_device(): lax.all_to_all(inner, 'mem', split_axis=0, concat_axis=0, tiled=True)  8.08 us
    all_to_all x1, starting transfers between devices, per_device(): lax.all_to_all(edge, 'mem', split_axis=0, concat_axis=0, tiled=True)  7.35 us
    ppermute x3, starting transfers between devices, depth_ring(): lax.ppermute(cells, 'mem', [(4 * y + (z + step) % 4, 4 * y + z) for y in...  4.39 us
  transfers between devices with their start and end apart: 10, of which 5 were waited for; matrix products, arithmetic and copies ran while one was open for 0% of the time, Pallas kernels for 26%

profile of v2, /device:TPU:6, one launch (start us, length us, event | category | flops | bytes accessed | tf_op | source)
XLA Modules:
  0.0 134.5 jit_solution(10709773057930777314)
XLA Ops:
  0.7 2.4 %copy.9 = bf16[8,16,80,128]{3,2,1,0:T(8,128)(2,1)S(1)} copy(bf16[8,16,80,128]{3,1,2,0:T(8,128)(2,1)} %bitcast.22) | data formatting | bytes 5242880 | tf_op jit(solution)/shard_map/transpose | solution.py:440
  3.3 1.5 %fusion.1 = (bf16[2592,128]{1,0:T(8,128)(2,1)}, bf16[2592,128]{1,0:T(8,128)(2,1)}) fusion(bf16[24,128]{1,0:T(8,128)(2,1)S(1)} %maximum_bitcast_fusion, bf16[2560,128]{1,0:T(8,128)(2,1)S(1)} %bitcast.23, bf16[2592]{0:T(1024)(128)(2,1)S(1)} %pad.11.clone, bf16[2560,128]{1,0:T(8,128)(2,1)S(1)} %bitcast.24), kind=kLoop, calls=%fused_computation.3 | loop fusion | flops 3317760 | bytes 2649152 | tf_op jit(solution)/shard_map/concatenate | solution.py:447
  4.8 1.7 %collective-permute-start.1 = (bf16[2592,128]{1,0:T(8,128)(2,1)}, bf16[2592,128]{1,0:T(8,128)(2,1)}, u32[]{:S(2)}, u32[]{:S(2)}) collective-permute-start(bf16[2592,128]{1,0:T(8,128)(2,1)} %get-tuple-element.25), channel_id=1, source_target_pairs={{0,120},{8,0},{16,8},{24,16},{32,24},{40,32},{48,40},{56,48},{64,5... | collective-permute-start | bytes 1990664 | tf_op jit(solution)/shard_map/ppermute | solution.py:419
  6.6 13.3 %shard_map.82 = (bf16[8,80,8,128]{3,2,1,0:T(8,128)(2,1)S(1)}, bf16[8,960,128]{2,1,0:T(8,128)(2,1)S(1)}, f32[8,320,128]{2,1,0:T(8,128)S(1)}, bf16[240,240]{1,0:T(8,128)(2,1)S(1)}, bf16[240,240]{1,0:T(8,128)(2,1)S(1)}) custom-call(bf16[8,1280,128]{2,1,0:T(8,128)(2,1)S(1)} %bitcast.15, bf16[9,80,80]{2,1,0:T(8,128)(2,1)S(1)} %copy-done.4, ...), custom_call_target="tpu_custom_call" | custom-call | flops 12000000000 | bytes 8000000 | tf_op jit(solution)/shard_map/pallas_call | solution.py:196
  19.9 1.1 copy-done.1
  20.9 1.3 copy-done.8
  22.2 1.1 copy-done.10
  23.9 8.1 %all-to-all-start = ((bf16[8,80,8,128]{3,2,1,0:T(8,128)(2,1)}), bf16[8,80,8,128]{3,2,1,0:T(8,128)(2,1)}, u32[]{:S(2)}, u32[]{:S(2)}) async-start(bf16[8,80,8,128]{3,2,1,0:T(8,128)(2,1)} %copy-done.1), calls=%async_computation | async-start | bytes 2621440 | tf_op jit(solution)/shard_map/all_to_all | solution.py:452
  32.0 1.3 copy-done.2
  33.4 1.5 %copy-done.9 = bf16[8,960,128]{2,1,0:T(8,128)(2,1)S(1)} copy-done((bf16[8,960,128]{2,1,0:T(8,128)(2,1)S(1)}, bf16[8,960,128]{2,1,0:T(8,128)(2,1)}, u32[]{:S(2)}) %copy-start.9) | copy-done | bytes 1966104
  34.9 1.3 copy-done.11
  37.1 19.3 %shard_map.83 = (bf16[8,80,8,128]{3,2,1,0:T(8,128)(2,1)S(1)}, bf16[24,8,128]{2,1,0:T(8,128)(2,1)S(1)}) custom-call(bf16[8,80,8,128]{3,2,1,0:T(8,128)(2,1)S(1)} %copy-done.2, s32[8,128]{1,0:T(8,128)S(1)} %bitcast.19, bf16[240,240]{1,0:T(8,128)(2,1)S(1)} %get-tuple-element.13.first, bf16[240,240]{1,0:T(8,128)(2,1)S(1)} %copy-done.13, ...), custom_call_target="tpu_custom_call" | custom-call | flops 8999999488 | bytes 8000000 | tf_op jit(solution)/shard_map/pallas_call | solution.py:223
  56.5 1.0 copy-done
  57.5 7.3 %all-to-all-start.1 = ((bf16[8,80,8,128]{3,2,1,0:T(8,128)(2,1)}), bf16[8,80,8,128]{3,2,1,0:T(8,128)(2,1)S(1)}, u32[]{:S(2)}, u32[]{:S(2)}) async-start(bf16[8,80,8,128]{3,2,1,0:T(8,128)(2,1)} %copy-done), calls=%async_computation.1 | async-start | bytes 2621440 | tf_op jit(solution)/shard_map/all_to_all | solution.py:454
  65.0 1.7 %collective-permute-start.3 = (bf16[8,8,128]{2,1,0:T(8,128)(2,1)S(1)}, bf16[8,8,128]{2,1,0:T(8,128)(2,1)S(1)}, u32[]{:S(2)}, u32[]{:S(2)}) collective-permute-start(bf16[8,8,128]{2,1,0:T(8,128)(2,1)S(1)} %get-tuple-element.23), channel_id=1, source_target_pairs={{0,120},{8,0},{16,8},{24,16},{32,24},{40,32},{48,40},{56,48},{64,5... | collective-permute-start | bytes 49160 | tf_op jit(solution)/shard_map/ppermute | solution.py:419
  66.7 1.4 %collective-permute-done.2 = bf16[8,8,128]{2,1,0:T(8,128)(2,1)S(1)} collective-permute-done((bf16[8,8,128]{2,1,0:T(8,128)(2,1)S(1)}, bf16[8,8,128]{2,1,0:T(8,128)(2,1)S(1)}, u32[]{:S(2)}, u32[]{:S(2)}) %collective-permute-start.2) | collective-permute-done | bytes 16416 | tf_op jit(solution)/shard_map/ppermute | solution.py:419
  68.4 4.2 %collective-permute-start.4 = (bf16[8,8,128]{2,1,0:T(8,128)(2,1)S(1)}, bf16[8,8,128]{2,1,0:T(8,128)(2,1)S(1)}, u32[]{:S(2)}, u32[]{:S(2)}) collective-permute-start(bf16[8,8,128]{2,1,0:T(8,128)(2,1)S(1)} %select_select_fusion.here), channel_id=1, source_target_pairs={{0,4},{1,5},{2,6},{3,7},{4,0},{5,1},{6,2},{7,3},{8,12},{9,13},{10,... | collective-permute-start | bytes 49160 | tf_op jit(solution)/shard_map/ppermute | solution.py:461
  74.0 8.5 %collective-permute-done.4.pair = bf16[8,8,128]{2,1,0:T(8,128)(2,1)S(1)} collective-permute-done((bf16[8,8,128]{2,1,0:T(8,128)(2,1)S(1)}, bf16[8,8,128]{2,1,0:T(8,128)(2,1)S(1)}, u32[]{:S(2)}, u32[]{:S(2)}) %collective-permute-start.4) | collective-permute-done | bytes 16416 | tf_op jit(solution)/shard_map/ppermute | solution.py:461
  82.4 2.7 %collective-permute-start.5 = (bf16[2,8,8,128]{3,2,1,0:T(8,128)(2,1)S(1)}, bf16[2,8,8,128]{3,2,1,0:T(8,128)(2,1)S(1)}, u32[]{:S(2)}, u32[]{:S(2)}) collective-permute-start(bf16[2,8,8,128]{3,2,1,0:T(8,128)(2,1)S(1)} %pad_maximum_fusion.2), channel_id=1, source_target_pairs={{1,0},{2,1},{3,2},{0,3},{5,4},{6,5},{7,6},{4,7},{9,8},{10,9},{11,1... | collective-permute-start | bytes 98312 | tf_op jit(solution)/shard_map/ppermute | solution.py:423
  86.9 3.6 %collective-permute-done.6.across = bf16[2,8,8,128]{3,2,1,0:T(8,128)(2,1)S(1)} collective-permute-done((bf16[2,8,8,128]{3,2,1,0:T(8,128)(2,1)S(1)}, bf16[2,8,8,128]{3,2,1,0:T(8,128)(2,1)S(1)}, u32[]{:S(2)}, u32[]{:S(2)}) %collective-permute-start.6) | collective-permute-done | bytes 32800 | tf_op jit(solution)/shard_map/ppermute | solution.py:423
  91.1 3.0 %shard_map.84.weights = bf16[256,256]{1,0:T(8,128)(2,1)S(1)} custom-call(bf16[8,8,128]{2,1,0:T(8,128)(2,1)S(1)} %select_select_fusion.here, bf16[8,8,128]{2,1,0:T(8,128)(2,1)S(1)} %collective-permute-done.4.pair, bf16[2,8,8,128]{3,2,1,0:T(8,128)(2,1)S(1)} %collective-permute-done.5.ahead, bf16[2,8,8,128]{3,2,1,0:T(8,128)(2,1)S(1)} %collective-permute-done.6.across, ...), custom_call_target="tpu_custom_call" | custom-call | flops 100000000 | bytes 500000 | tf_op jit(solution)/shard_map/pallas_call | solution.py:318
  94.1 4.3 %shard_map.85 = bf16[8,2,80,8,128]{4,3,2,1,0:T(8,128)(2,1)S(1)} custom-call(bf16[8,80,8,128]{3,2,1,0:T(8,128)(2,1)} %all-to-all-done.inner, bf16[8,80,8,128]{3,2,1,0:T(8,128)(2,1)S(1)} %all-to-all-done.1.edge, bf16[256,256]{1,0:T(8,128)(2,1)S(1)} %shard_map.84.weights), custom_call_target="tpu_custom_call" | custom-call | flops 700000000 | bytes 5300000 | tf_op jit(solution)/shard_map/pallas_call | solution.py:360
  98.5 34.2 %all_to_all.15 = bf16[8,2,80,8,128]{4,3,2,1,0:T(8,128)(2,1)S(1)} all-to-all(bf16[8,2,80,8,128]{4,3,2,1,0:T(8,128)(2,1)S(1)} %shard_map.85), channel_id=1, replica_groups=mesh['space'=16,'mem'=8] {'mem'}, dimensions={0} | all-to-all | bytes 5242880 | tf_op jit(solution)/shard_map/all_to_all | solution.py:473
  132.7 1.8 %shard_map.86 = bf16[8,80,16,128]{3,2,1,0:T(8,128)(2,1)} custom-call(bf16[16,80,8,128]{3,2,1,0:T(8,128)(2,1)S(1)} %bitcast.13), custom_call_target="tpu_custom_call" | custom-call | flops 600000000 | bytes 5300000 | tf_op jit(solution)/shard_map/pallas_call | solution.py:401
  (43 shorter events, 5.2 us)
Async XLA Ops:
  3.3 3.3 %copy-start.4 = (bf16[9,80,80]{2,1,0:T(8,128)(2,1)S(1)}, bf16[9,80,80]{2,1,0:T(8,128)(2,1)}, u32[]{:S(2)}) copy-start(bf16[9,80,80]{2,1,0:T(8,128)(2,1)} %first_taps.1) | copy-start | bytes 345604
  3.3 3.3 %copy-start.5 = (bf16[9,80,80]{2,1,0:T(8,128)(2,1)S(1)}, bf16[9,80,80]{2,1,0:T(8,128)(2,1)}, u32[]{:S(2)}) copy-start(bf16[9,80,80]{2,1,0:T(8,128)(2,1)} %second_taps.1) | copy-start | bytes 345604
  4.8 27.2 %collective-permute-start = (bf16[2592,128]{1,0:T(8,128)(2,1)}, bf16[2592,128]{1,0:T(8,128)(2,1)S(1)}, u32[]{:S(2)}, u32[]{:S(2)}) collective-permute-start(bf16[2592,128]{1,0:T(8,128)(2,1)} %get-tuple-element.26), channel_id=1, source_target_pairs={{0,8},{8,16},{16,24},{24,32},{32,40},{40,48},{48,56},{56,64},{64,7... | collective-permute-start | bytes 1990664 | tf_op jit(solution)/shard_map/ppermute | solution.py:419
  4.8 27.2 %collective-permute-start.1 = (bf16[2592,128]{1,0:T(8,128)(2,1)}, bf16[2592,128]{1,0:T(8,128)(2,1)}, u32[]{:S(2)}, u32[]{:S(2)}) collective-permute-start(bf16[2592,128]{1,0:T(8,128)(2,1)} %get-tuple-element.25), channel_id=1, source_target_pairs={{0,120},{8,0},{16,8},{24,16},{32,24},{40,32},{48,40},{56,48},{64,5... | collective-permute-start | bytes 1990664 | tf_op jit(solution)/shard_map/ppermute | solution.py:419
  19.8 1.1 copy-start.1
  20.9 1.3 copy-start.8
  22.2 1.1 copy-start.10
  23.3 0.6 copy-start.12
  23.9 8.1 %copy-start.3 = (s32[1,1024]{1,0:T(1,128)S(1)}, s32[1,1024]{1,0:T(1,128)}, u32[]{:S(2)}) copy-start(s32[1,1024]{1,0:T(1,128)} %cells.1) | copy-start | bytes 12292
  23.9 33.6 %all-to-all-start = ((bf16[8,80,8,128]{3,2,1,0:T(8,128)(2,1)}), bf16[8,80,8,128]{3,2,1,0:T(8,128)(2,1)}, u32[]{:S(2)}, u32[]{:S(2)}) async-start(bf16[8,80,8,128]{3,2,1,0:T(8,128)(2,1)} %copy-done.1), calls=%async_computation | async-start | bytes 2621440 | tf_op jit(solution)/shard_map/all_to_all | solution.py:452
  32.0 1.3 copy-start.2
  33.4 1.5 %copy-start.9 = (bf16[8,960,128]{2,1,0:T(8,128)(2,1)S(1)}, bf16[8,960,128]{2,1,0:T(8,128)(2,1)}, u32[]{:S(2)}) copy-start(bf16[8,960,128]{2,1,0:T(8,128)(2,1)} %copy-done.8) | copy-start | bytes 5898244
  34.9 1.3 copy-start.11
  36.2 0.9 copy-start.13
  56.5 1.1 copy-start
  57.5 33.6 %copy-start.6 = (f32[1,1024]{1,0:T(1,128)S(1)}, f32[1,1024]{1,0:T(1,128)}, u32[]{:S(2)}) copy-start(f32[1,1024]{1,0:T(1,128)} %observed.1) | copy-start | bytes 12292
  57.5 33.6 %copy-start.7 = (f32[1,1024]{1,0:T(1,128)S(1)}, f32[1,1024]{1,0:T(1,128)}, u32[]{:S(2)}) copy-start(f32[1,1024]{1,0:T(1,128)} %variance.1) | copy-start | bytes 12292
  57.5 36.6 %all-to-all-start.1 = ((bf16[8,80,8,128]{3,2,1,0:T(8,128)(2,1)}), bf16[8,80,8,128]{3,2,1,0:T(8,128)(2,1)S(1)}, u32[]{:S(2)}, u32[]{:S(2)}) async-start(bf16[8,80,8,128]{3,2,1,0:T(8,128)(2,1)} %copy-done), calls=%async_computation.1 | async-start | bytes 2621440 | tf_op jit(solution)/shard_map/all_to_all | solution.py:454
  64.9 3.2 %collective-permute-start.2 = (bf16[8,8,128]{2,1,0:T(8,128)(2,1)S(1)}, bf16[8,8,128]{2,1,0:T(8,128)(2,1)S(1)}, u32[]{:S(2)}, u32[]{:S(2)}) collective-permute-start(bf16[8,8,128]{2,1,0:T(8,128)(2,1)S(1)} %get-tuple-element.24), channel_id=1, source_target_pairs={{0,8},{8,16},{16,24},{24,32},{32,40},{40,48},{48,56},{56,64},{64,7... | collective-permute-start | bytes 49160 | tf_op jit(solution)/shard_map/ppermute | solution.py:419
  65.0 3.4 %collective-permute-start.3 = (bf16[8,8,128]{2,1,0:T(8,128)(2,1)S(1)}, bf16[8,8,128]{2,1,0:T(8,128)(2,1)S(1)}, u32[]{:S(2)}, u32[]{:S(2)}) collective-permute-start(bf16[8,8,128]{2,1,0:T(8,128)(2,1)S(1)} %get-tuple-element.23), channel_id=1, source_target_pairs={{0,120},{8,0},{16,8},{24,16},{32,24},{40,32},{48,40},{56,48},{64,5... | collective-permute-start | bytes 49160 | tf_op jit(solution)/shard_map/ppermute | solution.py:419
  68.4 14.0 %collective-permute-start.4 = (bf16[8,8,128]{2,1,0:T(8,128)(2,1)S(1)}, bf16[8,8,128]{2,1,0:T(8,128)(2,1)S(1)}, u32[]{:S(2)}, u32[]{:S(2)}) collective-permute-start(bf16[8,8,128]{2,1,0:T(8,128)(2,1)S(1)} %select_select_fusion.here), channel_id=1, source_target_pairs={{0,4},{1,5},{2,6},{3,7},{4,0},{5,1},{6,2},{7,3},{8,12},{9,13},{10,... | collective-permute-start | bytes 49160 | tf_op jit(solution)/shard_map/ppermute | solution.py:461
  82.4 4.5 %collective-permute-start.5 = (bf16[2,8,8,128]{3,2,1,0:T(8,128)(2,1)S(1)}, bf16[2,8,8,128]{3,2,1,0:T(8,128)(2,1)S(1)}, u32[]{:S(2)}, u32[]{:S(2)}) collective-permute-start(bf16[2,8,8,128]{3,2,1,0:T(8,128)(2,1)S(1)} %pad_maximum_fusion.2), channel_id=1, source_target_pairs={{1,0},{2,1},{3,2},{0,3},{5,4},{6,5},{7,6},{4,7},{9,8},{10,9},{11,1... | collective-permute-start | bytes 98312 | tf_op jit(solution)/shard_map/ppermute | solution.py:423
  85.1 5.4 %collective-permute-start.6 = (bf16[2,8,8,128]{3,2,1,0:T(8,128)(2,1)S(1)}, bf16[2,8,8,128]{3,2,1,0:T(8,128)(2,1)S(1)}, u32[]{:S(2)}, u32[]{:S(2)}) collective-permute-start(bf16[2,8,8,128]{3,2,1,0:T(8,128)(2,1)S(1)} %pad_maximum_fusion.2), channel_id=1, source_target_pairs={{2,0},{3,1},{0,2},{1,3},{6,4},{7,5},{4,6},{5,7},{10,8},{11,9},{8,1... | collective-permute-start | bytes 98312 | tf_op jit(solution)/shard_map/ppermute | solution.py:423
  86.0 5.1 %collective-permute-start.7 = (bf16[2,8,8,128]{3,2,1,0:T(8,128)(2,1)S(1)}, bf16[2,8,8,128]{3,2,1,0:T(8,128)(2,1)S(1)}, u32[]{:S(2)}, u32[]{:S(2)}) collective-permute-start(bf16[2,8,8,128]{3,2,1,0:T(8,128)(2,1)S(1)} %pad_maximum_fusion.2), channel_id=1, source_target_pairs={{3,0},{0,1},{1,2},{2,3},{7,4},{4,5},{5,6},{6,7},{11,8},{8,9},{9,10... | collective-permute-start | bytes 98312 | tf_op jit(solution)/shard_map/ppermute | solution.py:423

commit v3 on v2

--- a/solution.py
+++ b/solution.py
@@ -9,6 +9,9 @@
 STEP_SIZE = 0.5
 HALO = 4
 CH = 80
+PAIR_A = 4
+PAIR_B = 8
+LAG = 3
 
 
 def vmem_params():
@@ -26,16 +29,14 @@
     return p[80:160] + jnp.where(lane == 0, 0.0, below) + jnp.where(lane == 127, 0.0, above)
 
 
-def conv_columns(source, first, taps, columns, emit):
+def conv_pair(source, at, taps, emit, k):
     lane = lax.broadcasted_iota(jnp.int32, (CH, 128), 1)
-    for k in range(0, columns, 2):
-        at = CH * (first + k)
-        window = jnp.concatenate(
-            [source[pl.ds(at, 3 * CH), :], source[pl.ds(at + CH, 3 * CH), :]], axis=1
-        )
-        partial = jnp.dot(taps, window, preferred_element_type=jnp.float32)
-        emit(k, shifted_sum(partial[:, :128], lane))
-        emit(k + 1, shifted_sum(partial[:, 128:], lane))
+    window = jnp.concatenate(
+        [source[pl.ds(CH * at, 3 * CH), :], source[pl.ds(CH * (at + 1), 3 * CH), :]], axis=1
+    )
+    partial = jnp.dot(taps, window, preferred_element_type=jnp.float32)
+    emit(k, shifted_sum(partial[:, :128], lane))
+    emit(k + 1, shifted_sum(partial[:, 128:], lane))
 
 
 def build_taps(taps, matrix):
@@ -44,43 +45,113 @@
         matrix[pl.ds(CH * b, CH), :] = row.astype(jnp.bfloat16)
 
 
-def inner_kernel(own, first_taps, second_taps, out, halves, rates, taps_a, taps_b, h, s, g, rate, fields):
-    build_taps(first_taps, taps_a)
-    build_taps(second_taps, taps_b)
-    a = taps_a[...]
-    b = taps_b[...]
-
-    def one(m, carry):
-        v = own.at[m]
-
-        def put_first(k, value):
-            h[pl.ds(CH * k, CH), :] = gelu(value).astype(jnp.bfloat16)
-
-        def put_section(k, value):
-            base = v[pl.ds(CH * (k + 2), CH), :].astype(jnp.float32)
-            s[pl.ds(CH * k, CH), :] = (base + STEP_SIZE * value).astype(jnp.bfloat16)
-            rate[pl.ds(CH * k, CH), :] = base + 0.5 * STEP_SIZE * value
-
-        def put_second(k, value):
-            g[pl.ds(CH * k, CH), :] = gelu(value).astype(jnp.bfloat16)
-
-        def put_forecast(k, value):
-            cells = rate[pl.ds(CH * (k + 2), CH), :] + 0.5 * STEP_SIZE * value
-            fields[pl.ds(8 * CH * k + m, CH, stride=8), :] = cells
-
-        conv_columns(v, 0, a, 14, put_first)
-        conv_columns(h, 0, b, 12, put_section)
-        conv_columns(s, 0, a, 10, put_second)
-        conv_columns(g, 0, b, 8, put_forecast)
-        for k, (ref, right) in enumerate(((h, 12), (s, 10), (g, 8))):
-            halves[m, pl.ds(2 * CH * k, 2 * CH), :] = ref[pl.ds(0, 2 * CH), :]
-            halves[m, pl.ds(2 * CH * (k + 3), 2 * CH), :] = ref[pl.ds(CH * right, 2 * CH), :]
-        rates[m, pl.ds(0, 2 * CH), :] = rate[pl.ds(0, 2 * CH), :]
-        rates[m, pl.ds(2 * CH, 2 * CH), :] = rate[pl.ds(10 * CH, 2 * CH), :]
+def run_interleaved(jobs):
+    for _, step in sorted(jobs, key=lambda job: job[0]):
+        step()
+
+
+def inner_kernel(
+    own, first_taps, second_taps, out, halves, rates, edges, taps_out,
+    taps, h, s, g, rate, fields, cells16, sems,
+):
+    members = own.shape[0]
+    build_taps(first_taps, taps.at[0])
+    build_taps(second_taps, taps.at[1])
+    a = taps[0]
+    b = taps[1]
+    copies = [
+        pltpu.make_async_copy(own.at[:, pl.ds(0, 4 * CH)], edges.at[:, pl.ds(0, 4 * CH)], sems.at[0]),
+        pltpu.make_async_copy(own.at[:, pl.ds(12 * CH, 4 * CH)], edges.at[:, pl.ds(4 * CH, 4 * CH)], sems.at[1]),
+        pltpu.make_async_copy(taps, taps_out, sems.at[2]),
+    ]
+    for copy in copies:
+        copy.start()
+
+    def group(n, carry):
+        jobs = []
+        for i in range(PAIR_A):
+            m = n * PAIR_A + i
+            v, hm, sm, gm, rm = own.at[m], h.at[m], s.at[m], g.at[m], rate.at[m]
+
+            def put_first(k, value, hm=hm):
+                hm[pl.ds(CH * k, CH), :] = gelu(value).astype(jnp.bfloat16)
+
+            def put_section(k, value, v=v, sm=sm, rm=rm):
+                base = v[pl.ds(CH * (k + 2), CH), :].astype(jnp.float32)
+                sm[pl.ds(CH * k, CH), :] = (base + STEP_SIZE * value).astype(jnp.bfloat16)
+                rm[pl.ds(CH * k, CH), :] = base + 0.5 * STEP_SIZE * value
+
+            def put_second(k, value, gm=gm):
+                gm[pl.ds(CH * k, CH), :] = gelu(value).astype(jnp.bfloat16)
+
+            def put_forecast(k, value, rm=rm, m=m):
+                cells = rm[pl.ds(CH * (k + 2), CH), :] + 0.5 * STEP_SIZE * value
+                fields[pl.ds(8 * CH * k + m, CH, stride=8), :] = cells
+
+            stages = ((v, a, 14, put_first), (hm, b, 12, put_section), (sm, a, 10, put_second), (gm, b, 8, put_forecast))
+            for level, (source, matrix, columns, emit) in enumerate(stages):
+                for k in range(0, columns, 2):
+                    jobs.append(((k // 2 + LAG * level, i, level), lambda source=source, k=k, matrix=matrix, emit=emit: conv_pair(source, k, matrix, emit, k)))
+        run_interleaved(jobs)
         return carry
 
-    lax.fori_loop(0, own.shape[0], one, 0)
-    out[...] = fields[...].astype(jnp.bfloat16).reshape(out.shape)
+    lax.fori_loop(0, members // PAIR_A, group, 0)
+    for k, (ref, right) in enumerate(((h, 12), (s, 10), (g, 8))):
+        for side, at in enumerate((0, right)):
+            copies.append(pltpu.make_async_copy(
+                ref.at[:, pl.ds(CH * at, 2 * CH)],
+                halves.at[:, pl.ds(2 * CH * (k + 3 * side), 2 * CH)],
+                sems.at[3 + 2 * k + side],
+            ))
+    for side, at in enumerate((0, 10)):
+        copies.append(pltpu.make_async_copy(
+            rate.at[:, pl.ds(CH * at, 2 * CH)], rates.at[:, pl.ds(2 * CH * side, 2 * CH)], sems.at[9 + side]
+        ))
+    for copy in copies[3:]:
+        copy.start()
+    cells16[...] = fields[...].astype(jnp.bfloat16).reshape(out.shape)
+    last = pltpu.make_async_copy(cells16, out, sems.at[11])
+    last.start()
+    for copy in copies:
+        copy.wait()
+    last.wait()
+
+
+def vmem():
+    return pl.BlockSpec(memory_space=pltpu.VMEM)
+
+def hbm():
+    return pl.BlockSpec(memory_space=pltpu.HBM)
+
+def inner_forecast(own, first_taps, second_taps):
+    members = own.shape[0]
+    bf16, f32 = jnp.bfloat16, jnp.float32
+    return pl.pallas_call(
+        inner_kernel,
+        in_specs=[vmem()] * 3,
+        out_specs=[hbm()] * 5,
+        out_shape=[
+            jax.ShapeDtypeStruct((8, CH, 8, 128), bf16),
+            jax.ShapeDtypeStruct((members, 12 * CH, 128), bf16),
+            jax.ShapeDtypeStruct((members, 4 * CH, 128), f32),
+            jax.ShapeDtypeStruct((members, 8 * CH, 128), bf16),
+            jax.ShapeDtypeStruct((2, 3 * CH, 3 * CH), bf16),
+        ],
+        scratch_shapes=[
+            pltpu.VMEM((2, 3 * CH, 3 * CH), bf16),
+            pltpu.VMEM((members, 14 * CH, 128), bf16),
+            pltpu.VMEM((members, 12 * CH, 128), bf16),
+            pltpu.VMEM((members, 10 * CH, 128), bf16),
+            pltpu.VMEM((members, 12 * CH, 128), f32),
+            pltpu.VMEM((64 * CH, 128), f32),
+            pltpu.VMEM((8, CH, 8, 128), bf16),
+            pltpu.SemaphoreType.DMA((12,)),
+        ],
+        compiler_params=vmem_params(),
+        cost_estimate=pl.CostEstimate(
+            flops=12_000_000_000, bytes_accessed=8_000_000, transcendentals=2_000_000
+        ),
+    )(own, first_taps, second_taps)
 
 
 def place_of(channel, lon, lat, part):
@@ -92,86 +163,125 @@
 
 
 def edge_kernel(
-    inner, cells, first, second, left, right, own, halves, rates, out, picked,
-    v, h, s, g, rate, fields, places, rows, turns, sems,
+    inner, cells, taps_in, left, right, edges, halves, rates, out, picked,
+    taps, v, h, s, g, rate, rated, fields, cells16, inner16, lists, drawn, places, rows, turns, sems, list_sems, out_sems, place_sems,
 ):
-    members = own.shape[0]
-    a = first[...]
-    b = second[...]
-    digits = CH * HALO * members
-    for k, source in enumerate((left, cells, right)):
+    members = edges.shape[0]
+    halo = CH * HALO
+    digits = halo * members
+
+    def loads(n):
+        at = pl.ds(n * PAIR_B, PAIR_B)
+        parts = []
+        for i in range(PAIR_B):
+            m = n * PAIR_B + i
+            spot = pl.ds(pl.multiple_of(halo * m, halo), halo)
+            parts.append((left.at[spot], v.at[m, pl.ds(0, 4 * CH)]))
+            parts.append((right.at[spot], v.at[m, pl.ds(12 * CH, 4 * CH)]))
+        parts.append((edges.at[at], v.at[at, pl.ds(4 * CH, 8 * CH)]))
+        for k, ref in enumerate((h, s, g)):
+            for side in range(2):
+                parts.append((
+                    halves.at[at, pl.ds(2 * CH * (k + 3 * side), 2 * CH)],
+                    ref.at[at, pl.ds((4 + 2 * side) * CH, 2 * CH)],
+                ))
+        parts.append((rates.at[at], rated.at[at]))
+        return [
+            pltpu.make_async_copy(source, target, sems.at[n, i])
+            for i, (source, target) in enumerate(parts)
+        ]
+
+    groups = members // PAIR_B
+    firsts = [pltpu.make_async_copy(taps_in, taps, list_sems.at[0])]
+    for i, source in enumerate((left, right)):
+        firsts.append(pltpu.make_async_copy(source.at[pl.ds(digits, 32)], lists.at[i], list_sems.at[1 + i]))
+    for copy in firsts:
+        copy.start()
+    for n in range(groups):
+        for copy in loads(n):
+            copy.start()
+    inner_copy = pltpu.make_async_copy(inner, inner16, list_sems.at[3])
+    inner_copy.start()
+    for copy in firsts:
+        copy.wait()
+    for k in range(3):
         if k == 1:
-            cell = source[...]
+            cell = cells[...]
             strip = cell >> 7
             channel = (strip * 43691) >> 21
             parts = (channel, strip - 48 * channel, cell & 127)
         else:
-            block = source[pl.ds(digits, 32), :].astype(jnp.float32).astype(jnp.int32)
+            block = lists[k // 2].astype(jnp.float32).astype(jnp.int32)
             parts = (block[0:8], block[8:16], block[16:24])
         row, turn = place_of(*parts, 2 - k)
         places[0, pl.ds(8 * k, 8), :] = row
         places[1, pl.ds(8 * k, 8), :] = turn
-    copies = [
-        pltpu.make_async_copy(places.at[0], rows, sems.at[0]),
-        pltpu.make_async_copy(places.at[1], turns, sems.at[1]),
+    place_copies = [
+        pltpu.make_async_copy(places.at[0], rows, place_sems.at[0]),
+        pltpu.make_async_copy(places.at[1], turns, place_sems.at[1]),
     ]
-    for copy in copies:
+    for copy in place_copies:
         copy.start()
-    fields[pl.ds(0, 64 * CH), :] = inner[...].astype(jnp.float32).reshape(64 * CH, 128)
-
-    def one(m, carry):
-        halo = pl.ds(pl.multiple_of(CH * HALO * m, CH * HALO), CH * HALO)
-        v[pl.ds(0, 4 * CH), :] = left[halo, :]
-        v[pl.ds(4 * CH, 4 * CH), :] = own[m, pl.ds(0, 4 * CH), :]
-        v[pl.ds(8 * CH, 4 * CH), :] = own[m, pl.ds(12 * CH, 4 * CH), :]
-        v[pl.ds(12 * CH, 4 * CH), :] = right[halo, :]
-        for k, ref in enumerate((h, s, g)):
-            ref[pl.ds(4 * CH, 2 * CH), :] = halves[m, pl.ds(2 * CH * k, 2 * CH), :]
-            ref[pl.ds(6 * CH, 2 * CH), :] = halves[m, pl.ds(2 * CH * (k + 3), 2 * CH), :]
-
-        def hidden(ref, at):
-            def put(k, value):
-                ref[pl.ds(CH * (at + k), CH), :] = gelu(value).astype(jnp.bfloat16)
-
-            return put
-
-        def section_left(k, value):
-            base = v[pl.ds(CH * (k + 2), CH), :].astype(jnp.float32)
-            s[pl.ds(CH * k, CH), :] = (base + STEP_SIZE * value).astype(jnp.bfloat16)
-            if k >= 2:
-                rate[pl.ds(CH * (k - 2), CH), :] = base + 0.5 * STEP_SIZE * value
-
-        def section_right(k, value):
-            base = v[pl.ds(CH * (k + 10), CH), :].astype(jnp.float32)
-            s[pl.ds(CH * (8 + k), CH), :] = (base + STEP_SIZE * value).astype(jnp.bfloat16)
-            if k < 2:
-                rate[pl.ds(CH * (k + 2), CH), :] = base + 0.5 * STEP_SIZE * value
-
-        def put_field(column, start, value):
-            value = (start + 0.5 * STEP_SIZE * value).astype(jnp.bfloat16).astype(jnp.float32)
-            fields[pl.ds(8 * CH * (8 + column) + m, CH, stride=8), :] = value
-
-        def forecast_left(k, value):
-            start = rate[pl.ds(CH * k, CH), :] if k < 2 else rates[m, pl.ds(CH * (k - 2), CH), :]
-            put_field(k, start, value)
-
-        def forecast_right(k, value):
-            start = rates[m, pl.ds(CH * (k + 2), CH), :] if k < 2 else rate[pl.ds(CH * k, CH), :]
-            put_field(k + 4, start, value)
-
-        conv_columns(v, 0, a, 4, hidden(h, 0))
-        conv_columns(v, 10, a, 4, hidden(h, 8))
-        conv_columns(h, 0, b, 4, section_left)
-        conv_columns(h, 6, b, 4, section_right)
-        conv_columns(s, 0, a, 4, hidden(g, 0))
-        conv_columns(s, 6, a, 4, hidden(g, 8))
-        conv_columns(g, 0, b, 4, forecast_left)
-        conv_columns(g, 6, b, 4, forecast_right)
+    a = taps[0]
+    b = taps[1]
+
+    def group(n, carry):
+        for copy in loads(n):
+            copy.wait()
+        jobs = []
+        for i in range(PAIR_B):
+            m = n * PAIR_B + i
+            vm, hm, sm, gm, rm, rdm = v.at[m], h.at[m], s.at[m], g.at[m], rate.at[m], rated.at[m]
+
+            def hidden(ref, at):
+                def put(k, value):
+                    ref[pl.ds(CH * (at + k), CH), :] = gelu(value).astype(jnp.bfloat16)
+
+                return put
+
+            def section_left(k, value, vm=vm, sm=sm, rm=rm):
+                base = vm[pl.ds(CH * (k + 2), CH), :].astype(jnp.float32)
+                sm[pl.ds(CH * k, CH), :] = (base + STEP_SIZE * value).astype(jnp.bfloat16)
+                if k >= 2:
+                    rm[pl.ds(CH * (k - 2), CH), :] = base + 0.5 * STEP_SIZE * value
+
+            def section_right(k, value, vm=vm, sm=sm, rm=rm):
+                base = vm[pl.ds(CH * (k + 10), CH), :].astype(jnp.float32)
+                sm[pl.ds(CH * (8 + k), CH), :] = (base + STEP_SIZE * value).astype(jnp.bfloat16)
+                if k < 2:
+                    rm[pl.ds(CH * (k + 2), CH), :] = base + 0.5 * STEP_SIZE * value
+
+            def put_field(column, start, value, m):
+                value = (start + 0.5 * STEP_SIZE * value).astype(jnp.bfloat16).astype(jnp.float32)
+                fields[pl.ds(8 * CH * (8 + column) + m, CH, stride=8), :] = value
+
+            def forecast_left(k, value, rm=rm, rdm=rdm, m=m):
+                start = rm[pl.ds(CH * k, CH), :] if k < 2 else rdm[pl.ds(CH * (k - 2), CH), :]
+                put_field(k, start, value, m)
+
+            def forecast_right(k, value, rm=rm, rdm=rdm, m=m):
+                start = rdm[pl.ds(CH * (k + 2), CH), :] if k < 2 else rm[pl.ds(CH * k, CH), :]
+                put_field(k + 4, start, value, m)
+
+            stages = (
+                (vm, 0, a, hidden(hm, 0)), (vm, 10, a, hidden(hm, 8)),
+                (hm, 0, b, section_left), (hm, 6, b, section_right),
+                (sm, 0, a, hidden(gm, 0)), (sm, 6, a, hidden(gm, 8)),
+                (gm, 0, b, forecast_left), (gm, 6, b, forecast_right),
+            )
+            for level, (source, at, matrix, emit) in enumerate(stages):
+                for k in (0, 2):
+                    jobs.append(((level // 2, i, level, k), lambda source=source, at=at, k=k, matrix=matrix, emit=emit: conv_pair(source, at + k, matrix, emit, k)))
+        run_interleaved(jobs)
         return carry
 
-    lax.fori_loop(0, members, one, 0)
-    out[...] = fields[pl.ds(64 * CH, 64 * CH), :].astype(jnp.bfloat16).reshape(out.shape)
-    for copy in copies:
+    lax.fori_loop(0, groups, group, 0)
+    cells16[...] = fields[pl.ds(64 * CH, 64 * CH), :].astype(jnp.bfloat16).reshape(out.shape)
+    out_copy = pltpu.make_async_copy(cells16, out, out_sems.at[0])
+    out_copy.start()
+    inner_copy.wait()
+    fields[pl.ds(0, 64 * CH), :] = inner16[...].astype(jnp.float32).reshape(64 * CH, 128)
+    for copy in place_copies:
         copy.wait()
     lane = lax.broadcasted_iota(jnp.int32, (8, 128), 1)
 
@@ -180,71 +290,53 @@
         for j in range(128):
             cell = fields[pl.ds(pl.multiple_of(rows[k, j], 8), 8), :]
             acc = jnp.where(lane == j, pltpu.roll(cell, turns[k, j], axis=1), acc)
-        picked[k] = acc.astype(jnp.bfloat16)
+        drawn[k] = acc.astype(jnp.bfloat16)
         return carry
 
-    lax.fori_loop(0, picked.shape[0], block, 0)
-
-
-def vmem():
-    return pl.BlockSpec(memory_space=pltpu.VMEM)
-
-
-def inner_forecast(own, first_taps, second_taps):
-    members = own.shape[0]
+    lax.fori_loop(0, drawn.shape[0], block, 0)
+    drawn_copy = pltpu.make_async_copy(drawn, picked, out_sems.at[1])
+    drawn_copy.start()
+    drawn_copy.wait()
+    out_copy.wait()
+
+
+def edge_forecast(inner, cells, taps, left, right, edges, halves, rates):
     bf16, f32 = jnp.bfloat16, jnp.float32
-    return pl.pallas_call(
-        inner_kernel,
-        in_specs=[vmem()] * 3,
-        out_specs=[vmem()] * 5,
-        out_shape=[
-            jax.ShapeDtypeStruct((8, CH, 8, 128), bf16),
-            jax.ShapeDtypeStruct((members, 12 * CH, 128), bf16),
-            jax.ShapeDtypeStruct((members, 4 * CH, 128), f32),
-            jax.ShapeDtypeStruct((3 * CH, 3 * CH), bf16),
-            jax.ShapeDtypeStruct((3 * CH, 3 * CH), bf16),
-        ],
-        scratch_shapes=[
-            pltpu.VMEM((14 * CH, 128), bf16),
-            pltpu.VMEM((12 * CH, 128), bf16),
-            pltpu.VMEM((10 * CH, 128), bf16),
-            pltpu.VMEM((12 * CH, 128), f32),
-            pltpu.VMEM((64 * CH, 128), f32),
-        ],
-        compiler_params=vmem_params(),
-        cost_estimate=pl.CostEstimate(
-            flops=12_000_000_000, bytes_accessed=8_000_000, transcendentals=2_000_000
-        ),
-    )(own, first_taps, second_taps)
-
-
-def edge_forecast(inner, cells, first, second, left, right, own, halves, rates):
-    bf16, f32 = jnp.bfloat16, jnp.float32
+    members = edges.shape[0]
     return pl.pallas_call(
         edge_kernel,
-        in_specs=[vmem()] * 9,
-        out_specs=[vmem()] * 2,
+        in_specs=[hbm(), vmem()] + [hbm()] * 6,
+        out_specs=[hbm()] * 2,
         out_shape=[
             jax.ShapeDtypeStruct((8, CH, 8, 128), bf16),
             jax.ShapeDtypeStruct((24, 8, 128), bf16),
         ],
         scratch_shapes=[
-            pltpu.VMEM((16 * CH, 128), bf16),
-            pltpu.VMEM((12 * CH, 128), bf16),
-            pltpu.VMEM((12 * CH, 128), bf16),
-            pltpu.VMEM((12 * CH, 128), bf16),
-            pltpu.VMEM((4 * CH, 128), f32),
+            pltpu.VMEM((2, 3 * CH, 3 * CH), bf16),
+            pltpu.VMEM((members, 16 * CH, 128), bf16),
+            pltpu.VMEM((members, 12 * CH, 128), bf16),
+            pltpu.VMEM((members, 12 * CH, 128), bf16),
+            pltpu.VMEM((members, 12 * CH, 128), bf16),
+            pltpu.VMEM((members, 4 * CH, 128), f32),
+            pltpu.VMEM((members, 4 * CH, 128), f32),
             pltpu.VMEM((128 * CH, 128), f32),
+            pltpu.VMEM((8, CH, 8, 128), bf16),
+            pltpu.VMEM((8, CH, 8, 128), bf16),
+            pltpu.VMEM((2, 32, 128), bf16),
+            pltpu.VMEM((24, 8, 128), bf16),
             pltpu.VMEM((2, 24, 128), jnp.int32),
             pltpu.SMEM((24, 128), jnp.int32),
             pltpu.SMEM((24, 128), jnp.int32),
+            pltpu.SemaphoreType.DMA((members // PAIR_B, 8 + 2 * PAIR_B)),
+            pltpu.SemaphoreType.DMA((4,)),
+            pltpu.SemaphoreType.DMA((2,)),
             pltpu.SemaphoreType.DMA((2,)),
         ],
         compiler_params=vmem_params(),
         cost_estimate=pl.CostEstimate(
             flops=9_000_000_000, bytes_accessed=8_000_000, transcendentals=2_000_000
         ),
-    )(inner, cells, first, second, left, right, own, halves, rates)
+    )(inner, cells, taps, left, right, edges, halves, rates)
 
 
 def transform_kernel(here, pair, ahead, across, behind, cells, numbers, observed, variance, out, stack):
@@ -328,20 +420,29 @@
     )(*pieces, cells, numbers, observed, variance)
 
 
-def mix_kernel(inner, edge, weights, out):
+def mix_kernel(inner, edge, weights, out, cells, sems):
     w = weights[...]
-
-    def block(k, carry):
+    blocks = CH // 8
+    copies = []
+    for k in range(blocks):
         for x, parts in enumerate((inner, edge)):
+            copy = pltpu.make_async_copy(
+                parts.at[:, pl.ds(8 * k, 8)], cells.at[x, k], sems.at[x, k]
+            )
+            copy.start()
+            copies.append(copy)
+    for k in range(blocks):
+        for x in range(2):
+            copies[2 * k + x].wait()
             centers = []
             halves = []
             for half in range(2):
                 stack = []
                 for q in range(4):
-                    cells = parts[:, 8 * k + 4 * half + q].astype(jnp.float32)
-                    center = jnp.sum(jnp.sum(cells, axis=0), axis=0, keepdims=True) * (1.0 / 64.0)
+                    value = cells[x, k, :, 4 * half + q].astype(jnp.float32)
+                    center = jnp.sum(jnp.sum(value, axis=0), axis=0, keepdims=True) * (1.0 / 64.0)
                     centers.append(center)
-                    stack.append((cells.reshape(64, 128) - center).astype(jnp.bfloat16))
+                    stack.append((value.reshape(64, 128) - center).astype(jnp.bfloat16))
                 halves.append(jnp.concatenate(stack, axis=0))
             mixed = jnp.dot(
                 w, jnp.concatenate(halves, axis=1), preferred_element_type=jnp.float32
@@ -351,17 +452,18 @@
                     value = mixed[64 * q : 64 * q + 64, 128 * half : 128 * half + 128]
                     value = value + centers[4 * half + q]
                     out[:, x, 8 * k + 4 * half + q] = value.astype(jnp.bfloat16).reshape(8, 8, 128)
-        return carry
-
-    lax.fori_loop(0, CH // 8, block, 0)
 
 
 def mix(inner, edge, weights):
     return pl.pallas_call(
         mix_kernel,
-        in_specs=[vmem()] * 3,
+        in_specs=[pl.BlockSpec(memory_space=pl.ANY)] * 2 + [vmem()],
         out_specs=vmem(),
         out_shape=jax.ShapeDtypeStruct((8, 2, CH, 8, 128), jnp.bfloat16),
+        scratch_shapes=[
+            pltpu.VMEM((2, CH // 8, 8, 8, 8, 128), jnp.bfloat16),
+            pltpu.SemaphoreType.DMA((2, CH // 8)),
+        ],
         compiler_params=vmem_params(),
         cost_estimate=pl.CostEstimate(
             flops=700_000_000, bytes_accessed=5_300_000, transcendentals=0
@@ -446,11 +548,11 @@
     left = ring(jnp.concatenate([tail, digits]), 1)
     right = ring(jnp.concatenate([head, digits]), -1)
 
-    inner, halves, rates, first, second = inner_forecast(
+    inner, halves, rates, edges, taps = inner_forecast(
         own, initial_kernel_taps, latter_kernel_taps
     )
     inner_parts = lax.all_to_all(inner, "mem", split_axis=0, concat_axis=0, tiled=True)
-    edge, picked = edge_forecast(inner, cells, first, second, left, right, own, halves, rates)
+    edge, picked = edge_forecast(inner, cells, taps, left, right, edges, halves, rates)
     edge_parts = lax.all_to_all(edge, "mem", split_axis=0, concat_axis=0, tiled=True)
 
     picked = picked.reshape(3, 8, 8, 128)

time: 135 us -> 128 us (0.948)
  Pallas kernels: 41.8 us -> 36.6 us
  local copies, waits for them, and re-layouts: 12.8 us -> 11.2 us
    pallas_call x3, Pallas kernels: 36.9 us -> 31.7 us  [the longest x1 15 us: edge_forecast(): pl.pallas_call(edge_kernel, in_specs=[hbm(), vmem()] + [hbm()] * 6, out_s...]
    unnamed x28 -> x24, local copies, waits for them, and re-layouts: 10.2 us -> 8.66 us
  transfers between devices with their start and end apart: 10 -> 10, of which waited for: 5 -> 5; matrix products, arithmetic and copies ran while one was open for 0% -> 0% of each run, Pallas kernels for 26% -> 23%
where the time goes in v3:
time: 128 us
  Pallas kernels  36.6 us (29%)
  blocking collectives  34.2 us (27%)
  starting transfers between devices  27.6 us (22%)
  waiting for transfers between devices  14.4 us (11%)
  local copies, waits for them, and re-layouts  11.2 us (9%)
  other arithmetic  2.35 us (2%)
  between operations  1.63 us (1%)
    all_to_all x1, blocking collectives, per_device(): back = lax.all_to_all(mixed, 'mem', split_axis=0, concat_axis=0, tiled=True)  34.2 us
    pallas_call x1, Pallas kernels, edge_forecast(): pl.pallas_call(edge_kernel, in_specs=[hbm(), vmem()] + [hbm()] * 6, out_s...  15 us
    pallas_call x1, Pallas kernels, inner_forecast(): pl.pallas_call(inner_kernel, in_specs=[vmem()] * 3, out_specs=[hbm()] * 5...  11.3 us
    unnamed x24, local copies, waits for them, and re-layouts  8.66 us
    ppermute x1, waiting for transfers between devices, per_device(): pair = lax.ppermute(here, 'mem', [(i, i ^ 4) for i in range(8)])  8.47 us
    all_to_all x1, starting transfers between devices, per_device(): lax.all_to_all(inner, 'mem', split_axis=0, concat_axis=0, tiled=True)  8.08 us
    all_to_all x1, starting transfers between devices, per_device(): lax.all_to_all(edge, 'mem', split_axis=0, concat_axis=0, tiled=True)  7.33 us
    pallas_call x1, Pallas kernels, mix(): pl.pallas_call(mix_kernel, in_specs=[pl.BlockSpec(memory_space=pl.ANY)] *...  5.35 us
  transfers between devices with their start and end apart: 10, of which 5 were waited for; matrix products, arithmetic and copies ran while one was open for 0% of the time, Pallas kernels for 23%

profile of v3, /device:TPU:6, one launch (start us, length us, event | category | flops | bytes accessed | tf_op | source)
XLA Modules:
  0.0 127.9 jit_solution(15139319401279413193)
XLA Ops:
  0.7 2.4 %copy.9 = bf16[8,16,80,128]{3,2,1,0:T(8,128)(2,1)S(1)} copy(bf16[8,16,80,128]{3,1,2,0:T(8,128)(2,1)} %bitcast.21) | data formatting | bytes 5242880 | tf_op jit(solution)/shard_map/transpose | solution.py:542
  3.3 1.5 %fusion.1 = (bf16[2592,128]{1,0:T(8,128)(2,1)}, bf16[2592,128]{1,0:T(8,128)(2,1)}) fusion(bf16[24,128]{1,0:T(8,128)(2,1)S(1)} %maximum_bitcast_fusion, bf16[2560,128]{1,0:T(8,128)(2,1)S(1)} %bitcast.22, bf16[2592]{0:T(1024)(128)(2,1)S(1)} %pad.11.clone, bf16[2560,128]{1,0:T(8,128)(2,1)S(1)} %bitcast.23), kind=kLoop, calls=%fused_computation.3 | loop fusion | flops 3317760 | bytes 2649152 | tf_op jit(solution)/shard_map/concatenate | solution.py:549
  4.8 1.7 %collective-permute-start.1 = (bf16[2592,128]{1,0:T(8,128)(2,1)}, bf16[2592,128]{1,0:T(8,128)(2,1)S(1)}, u32[]{:S(2)}, u32[]{:S(2)}) collective-permute-start(bf16[2592,128]{1,0:T(8,128)(2,1)} %get-tuple-element.25), channel_id=1, source_target_pairs={{0,120},{8,0},{16,8},{24,16},{32,24},{40,32},{48,40},{56,48},{64,5... | collective-permute-start | bytes 1990664 | tf_op jit(solution)/shard_map/ppermute | solution.py:521
  6.6 11.3 %shard_map.82 = (bf16[8,80,8,128]{3,2,1,0:T(8,128)(2,1)}, bf16[8,960,128]{2,1,0:T(8,128)(2,1)S(1)}, f32[8,320,128]{2,1,0:T(8,128)S(1)}, bf16[8,640,128]{2,1,0:T(8,128)(2,1)S(1)}, bf16[2,240,240]{2,1,0:T(8,128)(2,1)S(1)}) custom-call(bf16[8,1280,128]{2,1,0:T(8,128)(2,1)S(1)} %bitcast.15, bf16[9,80,80]{2,1,0:T(8,128)(2,1)S(1)} %copy-done.2, ...), custom_call_target="tpu_custom_call" | custom-call | flops 12000000000 | bytes 8000000 | tf_op jit(solution)/shard_map/pallas_call | solution.py:129
  17.9 1.3 copy-done.6
  19.2 1.1 copy-done.8
  20.3 1.1 copy-done.10
  21.3 8.1 %all-to-all-start = ((bf16[8,80,8,128]{3,2,1,0:T(8,128)(2,1)}), bf16[8,80,8,128]{3,2,1,0:T(8,128)(2,1)S(1)}, u32[]{:S(2)}, u32[]{:S(2)}) async-start(bf16[8,80,8,128]{3,2,1,0:T(8,128)(2,1)} %get-tuple-element.12.inner), calls=%async_computation | async-start | bytes 2621440 | tf_op jit(solution)/shard_map/all_to_all | solution.py:554
  29.5 1.5 %copy-done.7 = bf16[8,960,128]{2,1,0:T(8,128)(2,1)S(1)} copy-done((bf16[8,960,128]{2,1,0:T(8,128)(2,1)S(1)}, bf16[8,960,128]{2,1,0:T(8,128)(2,1)}, u32[]{:S(2)}) %copy-start.7) | copy-done | bytes 1966104
  31.0 1.3 %copy-done.9 = f32[8,320,128]{2,1,0:T(8,128)S(1)} copy-done((f32[8,320,128]{2,1,0:T(8,128)S(1)}, f32[8,320,128]{2,1,0:T(8,128)}, u32[]{:S(2)}) %copy-start.9) | copy-done | bytes 1310744
  32.3 1.3 %copy-done.11 = bf16[8,640,128]{2,1,0:T(8,128)(2,1)S(1)} copy-done((bf16[8,640,128]{2,1,0:T(8,128)(2,1)S(1)}, bf16[8,640,128]{2,1,0:T(8,128)(2,1)}, u32[]{:S(2)}) %copy-start.11) | copy-done | bytes 1310744
  33.6 15.0 %shard_map.83 = (bf16[8,80,8,128]{3,2,1,0:T(8,128)(2,1)S(1)}, bf16[24,8,128]{2,1,0:T(8,128)(2,1)S(1)}) custom-call(bf16[8,80,8,128]{3,2,1,0:T(8,128)(2,1)} %get-tuple-element.12.inner, s32[8,128]{1,0:T(8,128)S(1)} %bitcast.18, bf16[2,240,240]{2,1,0:T(8,128)(2,1)S(1)} %get-tuple-element.13.taps_in, bf16[2592,128]{1,0:T(8,128)(2,1)S(1)} %collective-permute-done.left, ...), custom_call_target="tpu_custom_call" | custom-call | flops 8999999488 | bytes 8000000 | tf_op jit(solution)/shard_map/pallas_call | solution.py:306
  48.7 1.0 copy-done
  49.7 7.3 %all-to-all-start.1 = ((bf16[8,80,8,128]{3,2,1,0:T(8,128)(2,1)}), bf16[8,80,8,128]{3,2,1,0:T(8,128)(2,1)S(1)}, u32[]{:S(2)}, u32[]{:S(2)}) async-start(bf16[8,80,8,128]{3,2,1,0:T(8,128)(2,1)} %copy-done), calls=%async_computation.1 | async-start | bytes 2621440 | tf_op jit(solution)/shard_map/all_to_all | solution.py:556
  57.2 1.7 %collective-permute-start.3 = (bf16[8,8,128]{2,1,0:T(8,128)(2,1)S(1)}, bf16[8,8,128]{2,1,0:T(8,128)(2,1)S(1)}, u32[]{:S(2)}, u32[]{:S(2)}) collective-permute-start(bf16[8,8,128]{2,1,0:T(8,128)(2,1)S(1)} %get-tuple-element.23), channel_id=1, source_target_pairs={{0,120},{8,0},{16,8},{24,16},{32,24},{40,32},{48,40},{56,48},{64,5... | collective-permute-start | bytes 49160 | tf_op jit(solution)/shard_map/ppermute | solution.py:521
  58.9 1.4 %collective-permute-done.2 = bf16[8,8,128]{2,1,0:T(8,128)(2,1)S(1)} collective-permute-done((bf16[8,8,128]{2,1,0:T(8,128)(2,1)S(1)}, bf16[8,8,128]{2,1,0:T(8,128)(2,1)S(1)}, u32[]{:S(2)}, u32[]{:S(2)}) %collective-permute-start.2) | collective-permute-done | bytes 16416 | tf_op jit(solution)/shard_map/ppermute | solution.py:521
  60.7 4.2 %collective-permute-start.4 = (bf16[8,8,128]{2,1,0:T(8,128)(2,1)S(1)}, bf16[8,8,128]{2,1,0:T(8,128)(2,1)S(1)}, u32[]{:S(2)}, u32[]{:S(2)}) collective-permute-start(bf16[8,8,128]{2,1,0:T(8,128)(2,1)S(1)} %select_select_fusion.here), channel_id=1, source_target_pairs={{0,4},{1,5},{2,6},{3,7},{4,0},{5,1},{6,2},{7,3},{8,12},{9,13},{10,... | collective-permute-start | bytes 49160 | tf_op jit(solution)/shard_map/ppermute | solution.py:563
  66.2 8.5 %collective-permute-done.4.pair = bf16[8,8,128]{2,1,0:T(8,128)(2,1)S(1)} collective-permute-done((bf16[8,8,128]{2,1,0:T(8,128)(2,1)S(1)}, bf16[8,8,128]{2,1,0:T(8,128)(2,1)S(1)}, u32[]{:S(2)}, u32[]{:S(2)}) %collective-permute-start.4) | collective-permute-done | bytes 16416 | tf_op jit(solution)/shard_map/ppermute | solution.py:563
  74.7 2.7 %collective-permute-start.5 = (bf16[2,8,8,128]{3,2,1,0:T(8,128)(2,1)S(1)}, bf16[2,8,8,128]{3,2,1,0:T(8,128)(2,1)S(1)}, u32[]{:S(2)}, u32[]{:S(2)}) collective-permute-start(bf16[2,8,8,128]{3,2,1,0:T(8,128)(2,1)S(1)} %pad_maximum_fusion.2), channel_id=1, source_target_pairs={{1,0},{2,1},{3,2},{0,3},{5,4},{6,5},{7,6},{4,7},{9,8},{10,9},{11,1... | collective-permute-start | bytes 98312 | tf_op jit(solution)/shard_map/ppermute | solution.py:525
  79.2 3.6 %collective-permute-done.6.across = bf16[2,8,8,128]{3,2,1,0:T(8,128)(2,1)S(1)} collective-permute-done((bf16[2,8,8,128]{3,2,1,0:T(8,128)(2,1)S(1)}, bf16[2,8,8,128]{3,2,1,0:T(8,128)(2,1)S(1)}, u32[]{:S(2)}, u32[]{:S(2)}) %collective-permute-start.6) | collective-permute-done | bytes 32800 | tf_op jit(solution)/shard_map/ppermute | solution.py:525
  83.4 3.0 %shard_map.84.weights = bf16[256,256]{1,0:T(8,128)(2,1)S(1)} custom-call(bf16[8,8,128]{2,1,0:T(8,128)(2,1)S(1)} %select_select_fusion.here, bf16[8,8,128]{2,1,0:T(8,128)(2,1)S(1)} %collective-permute-done.4.pair, bf16[2,8,8,128]{3,2,1,0:T(8,128)(2,1)S(1)} %collective-permute-done.5.ahead, bf16[2,8,8,128]{3,2,1,0:T(8,128)(2,1)S(1)} %collective-permute-done.6.across, ...), custom_call_target="tpu_custom_call" | custom-call | flops 100000000 | bytes 500000 | tf_op jit(solution)/shard_map/pallas_call | solution.py:410
  86.4 5.3 %shard_map.85 = bf16[8,2,80,8,128]{4,3,2,1,0:T(8,128)(2,1)S(1)} custom-call(bf16[8,80,8,128]{3,2,1,0:T(8,128)(2,1)S(1)} %all-to-all-done.inner, bf16[8,80,8,128]{3,2,1,0:T(8,128)(2,1)S(1)} %all-to-all-done.1.edge, bf16[256,256]{1,0:T(8,128)(2,1)S(1)} %shard_map.84.weights), custom_call_target="tpu_custom_call" | custom-call | flops 700000000 | bytes 5300000 | tf_op jit(solution)/shard_map/pallas_call | solution.py:458
  91.8 34.2 %all_to_all.15 = bf16[8,2,80,8,128]{4,3,2,1,0:T(8,128)(2,1)S(1)} all-to-all(bf16[8,2,80,8,128]{4,3,2,1,0:T(8,128)(2,1)S(1)} %shard_map.85), channel_id=1, replica_groups=mesh['space'=16,'mem'=8] {'mem'}, dimensions={0} | all-to-all | bytes 5242880 | tf_op jit(solution)/shard_map/all_to_all | solution.py:575
  125.9 1.8 %shard_map.86 = bf16[8,80,16,128]{3,2,1,0:T(8,128)(2,1)} custom-call(bf16[16,80,8,128]{3,2,1,0:T(8,128)(2,1)S(1)} %bitcast.13), custom_call_target="tpu_custom_call" | custom-call | flops 600000000 | bytes 5300000 | tf_op jit(solution)/shard_map/pallas_call | solution.py:503
  (39 shorter events, 3.7 us)
Async XLA Ops:
  3.3 3.3 %copy-start.2 = (bf16[9,80,80]{2,1,0:T(8,128)(2,1)S(1)}, bf16[9,80,80]{2,1,0:T(8,128)(2,1)}, u32[]{:S(2)}) copy-start(bf16[9,80,80]{2,1,0:T(8,128)(2,1)} %first_taps.1) | copy-start | bytes 345604
  3.3 3.3 %copy-start.3 = (bf16[9,80,80]{2,1,0:T(8,128)(2,1)S(1)}, bf16[9,80,80]{2,1,0:T(8,128)(2,1)}, u32[]{:S(2)}) copy-start(bf16[9,80,80]{2,1,0:T(8,128)(2,1)} %second_taps.1) | copy-start | bytes 345604
  4.8 24.6 %collective-permute-start = (bf16[2592,128]{1,0:T(8,128)(2,1)}, bf16[2592,128]{1,0:T(8,128)(2,1)S(1)}, u32[]{:S(2)}, u32[]{:S(2)}) collective-permute-start(bf16[2592,128]{1,0:T(8,128)(2,1)} %get-tuple-element.26), channel_id=1, source_target_pairs={{0,8},{8,16},{16,24},{24,32},{32,40},{40,48},{48,56},{56,64},{64,7... | collective-permute-start | bytes 1990664 | tf_op jit(solution)/shard_map/ppermute | solution.py:521
  4.8 24.6 %collective-permute-start.1 = (bf16[2592,128]{1,0:T(8,128)(2,1)}, bf16[2592,128]{1,0:T(8,128)(2,1)S(1)}, u32[]{:S(2)}, u32[]{:S(2)}) collective-permute-start(bf16[2592,128]{1,0:T(8,128)(2,1)} %get-tuple-element.25), channel_id=1, source_target_pairs={{0,120},{8,0},{16,8},{24,16},{32,24},{40,32},{48,40},{56,48},{64,5... | collective-permute-start | bytes 1990664 | tf_op jit(solution)/shard_map/ppermute | solution.py:521
  17.9 1.3 copy-start.6
  19.2 1.1 copy-start.8
  20.3 1.1 copy-start.10
  21.3 8.1 %copy-start.1 = (s32[1,1024]{1,0:T(1,128)S(1)}, s32[1,1024]{1,0:T(1,128)}, u32[]{:S(2)}) copy-start(s32[1,1024]{1,0:T(1,128)} %cells.1) | copy-start | bytes 12292
  21.3 28.4 %all-to-all-start = ((bf16[8,80,8,128]{3,2,1,0:T(8,128)(2,1)}), bf16[8,80,8,128]{3,2,1,0:T(8,128)(2,1)S(1)}, u32[]{:S(2)}, u32[]{:S(2)}) async-start(bf16[8,80,8,128]{3,2,1,0:T(8,128)(2,1)} %get-tuple-element.12.inner), calls=%async_computation | async-start | bytes 2621440 | tf_op jit(solution)/shard_map/all_to_all | solution.py:554
  29.4 1.5 %copy-start.7 = (bf16[8,960,128]{2,1,0:T(8,128)(2,1)S(1)}, bf16[8,960,128]{2,1,0:T(8,128)(2,1)}, u32[]{:S(2)}) copy-start(bf16[8,960,128]{2,1,0:T(8,128)(2,1)} %copy-done.6) | copy-start | bytes 5898244
  31.0 1.3 %copy-start.9 = (f32[8,320,128]{2,1,0:T(8,128)S(1)}, f32[8,320,128]{2,1,0:T(8,128)}, u32[]{:S(2)}) copy-start(f32[8,320,128]{2,1,0:T(8,128)} %copy-done.8) | copy-start | bytes 3932164
  32.3 1.3 %copy-start.11 = (bf16[8,640,128]{2,1,0:T(8,128)(2,1)S(1)}, bf16[8,640,128]{2,1,0:T(8,128)(2,1)}, u32[]{:S(2)}) copy-start(bf16[8,640,128]{2,1,0:T(8,128)(2,1)} %copy-done.10) | copy-start | bytes 3932164
  48.7 1.1 copy-start
  49.7 33.6 %copy-start.4 = (f32[1,1024]{1,0:T(1,128)S(1)}, f32[1,1024]{1,0:T(1,128)}, u32[]{:S(2)}) copy-start(f32[1,1024]{1,0:T(1,128)} %observed.1) | copy-start | bytes 12292
  49.7 33.6 %copy-start.5 = (f32[1,1024]{1,0:T(1,128)S(1)}, f32[1,1024]{1,0:T(1,128)}, u32[]{:S(2)}) copy-start(f32[1,1024]{1,0:T(1,128)} %variance.1) | copy-start | bytes 12292
  49.7 36.7 %all-to-all-start.1 = ((bf16[8,80,8,128]{3,2,1,0:T(8,128)(2,1)}), bf16[8,80,8,128]{3,2,1,0:T(8,128)(2,1)S(1)}, u32[]{:S(2)}, u32[]{:S(2)}) async-start(bf16[8,80,8,128]{3,2,1,0:T(8,128)(2,1)} %copy-done), calls=%async_computation.1 | async-start | bytes 2621440 | tf_op jit(solution)/shard_map/all_to_all | solution.py:556
  57.1 3.2 %collective-permute-start.2 = (bf16[8,8,128]{2,1,0:T(8,128)(2,1)S(1)}, bf16[8,8,128]{2,1,0:T(8,128)(2,1)S(1)}, u32[]{:S(2)}, u32[]{:S(2)}) collective-permute-start(bf16[8,8,128]{2,1,0:T(8,128)(2,1)S(1)} %get-tuple-element.24), channel_id=1, source_target_pairs={{0,8},{8,16},{16,24},{24,32},{32,40},{40,48},{48,56},{56,64},{64,7... | collective-permute-start | bytes 49160 | tf_op jit(solution)/shard_map/ppermute | solution.py:521
  57.2 3.5 %collective-permute-start.3 = (bf16[8,8,128]{2,1,0:T(8,128)(2,1)S(1)}, bf16[8,8,128]{2,1,0:T(8,128)(2,1)S(1)}, u32[]{:S(2)}, u32[]{:S(2)}) collective-permute-start(bf16[8,8,128]{2,1,0:T(8,128)(2,1)S(1)} %get-tuple-element.23), channel_id=1, source_target_pairs={{0,120},{8,0},{16,8},{24,16},{32,24},{40,32},{48,40},{56,48},{64,5... | collective-permute-start | bytes 49160 | tf_op jit(solution)/shard_map/ppermute | solution.py:521
  60.7 14.0 %collective-permute-start.4 = (bf16[8,8,128]{2,1,0:T(8,128)(2,1)S(1)}, bf16[8,8,128]{2,1,0:T(8,128)(2,1)S(1)}, u32[]{:S(2)}, u32[]{:S(2)}) collective-permute-start(bf16[8,8,128]{2,1,0:T(8,128)(2,1)S(1)} %select_select_fusion.here), channel_id=1, source_target_pairs={{0,4},{1,5},{2,6},{3,7},{4,0},{5,1},{6,2},{7,3},{8,12},{9,13},{10,... | collective-permute-start | bytes 49160 | tf_op jit(solution)/shard_map/ppermute | solution.py:563
  74.7 4.5 %collective-permute-start.5 = (bf16[2,8,8,128]{3,2,1,0:T(8,128)(2,1)S(1)}, bf16[2,8,8,128]{3,2,1,0:T(8,128)(2,1)S(1)}, u32[]{:S(2)}, u32[]{:S(2)}) collective-permute-start(bf16[2,8,8,128]{3,2,1,0:T(8,128)(2,1)S(1)} %pad_maximum_fusion.2), channel_id=1, source_target_pairs={{1,0},{2,1},{3,2},{0,3},{5,4},{6,5},{7,6},{4,7},{9,8},{10,9},{11,1... | collective-permute-start | bytes 98312 | tf_op jit(solution)/shard_map/ppermute | solution.py:525
  77.4 5.4 %collective-permute-start.6 = (bf16[2,8,8,128]{3,2,1,0:T(8,128)(2,1)S(1)}, bf16[2,8,8,128]{3,2,1,0:T(8,128)(2,1)S(1)}, u32[]{:S(2)}, u32[]{:S(2)}) collective-permute-start(bf16[2,8,8,128]{3,2,1,0:T(8,128)(2,1)S(1)} %pad_maximum_fusion.2), channel_id=1, source_target_pairs={{2,0},{3,1},{0,2},{1,3},{6,4},{7,5},{4,6},{5,7},{10,8},{11,9},{8,1... | collective-permute-start | bytes 98312 | tf_op jit(solution)/shard_map/ppermute | solution.py:525
  78.2 5.1 %collective-permute-start.7 = (bf16[2,8,8,128]{3,2,1,0:T(8,128)(2,1)S(1)}, bf16[2,8,8,128]{3,2,1,0:T(8,128)(2,1)S(1)}, u32[]{:S(2)}, u32[]{:S(2)}) collective-permute-start(bf16[2,8,8,128]{3,2,1,0:T(8,128)(2,1)S(1)} %pad_maximum_fusion.2), channel_id=1, source_target_pairs={{3,0},{0,1},{1,2},{2,3},{7,4},{4,5},{5,6},{6,7},{11,8},{8,9},{9,10... | collective-permute-start | bytes 98312 | tf_op jit(solution)/shard_map/ppermute | solution.py:525

commit v4 on v3

v4 whole, which is shorter than its diff:
```python
import functools

import jax
import jax.numpy as jnp
from jax import lax
from jax.experimental import pallas as pl
from jax.experimental.pallas import tpu as pltpu
from jax.sharding import PartitionSpec as P

NS_ITERS = 4
STEP_SIZE = 0.5
HALO = 4
CH = 80
PAIR_A = 4
LAG = 3


def vmem_params():
    return pltpu.CompilerParams(vmem_limit_bytes=40 << 20)


def gelu(x):
    c = 0.7978845608028654
    return 0.5 * x * (1.0 + jnp.tanh(c * (x + 0.044715 * (x * x * x))))


def shifted_sum(p, lane):
    below = pltpu.roll(p[0:80], 1, axis=1)
    above = pltpu.roll(p[160:240], 127, axis=1)
    return p[80:160] + jnp.where(lane == 0, 0.0, below) + jnp.where(lane == 127, 0.0, above)


def conv_pair(source, at, taps, emit, k):
    lane = lax.broadcasted_iota(jnp.int32, (CH, 128), 1)
    window = jnp.concatenate(
        [source[pl.ds(CH * at, 3 * CH), :], source[pl.ds(CH * (at + 1), 3 * CH), :]], axis=1
    )
    partial = jnp.dot(taps, window, preferred_element_type=jnp.float32)
    emit(k, shifted_sum(partial[:, :128], lane))
    emit(k + 1, shifted_sum(partial[:, 128:], lane))


def build_taps(taps, matrix):
    for b in range(3):
        row = jnp.concatenate([taps[3 * a + b].astype(jnp.float32) for a in range(3)], axis=1)
        matrix[pl.ds(CH * b, CH), :] = row.astype(jnp.bfloat16)


def run_interleaved(jobs):
    for _, step in sorted(jobs, key=lambda job: job[0]):
        step()


def inner_kernel(
    own, first_taps, second_taps, out, left_halves, left_rates, right_halves, right_rates, taps_out,
    taps, h, s, g, rate, fields, cells16, sems,
):
    members = own.shape[0]
    build_taps(first_taps, taps.at[0])
    build_taps(second_taps, taps.at[1])
    a = taps[0]
    b = taps[1]
    copies = [
        pltpu.make_async_copy(taps, taps_out, sems.at[0]),
        pltpu.make_async_copy(
            own.at[:, pl.ds(12 * CH, 4 * CH)], right_halves.at[:, pl.ds(6 * CH, 4 * CH)], sems.at[1]
        ),
    ]
    for copy in copies:
        copy.start()

    def group(n, carry):
        jobs = []
        for i in range(PAIR_A):
            m = n * PAIR_A + i
            v, hm, sm, gm, rm = own.at[m], h.at[m], s.at[m], g.at[m], rate.at[m]

            def put_first(k, value, hm=hm):
                hm[pl.ds(CH * k, CH), :] = gelu(value).astype(jnp.bfloat16)

            def put_section(k, value, v=v, sm=sm, rm=rm):
                base = v[pl.ds(CH * (k + 2), CH), :].astype(jnp.float32)
                sm[pl.ds(CH * k, CH), :] = (base + STEP_SIZE * value).astype(jnp.bfloat16)
                rm[pl.ds(CH * k, CH), :] = base + 0.5 * STEP_SIZE * value

            def put_second(k, value, gm=gm):
                gm[pl.ds(CH * k, CH), :] = gelu(value).astype(jnp.bfloat16)

            def put_forecast(k, value, rm=rm, m=m):
                cells = rm[pl.ds(CH * (k + 2), CH), :] + 0.5 * STEP_SIZE * value
                fields[pl.ds(8 * CH * k + m, CH, stride=8), :] = cells

            stages = (
                (v, a, 14, put_first),
                (hm, b, 12, put_section),
                (sm, a, 10, put_second),
                (gm, b, 8, put_forecast),
            )
            for level, (source, matrix, columns, emit) in enumerate(stages):
                for k in range(0, columns, 2):
                    step = functools.partial(conv_pair, source, k, matrix, emit, k)
                    jobs.append(((k // 2 + LAG * level, i, level), step))
        run_interleaved(jobs)
        return carry

    lax.fori_loop(0, members // PAIR_A, group, 0)
    for k, (ref, at) in enumerate(((h, 12), (s, 10), (g, 8))):
        target = pl.ds(2 * CH * k, 2 * CH)
        copies.append(
            pltpu.make_async_copy(ref.at[:, pl.ds(0, 2 * CH)], left_halves.at[:, target], sems.at[2 + k])
        )
        copies.append(
            pltpu.make_async_copy(
                ref.at[:, pl.ds(CH * at, 2 * CH)], right_halves.at[:, target], sems.at[5 + k]
            )
        )
    pair = pl.ds(0, 2 * CH)
    copies.append(pltpu.make_async_copy(rate.at[:, pair], left_rates, sems.at[8]))
    copies.append(
        pltpu.make_async_copy(
            rate.at[:, pl.ds(CH * 10, 2 * CH)], right_rates.at[:, pair], sems.at[9]
        )
    )
    for copy in copies[2:]:
        copy.start()
    cells16[...] = fields[...].astype(jnp.bfloat16).reshape(cells16.shape)
    last = pltpu.make_async_copy(cells16, out.at[pl.ds(0, 8)], sems.at[10])
    last.start()
    for copy in copies:
        copy.wait()
    last.wait()


def vmem():
    return pl.BlockSpec(memory_space=pltpu.VMEM)


def anywhere():
    return pl.BlockSpec(memory_space=pl.ANY)


WIDE16 = 32768
WIDE32 = 16384


def inner_forecast(own, first_taps, second_taps):
    members = own.shape[0]
    bf16, f32 = jnp.bfloat16, jnp.float32
    return pl.pallas_call(
        inner_kernel,
        in_specs=[vmem()] * 3,
        out_specs=[anywhere()] * 6,
        out_shape=[
            jax.ShapeDtypeStruct((12, CH, 8, 128), bf16),
            jax.ShapeDtypeStruct((members, 6 * CH, 128), bf16),
            jax.ShapeDtypeStruct((members, 2 * CH, 128), f32),
            jax.ShapeDtypeStruct((members, WIDE16, 128), bf16),
            jax.ShapeDtypeStruct((members, WIDE32, 128), f32),
            jax.ShapeDtypeStruct((2, 3 * CH, 3 * CH), bf16),
        ],
        scratch_shapes=[
            pltpu.VMEM((2, 3 * CH, 3 * CH), bf16),
            pltpu.VMEM((members, 14 * CH, 128), bf16),
            pltpu.VMEM((members, 12 * CH, 128), bf16),
            pltpu.VMEM((members, 10 * CH, 128), bf16),
            pltpu.VMEM((members, 12 * CH, 128), f32),
            pltpu.VMEM((64 * CH, 128), f32),
            pltpu.VMEM((8, CH, 8, 128), bf16),
            pltpu.SemaphoreType.DMA((11,)),
        ],
        compiler_params=vmem_params(),
        cost_estimate=pl.CostEstimate(
            flops=12_000_000_000, bytes_accessed=8_000_000, transcendentals=2_000_000
        ),
    )(own, first_taps, second_taps)


def edge_loads(side, halves, rates, own, halo, v, h, s, g, rated, sems):
    members = v.shape[0]
    saved = 4 if side == 0 else 0
    copies = []
    for m in range(members):
        source = halo.at[pl.ds(CH * HALO * m, CH * HALO)]
        copies.append((source, v.at[m, pl.ds(0 if side == 0 else 4 * CH, 4 * CH)]))
    copies.append((own, v.at[:, pl.ds(4 * CH if side == 0 else 0, 4 * CH)]))
    for k, ref in enumerate((h, s, g)):
        copies.append((halves.at[:, pl.ds(2 * CH * k, 2 * CH)], ref.at[:, pl.ds(saved * CH, 2 * CH)]))
    copies.append((rates, rated))
    return [
        pltpu.make_async_copy(source, target, sems.at[i])
        for i, (source, target) in enumerate(copies)
    ]


def edge_columns(side, taps, v, h, s, g, rate, rated, fields, start):
    a = taps[0]
    b = taps[1]
    jobs = []
    made = 0 if side == 0 else 2
    for m in range(v.shape[0]):
        vm, hm, sm, gm, rm, rdm = v.at[m], h.at[m], s.at[m], g.at[m], rate.at[m], rated.at[m]

        def hidden(ref):
            def put(k, value):
                ref[pl.ds(CH * (made + k), CH), :] = gelu(value).astype(jnp.bfloat16)

            return put

        def section(k, value, vm=vm, sm=sm, rm=rm):
            base = vm[pl.ds(CH * (k + 2), CH), :].astype(jnp.float32)
            sm[pl.ds(CH * (made + k), CH), :] = (base + STEP_SIZE * value).astype(jnp.bfloat16)
            inside = k - 2 if side == 0 else k
            if 0 <= inside < 2:
                rm[pl.ds(CH * inside, CH), :] = base + 0.5 * STEP_SIZE * value

        def forecast(k, value, rm=rm, rdm=rdm, m=m):
            source = rm if (k < 2) == (side == 0) else rdm
            value = source[pl.ds(CH * (k % 2), CH), :] + 0.5 * STEP_SIZE * value
            value = value.astype(jnp.bfloat16).astype(jnp.float32)
            fields[pl.ds(start + 8 * CH * k + m, CH, stride=8), :] = value

        stages = (
            (vm, made, a, hidden(hm)),
            (hm, 0, b, section),
            (sm, 0, a, hidden(gm)),
            (gm, 0, b, forecast),
        )
        for level, (source, at, matrix, emit) in enumerate(stages):
            for k in (0, 2):
                step = functools.partial(conv_pair, source, at + k, matrix, emit, k)
                jobs.append(((level, m, k), step))
    run_interleaved(jobs)


def edge_scratch(members):
    bf16, f32 = jnp.bfloat16, jnp.float32
    return [
        pltpu.VMEM((members, 8 * CH, 128), bf16),
        pltpu.VMEM((members, 6 * CH, 128), bf16),
        pltpu.VMEM((members, 6 * CH, 128), bf16),
        pltpu.VMEM((members, 6 * CH, 128), bf16),
        pltpu.VMEM((members, 2 * CH, 128), f32),
        pltpu.VMEM((members, 2 * CH, 128), f32),
        pltpu.VMEM((4, CH, 8, 128), bf16),
        pltpu.SemaphoreType.DMA((members + 6,)),
    ]


def left_kernel(
    chunk, taps, halo, own, halves, rates, out, v, h, s, g, rate, rated, cells16, sems, fields
):
    copies = edge_loads(0, halves, rates, own.at[:, pl.ds(0, 4 * CH)], halo, v, h, s, g, rated, sems)
    for copy in copies:
        copy.start()
    for copy in copies:
        copy.wait()
    edge_columns(0, taps, v, h, s, g, rate, rated, fields, 0)
    cells16[...] = fields[...].astype(jnp.bfloat16).reshape(cells16.shape)
    last = pltpu.make_async_copy(cells16, out.at[pl.ds(8, 4)], sems.at[len(copies)])
    last.start()
    last.wait()


def left_forecast(chunk, taps, halo, own, halves, rates):
    members = own.shape[0]
    return pl.pallas_call(
        left_kernel,
        in_specs=[anywhere(), vmem()] + [anywhere()] * 4,
        out_specs=anywhere(),
        out_shape=jax.ShapeDtypeStruct((12, CH, 8, 128), jnp.bfloat16),
        scratch_shapes=edge_scratch(members) + [pltpu.VMEM((32 * CH, 128), jnp.float32)],
        input_output_aliases={0: 0},
        compiler_params=vmem_params(),
        cost_estimate=pl.CostEstimate(
            flops=5_000_000_000, bytes_accessed=4_000_000, transcendentals=1_000_000
        ),
    )(chunk, taps, halo, own, halves, rates)


def place_of(channel, lon, lat, part):
    slot = lax.broadcasted_iota(jnp.int32, (8, 128), 1)
    lon = lon - 16 * part
    column = jnp.where(lon < 4, lon + 8, jnp.where(lon < 12, lon - 4, lon))
    here = (lon >= 0) & (lon < 16)
    return jnp.where(here, (column * CH + channel) * 8, 0), (slot - lat) & 127


def right_kernel(
    chunk, cells, first_taps, second_taps, left, right, halves, rates, out, picked,
    v, h, s, g, rate, rated, cells16, sems, taps, fields, chunk16, lists, drawn, places, rows, turns, list_sems, place_sems,
):
    members = v.shape[0]
    digits = CH * HALO * members
    copies = edge_loads(
        1,
        halves,
        rates.at[:, pl.ds(0, 2 * CH)],
        halves.at[:, pl.ds(6 * CH, 4 * CH)],
        right, v, h, s, g, rated, sems,
    )
    list_copies = [
        pltpu.make_async_copy(source.at[pl.ds(digits, 32)], lists.at[i], list_sems.at[i])
        for i, source in enumerate((left, right))
    ]
    chunk_copy = pltpu.make_async_copy(chunk, chunk16, list_sems.at[2])
    for copy in list_copies + copies + [chunk_copy]:
        copy.start()
    build_taps(first_taps, taps.at[0])
    build_taps(second_taps, taps.at[1])
    for copy in list_copies:
        copy.wait()
    for k in range(3):
        if k == 1:
            cell = cells[...]
            strip = cell >> 7
            channel = (strip * 43691) >> 21
            parts = (channel, strip - 48 * channel, cell & 127)
        else:
            block = lists[k // 2].astype(jnp.float32).astype(jnp.int32)
            parts = (block[0:8], block[8:16], block[16:24])
        row, turn = place_of(*parts, 2 - k)
        places[0, pl.ds(8 * k, 8), :] = row
        places[1, pl.ds(8 * k, 8), :] = turn
    place_copies = [
        pltpu.make_async_copy(places.at[0], rows, place_sems.at[0]),
        pltpu.make_async_copy(places.at[1], turns, place_sems.at[1]),
    ]
    for copy in place_copies:
        copy.start()
    for copy in copies:
        copy.wait()
    edge_columns(1, taps, v, h, s, g, rate, rated, fields, 96 * CH)
    cells16[...] = fields[pl.ds(96 * CH, 32 * CH), :].astype(jnp.bfloat16).reshape(cells16.shape)
    out_copy = pltpu.make_async_copy(cells16, out, sems.at[len(copies)])
    out_copy.start()
    chunk_copy.wait()
    fields[pl.ds(0, 96 * CH), :] = chunk16[...].astype(jnp.float32).reshape(96 * CH, 128)
    for copy in place_copies:
        copy.wait()
    lane = lax.broadcasted_iota(jnp.int32, (8, 128), 1)

    def block(k, carry):
        acc = jnp.zeros((8, 128), jnp.float32)
        for j in range(128):
            cell = fields[pl.ds(pl.multiple_of(rows[k, j], 8), 8), :]
            acc = jnp.where(lane == j, pltpu.roll(cell, turns[k, j], axis=1), acc)
        drawn[k] = acc.astype(jnp.bfloat16)
        return carry

    lax.fori_loop(0, drawn.shape[0], block, 0)
    drawn_copy = pltpu.make_async_copy(drawn, picked, place_sems.at[2])
    drawn_copy.start()
    drawn_copy.wait()
    out_copy.wait()


def right_forecast(chunk, cells, first_taps, second_taps, left, right, halves, rates):
    bf16, f32 = jnp.bfloat16, jnp.float32
    members = halves.shape[0]
    return pl.pallas_call(
        right_kernel,
        in_specs=[anywhere()] + [vmem()] * 3 + [anywhere()] * 4,
        out_specs=[anywhere()] * 2,
        out_shape=[
            jax.ShapeDtypeStruct((4, CH, 8, 128), bf16),
            jax.ShapeDtypeStruct((24, 8, 128), bf16),
        ],
        scratch_shapes=edge_scratch(members) + [
            pltpu.VMEM((2, 3 * CH, 3 * CH), bf16),
            pltpu.VMEM((128 * CH, 128), f32),
            pltpu.VMEM((12, CH, 8, 128), bf16),
            pltpu.VMEM((2, 32, 128), bf16),
            pltpu.VMEM((24, 8, 128), bf16),
            pltpu.VMEM((2, 24, 128), jnp.int32),
            pltpu.SMEM((24, 128), jnp.int32),
            pltpu.SMEM((24, 128), jnp.int32),
            pltpu.SemaphoreType.DMA((3,)),
            pltpu.SemaphoreType.DMA((3,)),
        ],
        compiler_params=vmem_params(),
        cost_estimate=pl.CostEstimate(
            flops=5_000_000_000, bytes_accessed=8_000_000, transcendentals=1_000_000
        ),
    )(chunk, cells, first_taps, second_taps, left, right, halves, rates)


def transform_kernel(parts, cells, numbers, observed, variance, out, values, stack, sem):
    f32 = jnp.float32
    exact = lax.Precision.HIGHEST
    load = pltpu.make_async_copy(parts.at[:, pl.ds(40, 8)], values, sem)
    load.start()
    load.wait()
    for group in range(8):
        for block in range(8):
            stack[pl.ds(8 * group, 8), pl.ds(128 * block, 128)] = values[group, block].astype(f32)
    model_obs = stack[...]
    center = jnp.sum(model_obs, axis=0, keepdims=True) * (1.0 / 64.0)
    spread = model_obs - center
    cell = cells[...]
    strip = cell >> 7
    lon = strip - 48 * ((strip * 43691) >> 21)
    scaled = (lon.astype(f32) - 23.5) / numbers[1].astype(f32)
    taper = jnp.exp(-0.5 * scaled * scaled)
    slot = lax.broadcasted_iota(jnp.int32, cell.shape, 1)
    weight = jnp.where(slot < numbers[0], taper / variance[...], 0.0)
    weighted = spread * weight

    def product(x, y):
        return jnp.dot(x, y, precision=exact, preferred_element_type=f32)

    gram = lax.dot_general(
        weighted, spread, (((1,), (1,)), ((), ())), precision=exact, preferred_element_type=f32
    )
    right_side = jnp.sum(weighted * (observed[...] - center), axis=1, keepdims=True)
    i = lax.broadcasted_iota(jnp.int32, (64, 64), 0)
    j = lax.broadcasted_iota(jnp.int32, (64, 64), 1)
    eye = jnp.where(i == j, 1.0, 0.0).astype(f32)
    norm = 63.0 + jnp.sqrt(jnp.sum(jnp.sum(gram * gram, axis=1, keepdims=True), axis=0, keepdims=True))
    iterate = (63.0 * eye + gram) / norm
    root = 1.5 * eye - 0.5 * iterate
    iterate = product(iterate, root)
    for sweep in range(1, NS_ITERS):
        factor = 1.5 * eye - 0.5 * product(root, iterate)
        if sweep < NS_ITERS - 1:
            iterate = product(iterate, factor)
        root = product(factor, root)
    wide = jnp.broadcast_to(right_side, (64, 128))
    shift = product(root, product(root, wide)) / norm
    transform = (shift[:, :64] + jnp.sqrt(63.0 / norm) * root).astype(jnp.bfloat16)
    i = lax.broadcasted_iota(jnp.int32, (64, 256), 0)
    j = lax.broadcasted_iota(jnp.int32, (64, 256), 1)
    for q in range(4):
        place = jnp.where(j == i + 64 * q, 1.0, 0.0).astype(jnp.bfloat16)
        turned = lax.dot_general(
            transform, place, (((0,), (0,)), ((), ())), preferred_element_type=f32
        )
        out[pl.ds(64 * q, 64), :] = turned.astype(jnp.bfloat16)


def transform_of(parts, cells, numbers, observed, variance):
    smem = pl.BlockSpec(memory_space=pltpu.SMEM)
    return pl.pallas_call(
        transform_kernel,
        in_specs=[anywhere(), vmem(), smem, vmem(), vmem()],
        out_specs=vmem(),
        out_shape=jax.ShapeDtypeStruct((256, 256), jnp.bfloat16),
        scratch_shapes=[
            pltpu.VMEM((8, 8, 8, 128), jnp.bfloat16),
            pltpu.VMEM((64, 1024), jnp.float32),
            pltpu.SemaphoreType.DMA,
        ],
        compiler_params=vmem_params(),
        cost_estimate=pl.CostEstimate(
            flops=100_000_000, bytes_accessed=500_000, transcendentals=1000
        ),
    )(parts, cells, numbers, observed, variance)


def mix_rows(parts, first, w, out, start):
    centers = []
    halves = []
    for half in range(2):
        stack = []
        for q in range(4):
            value = parts[:, first + 4 * half + q].astype(jnp.float32)
            center = jnp.sum(jnp.sum(value, axis=0), axis=0, keepdims=True) * (1.0 / 64.0)
            centers.append(center)
            stack.append((value.reshape(64, 128) - center).astype(jnp.bfloat16))
        halves.append(jnp.concatenate(stack, axis=0))
    mixed = jnp.dot(w, jnp.concatenate(halves, axis=1), preferred_element_type=jnp.float32)
    for half in range(2):
        for q in range(4):
            value = mixed[64 * q : 64 * q + 64, 128 * half : 128 * half + 128]
            value = value + centers[4 * half + q]
            out[:, start + 4 * half + q] = value.astype(jnp.bfloat16).reshape(8, 8, 128)


def mix_kernel(first, second, weights, out):
    w = weights[...]

    def block(n, carry):
        for k in range(5):
            row = (5 * n + k) * 8
            mix_rows(first, row, w, out, row)
        return carry

    lax.fori_loop(0, 3, block, 0)
    for k in range(5):
        mix_rows(second, 8 * k, w, out, 120 + 8 * k)


def mix(first, second, weights):
    return pl.pallas_call(
        mix_kernel,
        in_specs=[vmem()] * 3,
        out_specs=vmem(),
        out_shape=jax.ShapeDtypeStruct((8, 160, 8, 128), jnp.bfloat16),
        compiler_params=vmem_params(),
        cost_estimate=pl.CostEstimate(
            flops=700_000_000, bytes_accessed=5_300_000, transcendentals=0
        ),
    )(first, second, weights)


CHUNKS = 5


def order_kernel(cells, out, scratch, sems):
    to = lax.broadcasted_iota(jnp.int32, (128, 128), 0)
    at = lax.broadcasted_iota(jnp.int32, (128, 128), 1)
    slot = at >> 3
    column = jnp.where(slot < 8, slot + 4, jnp.where(slot < 12, slot - 8, slot))
    move = jnp.where(to == (at & 7) * 16 + column, 1.0, 0.0).astype(jnp.bfloat16)

    def cell(i, c):
        if i < 12:
            return cells[(CH * i + c) // 120, (CH * i + c) % 120]
        return cells[(CH * (i - 12) + c) // 40, 120 + (CH * (i - 12) + c) % 40]

    def rows(c):
        return jnp.stack([cell(i, c) for i in range(16)]).reshape(128, 128)

    depth = CH // CHUNKS
    copies = []
    for chunk in range(CHUNKS):
        for c in range(depth * chunk, depth * (chunk + 1), 2):
            both = jnp.concatenate([rows(c), rows(c + 1)], axis=1)
            moved = jnp.dot(move, both, preferred_element_type=jnp.float32).astype(jnp.bfloat16)
            scratch[:, c] = moved[:, :128].reshape(8, 16, 128)
            scratch[:, c + 1] = moved[:, 128:].reshape(8, 16, 128)
        span = pl.ds(depth * chunk, depth)
        copy = pltpu.make_async_copy(scratch.at[:, span], out.at[:, span], sems.at[chunk])
        copy.start()
        copies.append(copy)
    for copy in copies:
        copy.wait()


def order(cells):
    return pl.pallas_call(
        order_kernel,
        in_specs=[vmem()],
        out_specs=anywhere(),
        out_shape=jax.ShapeDtypeStruct((8, CH, 16, 128), jnp.bfloat16),
        scratch_shapes=[
            pltpu.VMEM((8, CH, 16, 128), jnp.bfloat16),
            pltpu.SemaphoreType.DMA((CHUNKS,)),
        ],
        compiler_params=vmem_params(),
        cost_estimate=pl.CostEstimate(
            flops=600_000_000, bytes_accessed=5_300_000, transcendentals=0
        ),
    )(cells)


def ring(cells, step):
    count = lax.axis_size("space")
    return lax.ppermute(cells, "space", [(i, (i + step) % count) for i in range(count)])


def per_device(
    prior_ensemble,
    initial_kernel_taps,
    latter_kernel_taps,
    observed_cells,
    observed_count,
    local_radius,
    observed_value,
    error_variance,
):
    members = prior_ensemble.shape[0]
    bf16 = jnp.bfloat16
    own = jnp.swapaxes(prior_ensemble, 1, 2).reshape(members, 16 * CH, 128)
    cells = observed_cells.reshape(8, 128)
    digits = jnp.stack([cells // 6144, cells // 128 % 48, cells % 128]).reshape(24, 128).astype(bf16)
    digits = jnp.concatenate([digits, jnp.zeros((8, 128), bf16)])
    tail = own[:, (16 - HALO) * CH :].reshape(-1, 128)
    head = own[:, : HALO * CH].reshape(-1, 128)
    left = ring(jnp.concatenate([tail, digits]), 1)
    right = ring(jnp.concatenate([head, digits]), -1)

    chunk, left_halves, left_rates, right_halves, right_rates, taps = inner_forecast(
        own, initial_kernel_taps, latter_kernel_taps
    )
    chunk = left_forecast(chunk, taps, left, own, left_halves, left_rates)
    first_parts = lax.all_to_all(
        chunk.reshape(8, 120, 8, 128), "mem", split_axis=0, concat_axis=0, tiled=True
    )
    edge, picked = right_forecast(
        chunk, cells, initial_kernel_taps, latter_kernel_taps, left, right, right_halves, right_rates
    )

    picked = picked.reshape(3, 8, 8, 128)
    from_left = ring(picked[2], 1)
    from_right = ring(picked[0], -1)
    part = (cells // 128 % 48 // 16).reshape(8, 1, 128)
    here = jnp.where(part == 0, from_left, jnp.where(part == 1, picked[1], from_right))
    message = jnp.concatenate(
        [edge.reshape(8, 40, 8, 128), jnp.broadcast_to(here[None], (8, 8, 8, 128))], axis=1
    )
    second_parts = lax.all_to_all(message, "mem", split_axis=0, concat_axis=0, tiled=True)
    numbers = jnp.stack([observed_count[0], local_radius[0]])
    weights = transform_of(
        second_parts, observed_cells, numbers, observed_value, error_variance
    )
    mixed = mix(first_parts, second_parts, weights)
    back = lax.all_to_all(mixed, "mem", split_axis=0, concat_axis=0, tiled=True)
    return order(back)


def solution(mesh):
    return jax.shard_map(
        per_device,
        mesh=mesh,
        in_specs=(
            P("mem", None, "space", None),
            P(),
            P(),
            P("space", None),
            P("space"),
            P("space"),
            P("space", None),
            P("space", None),
        ),
        out_specs=P("mem", None, "space", None),
        check_vma=False,
    )
```

time: 128 us -> 135 us (1.055); the launches traced: 128 us -> 133 us
  blocking collectives: 34.2 us -> 59.1 us
  starting transfers between devices: 27.6 us -> 7.67 us
  waiting for transfers between devices: 14.4 us -> 23.5 us
  local copies, waits for them, and re-layouts: 11.2 us -> 2.63 us
    all_to_all x2 -> x1, waiting for transfers between devices: 0.01 us -> 20.9 us  [per_device(): lax.all_to_all(chunk.reshape(8, 120, 8, 128), 'mem', split_axis=0, concat...]
    all_to_all x0 -> x1, blocking collectives: none -> 19.3 us  [per_device(): lax.all_to_all(message, 'mem', split_axis=0, concat_axis=0, tiled=True)]
    ppermute x4 -> x0, waiting for transfers between devices: 12.7 us -> none  [the longest x1 8.47 us: per_device(): pair = lax.ppermute(here, 'mem', [(i, i ^ 4) for i in range(8)])]
    all_to_all x2 -> x1, starting transfers between devices: 15.4 us -> 3.89 us  [per_device(): lax.all_to_all(chunk.reshape(8, 120, 8, 128), 'mem', split_axis=0, concat...]
    unnamed x24 -> x10, local copies, waits for them, and re-layouts: 8.66 us -> 0.03 us
    ppermute x4 -> x0, starting transfers between devices: 8.6 us -> none  [the longest x3 4.39 us: depth_ring(): lax.ppermute(cells, 'mem', [(4 * y + (z + step) % 4, 4 * y + z) for y in...]
    all_to_all x1, blocking collectives: 34.2 us -> 39.8 us  [per_device(): back = lax.all_to_all(mixed, 'mem', split_axis=0, concat_axis=0, tiled=True)]
    pallas_call x5 -> x6, Pallas kernels: 36.6 us -> 37.1 us  [the longest x1 13 us: right_forecast(): pl.pallas_call(right_kernel, in_specs=[anywhere()] + [vmem()] * 3 + [anyw...]
  transfers between devices with their start and end apart: 10 -> 5, of which waited for: 5 -> 3; matrix products, arithmetic and copies ran while one was open for 0% -> 0% of each run, Pallas kernels for 23% -> 15%
where the time goes in v4:
time: 135 us; the launch traced here: 133 us
  blocking collectives  59.1 us (44%)
  Pallas kernels  37.1 us (27%)
  waiting for transfers between devices  23.5 us (17%)
  starting transfers between devices  7.67 us (6%)
  local copies, waits for them, and re-layouts  2.63 us (2%)
  between operations  1.62 us (1%)
    all_to_all x1, blocking collectives, per_device(): back = lax.all_to_all(mixed, 'mem', split_axis=0, concat_axis=0, tiled=True)  39.8 us
    all_to_all x1, waiting for transfers between devices, per_device(): lax.all_to_all(chunk.reshape(8, 120, 8, 128), 'mem', split_axis=0, concat...  20.9 us
    all_to_all x1, blocking collectives, per_device(): lax.all_to_all(message, 'mem', split_axis=0, concat_axis=0, tiled=True)  19.3 us
    pallas_call x1, Pallas kernels, right_forecast(): pl.pallas_call(right_kernel, in_specs=[anywhere()] + [vmem()] * 3 + [anyw...  13 us
    pallas_call x1, Pallas kernels, inner_forecast(): pl.pallas_call(inner_kernel, in_specs=[vmem()] * 3, out_specs=[anywhere()...  11.5 us
    pallas_call x1, Pallas kernels, left_forecast(): pl.pallas_call(left_kernel, in_specs=[anywhere(), vmem()] + [anywhere()]...  5.79 us
    all_to_all x1, starting transfers between devices, per_device(): lax.all_to_all(chunk.reshape(8, 120, 8, 128), 'mem', split_axis=0, concat...  3.89 us
    ppermute x4, starting transfers between devices, ring(): lax.ppermute(cells, 'space', [(i, (i + step) % count) for i in range(coun...  3.79 us
  transfers between devices with their start and end apart: 5, of which 3 were waited for; matrix products, arithmetic and copies ran while one was open for 0% of the time, Pallas kernels for 15%

profile of v4, /device:TPU:6, one launch (start us, length us, event | category | flops | bytes accessed | tf_op | source)
XLA Modules:
  0.0 133.0 jit_solution(13737194970607245330)
XLA Ops:
  0.0 0.7 fusion.2
  0.7 2.4 %copy.10 = bf16[8,16,80,128]{3,2,1,0:T(8,128)(2,1)S(1)} copy(bf16[8,16,80,128]{3,1,2,0:T(8,128)(2,1)} %bitcast.17) | data formatting | bytes 5242880 | tf_op jit(solution)/shard_map/transpose | solution.py:573
  3.1 0.1 fusion.13
  3.2 0.0 copy-start.1
  3.3 0.1 pad.9.clone
  3.3 0.4 fusion.1
  3.8 0.1 collective-permute-start
  3.8 1.7 %collective-permute-start.1 = (bf16[2592,128]{1,0:T(8,128)(2,1)S(1)}, bf16[2592,128]{1,0:T(8,128)(2,1)S(1)}, u32[]{:S(2)}, u32[]{:S(2)}) collective-permute-start(bf16[2592,128]{1,0:T(8,128)(2,1)S(1)} %get-tuple-element.27), channel_id=1, source_target_pairs={{0,120},{8,0},{16,8},{24,16},{32,24},{40,32},{48,40},{56,48},{64,5... | collective-permute-start | bytes 1990664 | tf_op jit(solution)/shard_map/ppermute | solution.py:558
  5.6 11.5 %shard_map.82 = (bf16[12,80,8,128]{3,2,1,0:T(8,128)(2,1)}, bf16[8,480,128]{2,1,0:T(8,128)(2,1)S(1)}, f32[8,160,128]{2,1,0:T(8,128)S(1)}, bf16[8,32768,128]{2,1,0...) custom-call(bf16[8,1280,128]{2,1,0:T(8,128)(2,1)S(1)} %bitcast.11, ...), custom_call_target="tpu_custom_call" | custom-call | flops 12000000000 | bytes 8000000 | tf_op jit(solution)/shard_map/pallas_call | solution.py:149
  17.1 5.8 %shard_map.83.chunk = bf16[12,80,8,128]{3,2,1,0:T(8,128)(2,1)} custom-call(bf16[12,80,8,128]{3,2,1,0:T(8,128)(2,1)} %get-tuple-element.13.chunk, bf16[2,240,240]{2,1,0:T(8,128)(2,1)S(1)} %get-tuple-element.14.taps, bf16[2592,128]{1,0:T(8,128)(2,1)S(1)} %collective-permute-done.halo.left, ...), custom_call_target="tpu_custom_call", output_to_operand_aliasing={{}: (0, {})} | custom-call | flops 5000000000 | bytes 4000000 | tf_op jit(solution)/shard_map/pallas_call | solution.py:266
  22.9 13.0 %shard_map.84 = (bf16[4,80,8,128]{3,2,1,0:T(8,128)(2,1)S(1)}, bf16[24,8,128]{2,1,0:T(8,128)(2,1)S(1)}) custom-call(bf16[12,80,8,128]{3,2,1,0:T(8,128)(2,1)} %shard_map.83.chunk, s32[8,128]{1,0:T(8,128)S(1)} %bitcast.16, bf16[9,80,80]{2,1,0:T(8,128)(2,1)S(1)} %copy-done, bf16[9,80,80]{2,1,0:T(8,128)(2,1)S(1)} %copy-done.1, ...), custom_call_target="tpu_custom_call" | custom-call | flops 5000000000 | bytes 8000000 | tf_op jit(solution)/shard_map/pallas_call | solution.py:360
  35.9 0.3 collective-permute-start.2
  36.1 1.7 %collective-permute-start.3 = (bf16[8,8,128]{2,1,0:T(8,128)(2,1)S(1)}, bf16[8,8,128]{2,1,0:T(8,128)(2,1)S(1)}, u32[]{:S(2)}, u32[]{:S(2)}) collective-permute-start(bf16[8,8,128]{2,1,0:T(8,128)(2,1)S(1)} %get-tuple-element.25), channel_id=1, source_target_pairs={{0,120},{8,0},{16,8},{24,16},{32,24},{40,32},{48,40},{56,48},{64,5... | collective-permute-start | bytes 49160 | tf_op jit(solution)/shard_map/ppermute | solution.py:558
  37.9 1.4 %collective-permute-done.2 = bf16[8,8,128]{2,1,0:T(8,128)(2,1)S(1)} collective-permute-done((bf16[8,8,128]{2,1,0:T(8,128)(2,1)S(1)}, bf16[8,8,128]{2,1,0:T(8,128)(2,1)S(1)}, u32[]{:S(2)}, u32[]{:S(2)}) %collective-permute-start.2) | collective-permute-done | bytes 16416 | tf_op jit(solution)/shard_map/ppermute | solution.py:558
  39.3 1.2 collective-permute-done.3
  40.6 0.1 pad_maximum_fusion.2
  40.6 19.3 %all_to_all.15.parts.second = bf16[8,48,8,128]{3,2,1,0:T(8,128)(2,1)S(1)} all-to-all(bf16[8,48,8,128]{3,2,1,0:T(8,128)(2,1)S(1)} %pad_maximum_fusion.2), channel_id=1, replica_groups=mesh['space'=16,'mem'=8] {'mem'}, dimensions={0} | all-to-all | bytes 1572864 | tf_op jit(solution)/shard_map/all_to_all | solution.py:601
  59.9 3.9 %all-to-all-start = ((bf16[8,120,8,128]{3,2,1,0:T(8,128)(2,1)}), bf16[8,120,8,128]{3,2,1,0:T(8,128)(2,1)S(1)}, u32[]{:S(2)}, u32[]{:S(2)}) async-start(bf16[8,120,8,128]{3,2,1,0:T(8,128)(2,1)} %bitcast.5), calls=%async_computation | async-start | bytes 3932160 | tf_op jit(solution)/shard_map/all_to_all | solution.py:586
  65.1 0.1 pad_add_fusion.numbers
  65.2 3.1 %shard_map.85.weights = bf16[256,256]{1,0:T(8,128)(2,1)S(1)} custom-call(bf16[8,48,8,128]{3,2,1,0:T(8,128)(2,1)S(1)} %all_to_all.15.parts.second, s32[1,1024]{1,0:T(1,128)S(1)} %copy-done.2, s32[2]{0:T(128)S(1)} %pad_add_fusion.numbers, f32[1,1024]{1,0:T(1,128)S(1)} %copy-done.3, f32[1,1024]{1,0:T(1,128)S(1)} %copy-done.4), custom_call_target="tpu_custom_call" | custom-call | flops 100000000 | bytes 500000 | tf_op jit(solution)/shard_map/pallas_call | solution.py:442
  68.3 20.9 %all-to-all-done.first = bf16[8,120,8,128]{3,2,1,0:T(8,128)(2,1)S(1)} async-done(((bf16[8,120,8,128]{3,2,1,0:T(8,128)(2,1)}), bf16[8,120,8,128]{3,2,1,0:T(8,128)(2,1)S(1)}, u32[]{:S(2)}, u32[]{:S(2)}) %all-to-all-start) | async-done | bytes 1966112 | tf_op jit(solution)/shard_map/all_to_all | solution.py:586
  89.2 2.0 %shard_map.86 = bf16[8,160,8,128]{3,2,1,0:T(8,128)(2,1)S(1)} custom-call(bf16[8,120,8,128]{3,2,1,0:T(8,128)(2,1)S(1)} %all-to-all-done.first, bf16[8,48,8,128]{3,2,1,0:T(8,128)(2,1)S(1)} %all_to_all.15.parts.second, bf16[256,256]{1,0:T(8,128)(2,1)S(1)} %shard_map.85.weights), custom_call_target="tpu_custom_call" | custom-call | flops 700000000 | bytes 5300000 | tf_op jit(solution)/shard_map/pallas_call | solution.py:493
  91.2 39.8 %all_to_all.16.cells = bf16[8,160,8,128]{3,2,1,0:T(8,128)(2,1)S(1)} all-to-all(bf16[8,160,8,128]{3,2,1,0:T(8,128)(2,1)S(1)} %shard_map.86), channel_id=1, replica_groups=mesh['space'=16,'mem'=8] {'mem'}, dimensions={0} | all-to-all | bytes 5242880 | tf_op jit(solution)/shard_map/all_to_all | solution.py:607
  131.0 1.8 %shard_map.87 = bf16[8,80,16,128]{3,2,1,0:T(8,128)(2,1)} custom-call(bf16[8,160,8,128]{3,2,1,0:T(8,128)(2,1)S(1)} %all_to_all.16.cells), custom_call_target="tpu_custom_call" | custom-call | flops 600000000 | bytes 5300000 | tf_op jit(solution)/shard_map/pallas_call | solution.py:540
  (18 shorter events, 0.1 us)
Async XLA Ops:
  3.2 2.4 %copy-start = (bf16[9,80,80]{2,1,0:T(8,128)(2,1)S(1)}, bf16[9,80,80]{2,1,0:T(8,128)(2,1)}, u32[]{:S(2)}) copy-start(bf16[9,80,80]{2,1,0:T(8,128)(2,1)} %first_taps.3) | copy-start | bytes 345604
  3.2 2.3 %copy-start.1 = (bf16[9,80,80]{2,1,0:T(8,128)(2,1)S(1)}, bf16[9,80,80]{2,1,0:T(8,128)(2,1)}, u32[]{:S(2)}) copy-start(bf16[9,80,80]{2,1,0:T(8,128)(2,1)} %second_taps.3) | copy-start | bytes 345604
  3.8 13.3 %collective-permute-start = (bf16[2592,128]{1,0:T(8,128)(2,1)S(1)}, bf16[2592,128]{1,0:T(8,128)(2,1)S(1)}, u32[]{:S(2)}, u32[]{:S(2)}) collective-permute-start(bf16[2592,128]{1,0:T(8,128)(2,1)S(1)} %get-tuple-element.28), channel_id=1, source_target_pairs={{0,8},{8,16},{16,24},{24,32},{32,40},{40,48},{48,56},{56,64},{64,7... | collective-permute-start | bytes 1990664 | tf_op jit(solution)/shard_map/ppermute | solution.py:558
  3.8 13.2 %copy-start.2 = (s32[1,1024]{1,0:T(1,128)S(1)}, s32[1,1024]{1,0:T(1,128)}, u32[]{:S(2)}) copy-start(s32[1,1024]{1,0:T(1,128)} %cells.1) | copy-start | bytes 12292
  3.8 19.0 %collective-permute-start.1 = (bf16[2592,128]{1,0:T(8,128)(2,1)S(1)}, bf16[2592,128]{1,0:T(8,128)(2,1)S(1)}, u32[]{:S(2)}, u32[]{:S(2)}) collective-permute-start(bf16[2592,128]{1,0:T(8,128)(2,1)S(1)} %get-tuple-element.27), channel_id=1, source_target_pairs={{0,120},{8,0},{16,8},{24,16},{32,24},{40,32},{48,40},{56,48},{64,5... | collective-permute-start | bytes 1990664 | tf_op jit(solution)/shard_map/ppermute | solution.py:558
  35.9 3.4 %collective-permute-start.2 = (bf16[8,8,128]{2,1,0:T(8,128)(2,1)S(1)}, bf16[8,8,128]{2,1,0:T(8,128)(2,1)S(1)}, u32[]{:S(2)}, u32[]{:S(2)}) collective-permute-start(bf16[8,8,128]{2,1,0:T(8,128)(2,1)S(1)} %get-tuple-element.26), channel_id=1, source_target_pairs={{0,8},{8,16},{16,24},{24,32},{32,40},{40,48},{48,56},{56,64},{64,7... | collective-permute-start | bytes 49160 | tf_op jit(solution)/shard_map/ppermute | solution.py:558
  36.1 4.4 %collective-permute-start.3 = (bf16[8,8,128]{2,1,0:T(8,128)(2,1)S(1)}, bf16[8,8,128]{2,1,0:T(8,128)(2,1)S(1)}, u32[]{:S(2)}, u32[]{:S(2)}) collective-permute-start(bf16[8,8,128]{2,1,0:T(8,128)(2,1)S(1)} %get-tuple-element.25), channel_id=1, source_target_pairs={{0,120},{8,0},{16,8},{24,16},{32,24},{40,32},{48,40},{56,48},{64,5... | collective-permute-start | bytes 49160 | tf_op jit(solution)/shard_map/ppermute | solution.py:558
  59.9 5.3 %copy-start.3 = (f32[1,1024]{1,0:T(1,128)S(1)}, f32[1,1024]{1,0:T(1,128)}, u32[]{:S(2)}) copy-start(f32[1,1024]{1,0:T(1,128)} %observed.1) | copy-start | bytes 12292
  59.9 5.3 %copy-start.4 = (f32[1,1024]{1,0:T(1,128)S(1)}, f32[1,1024]{1,0:T(1,128)}, u32[]{:S(2)}) copy-start(f32[1,1024]{1,0:T(1,128)} %variance.1) | copy-start | bytes 12292
  59.9 29.2 %all-to-all-start = ((bf16[8,120,8,128]{3,2,1,0:T(8,128)(2,1)}), bf16[8,120,8,128]{3,2,1,0:T(8,128)(2,1)S(1)}, u32[]{:S(2)}, u32[]{:S(2)}) async-start(bf16[8,120,8,128]{3,2,1,0:T(8,128)(2,1)} %bitcast.5), calls=%async_computation | async-start | bytes 3932160 | tf_op jit(solution)/shard_map/all_to_all | solution.py:586

commit v5 on v4

--- a/solution.py
+++ b/solution.py
@@ -598,6 +598,7 @@
     message = jnp.concatenate(
         [edge.reshape(8, 40, 8, 128), jnp.broadcast_to(here[None], (8, 8, 8, 128))], axis=1
     )
+    message, first_parts = lax.optimization_barrier((message, first_parts))
     second_parts = lax.all_to_all(message, "mem", split_axis=0, concat_axis=0, tiled=True)
     numbers = jnp.stack([observed_count[0], local_radius[0]])
     weights = transform_of(

time: 135 us -> 121 us (0.90); the launches traced: 133 us -> 121 us
  blocking collectives: 59.1 us -> 38.8 us
  starting transfers between devices: 7.67 us -> 16.3 us
  waiting for transfers between devices: 23.5 us -> 20.5 us
  other arithmetic: 1.31 us -> 3.06 us
    all_to_all x1 -> x0, blocking collectives: 19.3 us -> none  [per_device(): lax.all_to_all(message, 'mem', split_axis=0, concat_axis=0, tiled=True)]
    all_to_all x1, waiting for transfers between devices: 20.9 us -> 6.25 us  [per_device(): lax.all_to_all(chunk.reshape(8, 120, 8, 128), 'mem', split_axis=0, concat...]
    all_to_all x0 -> x1, waiting for transfers between devices: none -> 12.5 us  [per_device(): lax.all_to_all(message, 'mem', split_axis=0, concat_axis=0, tiled=True)]
    all_to_all x0 -> x1, starting transfers between devices: none -> 4.76 us  [per_device(): lax.all_to_all(message, 'mem', split_axis=0, concat_axis=0, tiled=True)]
    all_to_all x1, starting transfers between devices: 3.89 us -> 7.96 us  [per_device(): lax.all_to_all(chunk.reshape(8, 120, 8, 128), 'mem', split_axis=0, concat...]
  transfers between devices with their start and end apart: 5 -> 6, of which waited for: 3 -> 4; matrix products, arithmetic and copies ran while one was open for 0% -> 1% of each run, Pallas kernels for 15% -> 25%
where the time goes in v5:
time: 121 us
  blocking collectives  38.8 us (32%)
  Pallas kernels  37 us (31%)
  waiting for transfers between devices  20.5 us (17%)
  starting transfers between devices  16.3 us (13%)
  local copies, waits for them, and re-layouts  3.56 us (3%)
  other arithmetic  3.06 us (3%)
  between operations  1.62 us (1%)
    all_to_all x1, blocking collectives, per_device(): back = lax.all_to_all(mixed, 'mem', split_axis=0, concat_axis=0, tiled=True)  38.8 us
    pallas_call x1, Pallas kernels, right_forecast(): pl.pallas_call(right_kernel, in_specs=[anywhere()] + [vmem()] * 3 + [anyw...  12.9 us
    all_to_all x1, waiting for transfers between devices, per_device(): lax.all_to_all(message, 'mem', split_axis=0, concat_axis=0, tiled=True)  12.5 us
    pallas_call x1, Pallas kernels, inner_forecast(): pl.pallas_call(inner_kernel, in_specs=[vmem()] * 3, out_specs=[anywhere()...  11.5 us
    all_to_all x1, starting transfers between devices, per_device(): lax.all_to_all(chunk.reshape(8, 120, 8, 128), 'mem', split_axis=0, concat...  7.96 us
    all_to_all x1, waiting for transfers between devices, per_device(): lax.all_to_all(chunk.reshape(8, 120, 8, 128), 'mem', split_axis=0, concat...  6.25 us
    pallas_call x1, Pallas kernels, left_forecast(): pl.pallas_call(left_kernel, in_specs=[anywhere(), vmem()] + [anywhere()]...  5.79 us
    all_to_all x1, starting transfers between devices, per_device(): lax.all_to_all(message, 'mem', split_axis=0, concat_axis=0, tiled=True)  4.76 us
  transfers between devices with their start and end apart: 6, of which 4 were waited for; matrix products, arithmetic and copies ran while one was open for 1% of the time, Pallas kernels for 25%

profile of v5, /device:TPU:6, one launch (start us, length us, event | category | flops | bytes accessed | tf_op | source)
XLA Modules:
  0.0 120.8 jit_solution(9761632766224745478)
XLA Ops:
  0.0 0.7 fusion.2
  0.7 2.4 %copy.10 = bf16[8,16,80,128]{3,2,1,0:T(8,128)(2,1)S(1)} copy(bf16[8,16,80,128]{3,1,2,0:T(8,128)(2,1)} %bitcast.17) | data formatting | bytes 5242880 | tf_op jit(solution)/shard_map/transpose | solution.py:573
  3.1 0.1 fusion.13
  3.3 0.1 pad.9.clone
  3.3 1.3 %fusion.1 = (bf16[2592,128]{1,0:T(8,128)(2,1)}, bf16[2592,128]{1,0:T(8,128)(2,1)S(1)}) fusion(bf16[24,128]{1,0:T(8,128)(2,1)S(1)} %maximum_bitcast_fusion, bf16[2560,128]{1,0:T(8,128)(2,1)S(1)} %bitcast.18, bf16[2592]{0:T(1024)(128)(2,1)S(1)} %pad.9.clone, bf16[2560,128]{1,0:T(8,128)(2,1)S(1)} %bitcast.19), kind=kLoop, calls=%fused_computation.4 | loop fusion | flops 3317760 | bytes 2649152 | tf_op jit(solution)/shard_map/concatenate | solution.py:580
  4.6 1.7 %collective-permute-start.1 = (bf16[2592,128]{1,0:T(8,128)(2,1)}, bf16[2592,128]{1,0:T(8,128)(2,1)S(1)}, u32[]{:S(2)}, u32[]{:S(2)}) collective-permute-start(bf16[2592,128]{1,0:T(8,128)(2,1)} %get-tuple-element.31), channel_id=1, source_target_pairs={{0,120},{8,0},{16,8},{24,16},{32,24},{40,32},{48,40},{56,48},{64,5... | collective-permute-start | bytes 1990664 | tf_op jit(solution)/shard_map/ppermute | solution.py:558
  6.4 11.5 %shard_map.82 = (bf16[12,80,8,128]{3,2,1,0:T(8,128)(2,1)}, bf16[8,480,128]{2,1,0:T(8,128)(2,1)S(1)}, f32[8,160,128]{2,1,0:T(8,128)S(1)}, bf16[8,32768,128]{2,1,0...) custom-call(bf16[8,1280,128]{2,1,0:T(8,128)(2,1)S(1)} %bitcast.11, ...), custom_call_target="tpu_custom_call" | custom-call | flops 12000000000 | bytes 8000000 | tf_op jit(solution)/shard_map/pallas_call | solution.py:149
  17.8 5.8 %shard_map.83.chunk = bf16[12,80,8,128]{3,2,1,0:T(8,128)(2,1)} custom-call(bf16[12,80,8,128]{3,2,1,0:T(8,128)(2,1)} %get-tuple-element.15.chunk, bf16[2,240,240]{2,1,0:T(8,128)(2,1)S(1)} %get-tuple-element.16.taps, bf16[2592,128]{1,0:T(8,128)(2,1)S(1)} %collective-permute-done.halo.left, ...), custom_call_target="tpu_custom_call", output_to_operand_aliasing={{}: (0, {})} | custom-call | flops 5000000000 | bytes 4000000 | tf_op jit(solution)/shard_map/pallas_call | solution.py:266
  23.6 8.0 %all-to-all-start = ((bf16[8,120,8,128]{3,2,1,0:T(8,128)(2,1)}), bf16[8,120,8,128]{3,2,1,0:T(8,128)(2,1)S(1)}, u32[]{:S(2)}, u32[]{:S(2)}) async-start(bf16[8,120,8,128]{3,2,1,0:T(8,128)(2,1)} %bitcast.8), calls=%async_computation | async-start | bytes 3932160 | tf_op jit(solution)/shard_map/all_to_all | solution.py:586
  31.7 0.9 copy-done.2
  32.6 12.9 %shard_map.84 = (bf16[4,80,8,128]{3,2,1,0:T(8,128)(2,1)S(1)}, bf16[24,8,128]{2,1,0:T(8,128)(2,1)S(1)}) custom-call(bf16[12,80,8,128]{3,2,1,0:T(8,128)(2,1)} %shard_map.83.chunk, s32[8,128]{1,0:T(8,128)S(1)} %bitcast.16, bf16[9,80,80]{2,1,0:T(8,128)(2,1)S(1)} %copy-done, bf16[9,80,80]{2,1,0:T(8,128)(2,1)S(1)} %copy-done.2, ...), custom_call_target="tpu_custom_call" | custom-call | flops 5000000000 | bytes 8000000 | tf_op jit(solution)/shard_map/pallas_call | solution.py:360
  45.5 0.1 collective-permute-start.2
  45.6 1.7 %collective-permute-start.3 = (bf16[8,8,128]{2,1,0:T(8,128)(2,1)S(1)}, bf16[8,8,128]{2,1,0:T(8,128)(2,1)S(1)}, u32[]{:S(2)}, u32[]{:S(2)}) collective-permute-start(bf16[8,8,128]{2,1,0:T(8,128)(2,1)S(1)} %get-tuple-element.29), channel_id=1, source_target_pairs={{0,120},{8,0},{16,8},{24,16},{32,24},{40,32},{48,40},{56,48},{64,5... | collective-permute-start | bytes 49160 | tf_op jit(solution)/shard_map/ppermute | solution.py:558
  47.4 1.4 %collective-permute-done.2 = bf16[8,8,128]{2,1,0:T(8,128)(2,1)S(1)} collective-permute-done((bf16[8,8,128]{2,1,0:T(8,128)(2,1)S(1)}, bf16[8,8,128]{2,1,0:T(8,128)(2,1)S(1)}, u32[]{:S(2)}, u32[]{:S(2)}) %collective-permute-start.2) | collective-permute-done | bytes 16416 | tf_op jit(solution)/shard_map/ppermute | solution.py:558
  48.8 0.3 collective-permute-done.3
  49.1 1.0 pad_maximum_fusion.2
  50.1 6.2 %all-to-all-done.first = bf16[8,120,8,128]{3,2,1,0:T(8,128)(2,1)S(1)} async-done(((bf16[8,120,8,128]{3,2,1,0:T(8,128)(2,1)}), bf16[8,120,8,128]{3,2,1,0:T(8,128)(2,1)S(1)}, u32[]{:S(2)}, u32[]{:S(2)}) %all-to-all-start) | async-done | bytes 1966112 | tf_op jit(solution)/shard_map/all_to_all | solution.py:586
  56.3 4.8 %all-to-all-start.1 = ((bf16[8,48,8,128]{3,2,1,0:T(8,128)(2,1)}), bf16[8,48,8,128]{3,2,1,0:T(8,128)(2,1)S(1)}, u32[]{:S(2)}, u32[]{:S(2)}) async-start(bf16[8,48,8,128]{3,2,1,0:T(8,128)(2,1)} %pad_maximum_fusion.2), calls=%async_computation.1 | async-start | bytes 1572864 | tf_op jit(solution)/shard_map/all_to_all | solution.py:602
  62.4 0.1 pad_add_fusion.numbers
  62.5 12.5 %all-to-all-done.1.parts.second = bf16[8,48,8,128]{3,2,1,0:T(8,128)(2,1)S(1)} async-done(((bf16[8,48,8,128]{3,2,1,0:T(8,128)(2,1)}), bf16[8,48,8,128]{3,2,1,0:T(8,128)(2,1)S(1)}, u32[]{:S(2)}, u32[]{:S(2)}) %all-to-all-start.1) | async-done | bytes 786464 | tf_op jit(solution)/shard_map/all_to_all | solution.py:602
  75.0 3.1 %shard_map.85.weights = bf16[256,256]{1,0:T(8,128)(2,1)S(1)} custom-call(bf16[8,48,8,128]{3,2,1,0:T(8,128)(2,1)S(1)} %all-to-all-done.1.parts.second, s32[1,1024]{1,0:T(1,128)S(1)} %copy-done.3, s32[2]{0:T(128)S(1)} %pad_add_fusion.numbers, f32[1,1024]{1,0:T(1,128)S(1)} %copy-done.4, f32[1,1024]{1,0:T(1,128)S(1)} %copy-done.5), custom_call_target="tpu_custom_call" | custom-call | flops 100000000 | bytes 500000 | tf_op jit(solution)/shard_map/pallas_call | solution.py:442
  78.0 2.0 %shard_map.86 = bf16[8,160,8,128]{3,2,1,0:T(8,128)(2,1)S(1)} custom-call(bf16[8,120,8,128]{3,2,1,0:T(8,128)(2,1)S(1)} %all-to-all-done.first, bf16[8,48,8,128]{3,2,1,0:T(8,128)(2,1)S(1)} %all-to-all-done.1.parts.second, bf16[256,256]{1,0:T(8,128)(2,1)S(1)} %shard_map.85.weights), custom_call_target="tpu_custom_call" | custom-call | flops 700000000 | bytes 5300000 | tf_op jit(solution)/shard_map/pallas_call | solution.py:493
  80.0 38.8 %all_to_all.15.cells = bf16[8,160,8,128]{3,2,1,0:T(8,128)(2,1)S(1)} all-to-all(bf16[8,160,8,128]{3,2,1,0:T(8,128)(2,1)S(1)} %shard_map.86), channel_id=1, replica_groups=mesh['space'=16,'mem'=8] {'mem'}, dimensions={0} | all-to-all | bytes 5242880 | tf_op jit(solution)/shard_map/all_to_all | solution.py:608
  118.8 1.8 %shard_map.87 = bf16[8,80,16,128]{3,2,1,0:T(8,128)(2,1)} custom-call(bf16[8,160,8,128]{3,2,1,0:T(8,128)(2,1)S(1)} %all_to_all.15.cells), custom_call_target="tpu_custom_call" | custom-call | flops 600000000 | bytes 5300000 | tf_op jit(solution)/shard_map/pallas_call | solution.py:540
  (21 shorter events, 0.1 us)
Async XLA Ops:
  3.2 3.1 %copy-start = (bf16[9,80,80]{2,1,0:T(8,128)(2,1)S(1)}, bf16[9,80,80]{2,1,0:T(8,128)(2,1)}, u32[]{:S(2)}) copy-start(bf16[9,80,80]{2,1,0:T(8,128)(2,1)} %first_taps.3) | copy-start | bytes 345604
  3.2 3.1 %copy-start.1 = (bf16[9,80,80]{2,1,0:T(8,128)(2,1)S(1)}, bf16[9,80,80]{2,1,0:T(8,128)(2,1)}, u32[]{:S(2)}) copy-start(bf16[9,80,80]{2,1,0:T(8,128)(2,1)} %second_taps.3) | copy-start | bytes 345604
  4.6 13.2 %collective-permute-start = (bf16[2592,128]{1,0:T(8,128)(2,1)S(1)}, bf16[2592,128]{1,0:T(8,128)(2,1)S(1)}, u32[]{:S(2)}, u32[]{:S(2)}) collective-permute-start(bf16[2592,128]{1,0:T(8,128)(2,1)S(1)} %get-tuple-element.32), channel_id=1, source_target_pairs={{0,8},{8,16},{16,24},{24,32},{32,40},{40,48},{48,56},{56,64},{64,7... | collective-permute-start | bytes 1990664 | tf_op jit(solution)/shard_map/ppermute | solution.py:558
  4.6 27.0 %collective-permute-start.1 = (bf16[2592,128]{1,0:T(8,128)(2,1)}, bf16[2592,128]{1,0:T(8,128)(2,1)S(1)}, u32[]{:S(2)}, u32[]{:S(2)}) collective-permute-start(bf16[2592,128]{1,0:T(8,128)(2,1)} %get-tuple-element.31), channel_id=1, source_target_pairs={{0,120},{8,0},{16,8},{24,16},{32,24},{40,32},{48,40},{56,48},{64,5... | collective-permute-start | bytes 1990664 | tf_op jit(solution)/shard_map/ppermute | solution.py:558
  23.6 8.0 %copy-start.3 = (s32[1,1024]{1,0:T(1,128)S(1)}, s32[1,1024]{1,0:T(1,128)}, u32[]{:S(2)}) copy-start(s32[1,1024]{1,0:T(1,128)} %cells.1) | copy-start | bytes 12292
  23.6 32.7 %all-to-all-start = ((bf16[8,120,8,128]{3,2,1,0:T(8,128)(2,1)}), bf16[8,120,8,128]{3,2,1,0:T(8,128)(2,1)S(1)}, u32[]{:S(2)}, u32[]{:S(2)}) async-start(bf16[8,120,8,128]{3,2,1,0:T(8,128)(2,1)} %bitcast.8), calls=%async_computation | async-start | bytes 3932160 | tf_op jit(solution)/shard_map/all_to_all | solution.py:586
  31.6 0.9 copy-start.2
  45.5 29.4 %copy-start.4 = (f32[1,1024]{1,0:T(1,128)S(1)}, f32[1,1024]{1,0:T(1,128)}, u32[]{:S(2)}) copy-start(f32[1,1024]{1,0:T(1,128)} %observed.1) | copy-start | bytes 12292
  45.5 29.4 %copy-start.5 = (f32[1,1024]{1,0:T(1,128)S(1)}, f32[1,1024]{1,0:T(1,128)}, u32[]{:S(2)}) copy-start(f32[1,1024]{1,0:T(1,128)} %variance.1) | copy-start | bytes 12292
  45.5 3.2 %collective-permute-start.2 = (bf16[8,8,128]{2,1,0:T(8,128)(2,1)S(1)}, bf16[8,8,128]{2,1,0:T(8,128)(2,1)S(1)}, u32[]{:S(2)}, u32[]{:S(2)}) collective-permute-start(bf16[8,8,128]{2,1,0:T(8,128)(2,1)S(1)} %get-tuple-element.30), channel_id=1, source_target_pairs={{0,8},{8,16},{16,24},{24,32},{32,40},{40,48},{48,56},{56,64},{64,7... | collective-permute-start | bytes 49160 | tf_op jit(solution)/shard_map/ppermute | solution.py:558
  45.6 3.5 %collective-permute-start.3 = (bf16[8,8,128]{2,1,0:T(8,128)(2,1)S(1)}, bf16[8,8,128]{2,1,0:T(8,128)(2,1)S(1)}, u32[]{:S(2)}, u32[]{:S(2)}) collective-permute-start(bf16[8,8,128]{2,1,0:T(8,128)(2,1)S(1)} %get-tuple-element.29), channel_id=1, source_target_pairs={{0,120},{8,0},{16,8},{24,16},{32,24},{40,32},{48,40},{56,48},{64,5... | collective-permute-start | bytes 49160 | tf_op jit(solution)/shard_map/ppermute | solution.py:558
  56.3 18.6 %all-to-all-start.1 = ((bf16[8,48,8,128]{3,2,1,0:T(8,128)(2,1)}), bf16[8,48,8,128]{3,2,1,0:T(8,128)(2,1)S(1)}, u32[]{:S(2)}, u32[]{:S(2)}) async-start(bf16[8,48,8,128]{3,2,1,0:T(8,128)(2,1)} %pad_maximum_fusion.2), calls=%async_computation.1 | async-start | bytes 1572864 | tf_op jit(solution)/shard_map/all_to_all | solution.py:602

commit v6 on v5

--- a/solution.py
+++ b/solution.py
@@ -11,7 +11,7 @@
 STEP_SIZE = 0.5
 HALO = 4
 CH = 80
-PAIR_A = 4
+PAIR_A = 8
 LAG = 3
 
 
@@ -43,6 +43,7 @@
 def build_taps(taps, matrix):
     for b in range(3):
         row = jnp.concatenate([taps[3 * a + b].astype(jnp.float32) for a in range(3)], axis=1)
+        row = jnp.concatenate([row, jnp.zeros((CH, 256 - 3 * CH), jnp.float32)], axis=1)
         matrix[pl.ds(CH * b, CH), :] = row.astype(jnp.bfloat16)
 
 
@@ -51,23 +52,58 @@
         step()
 
 
+SAVED = 0
+OWN = 12 * CH
+TAPS = 20 * CH
+WIDE16 = 32768
+WIDE32 = 16384
+
+
+def vmem():
+    return pl.BlockSpec(memory_space=pltpu.VMEM)
+
+
+def anywhere():
+    return pl.BlockSpec(memory_space=pl.ANY)
+
+
+def begin(copies, sems, first=0):
+    copies = [
+        pltpu.make_async_copy(source, target, sems.at[first + i])
+        for i, (source, target) in enumerate(copies)
+    ]
+    for copy in copies:
+        copy.start()
+    return copies
+
+
+def finish(copies):
+    for copy in copies:
+        copy.wait()
+
+
+def taps_moves(taps, wide):
+    moves = []
+    for t in range(2):
+        for half in range(2):
+            here = taps.at[t, :, pl.ds(128 * half, 128)]
+            moves.append((here, wide.at[2 * t + half, pl.ds(TAPS, 3 * CH)]))
+    return moves
+
+
 def inner_kernel(
-    own, first_taps, second_taps, out, left_halves, left_rates, right_halves, right_rates, taps_out,
-    taps, h, s, g, rate, fields, cells16, sems,
+    own, first_taps, second_taps, out, wide16, wide32, taps, h, s, g, rate, fields, cells16, sems
 ):
     members = own.shape[0]
     build_taps(first_taps, taps.at[0])
     build_taps(second_taps, taps.at[1])
-    a = taps[0]
-    b = taps[1]
-    copies = [
-        pltpu.make_async_copy(taps, taps_out, sems.at[0]),
-        pltpu.make_async_copy(
-            own.at[:, pl.ds(12 * CH, 4 * CH)], right_halves.at[:, pl.ds(6 * CH, 4 * CH)], sems.at[1]
-        ),
+    a = taps[0, :, : 3 * CH]
+    b = taps[1, :, : 3 * CH]
+    early = [
+        (own.at[:, pl.ds(12 * CH * side, 4 * CH)], wide16.at[:, pl.ds(OWN + 4 * CH * side, 4 * CH)])
+        for side in range(2)
     ]
-    for copy in copies:
-        copy.start()
+    early = begin(early + taps_moves(taps, wide16), sems)
 
     def group(n, carry):
         jobs = []
@@ -104,43 +140,22 @@
         return carry
 
     lax.fori_loop(0, members // PAIR_A, group, 0)
-    for k, (ref, at) in enumerate(((h, 12), (s, 10), (g, 8))):
-        target = pl.ds(2 * CH * k, 2 * CH)
-        copies.append(
-            pltpu.make_async_copy(ref.at[:, pl.ds(0, 2 * CH)], left_halves.at[:, target], sems.at[2 + k])
-        )
-        copies.append(
-            pltpu.make_async_copy(
-                ref.at[:, pl.ds(CH * at, 2 * CH)], right_halves.at[:, target], sems.at[5 + k]
-            )
-        )
-    pair = pl.ds(0, 2 * CH)
-    copies.append(pltpu.make_async_copy(rate.at[:, pair], left_rates, sems.at[8]))
-    copies.append(
-        pltpu.make_async_copy(
-            rate.at[:, pl.ds(CH * 10, 2 * CH)], right_rates.at[:, pair], sems.at[9]
-        )
-    )
-    for copy in copies[2:]:
-        copy.start()
-    cells16[...] = fields[...].astype(jnp.bfloat16).reshape(cells16.shape)
-    last = pltpu.make_async_copy(cells16, out.at[pl.ds(0, 8)], sems.at[10])
-    last.start()
-    for copy in copies:
-        copy.wait()
-    last.wait()
-
-
-def vmem():
-    return pl.BlockSpec(memory_space=pltpu.VMEM)
-
-
-def anywhere():
-    return pl.BlockSpec(memory_space=pl.ANY)
-
-
-WIDE16 = 32768
-WIDE32 = 16384
+    late = []
+    for side in range(2):
+        for k, (ref, right) in enumerate(((h, 12), (s, 10), (g, 8))):
+            target = wide16.at[:, pl.ds(SAVED + 6 * CH * side + 2 * CH * k, 2 * CH)]
+            late.append((ref.at[:, pl.ds(CH * right * side, 2 * CH)], target))
+        target = wide32.at[:, pl.ds(2 * CH * side, 2 * CH)]
+        late.append((rate.at[:, pl.ds(10 * CH * side, 2 * CH)], target))
+    late = begin(late, sems, len(early))
+    last = []
+    for x in range(8):
+        column = fields[pl.ds(8 * CH * x, 8 * CH), :].astype(jnp.bfloat16)
+        cells16[x] = column.reshape(CH, 8, 128)
+        if x % 2:
+            pair = pl.ds(x - 1, 2)
+            last += begin([(cells16.at[pair], out.at[pair])], sems, len(early) + len(late) + x // 2)
+    finish(early + late + last)
 
 
 def inner_forecast(own, first_taps, second_taps):
@@ -149,24 +164,21 @@
     return pl.pallas_call(
         inner_kernel,
         in_specs=[vmem()] * 3,
-        out_specs=[anywhere()] * 6,
+        out_specs=[anywhere()] * 3,
         out_shape=[
-            jax.ShapeDtypeStruct((12, CH, 8, 128), bf16),
-            jax.ShapeDtypeStruct((members, 6 * CH, 128), bf16),
-            jax.ShapeDtypeStruct((members, 2 * CH, 128), f32),
+            jax.ShapeDtypeStruct((8, CH, 8, 128), bf16),
             jax.ShapeDtypeStruct((members, WIDE16, 128), bf16),
             jax.ShapeDtypeStruct((members, WIDE32, 128), f32),
-            jax.ShapeDtypeStruct((2, 3 * CH, 3 * CH), bf16),
         ],
         scratch_shapes=[
-            pltpu.VMEM((2, 3 * CH, 3 * CH), bf16),
+            pltpu.VMEM((2, 3 * CH, 256), bf16),
             pltpu.VMEM((members, 14 * CH, 128), bf16),
             pltpu.VMEM((members, 12 * CH, 128), bf16),
             pltpu.VMEM((members, 10 * CH, 128), bf16),
             pltpu.VMEM((members, 12 * CH, 128), f32),
             pltpu.VMEM((64 * CH, 128), f32),
             pltpu.VMEM((8, CH, 8, 128), bf16),
-            pltpu.SemaphoreType.DMA((11,)),
+            pltpu.SemaphoreType.DMA((18,)),
         ],
         compiler_params=vmem_params(),
         cost_estimate=pl.CostEstimate(
@@ -175,30 +187,14 @@
     )(own, first_taps, second_taps)
 
 
-def edge_loads(side, halves, rates, own, halo, v, h, s, g, rated, sems):
-    members = v.shape[0]
-    saved = 4 if side == 0 else 0
-    copies = []
-    for m in range(members):
-        source = halo.at[pl.ds(CH * HALO * m, CH * HALO)]
-        copies.append((source, v.at[m, pl.ds(0 if side == 0 else 4 * CH, 4 * CH)]))
-    copies.append((own, v.at[:, pl.ds(4 * CH if side == 0 else 0, 4 * CH)]))
-    for k, ref in enumerate((h, s, g)):
-        copies.append((halves.at[:, pl.ds(2 * CH * k, 2 * CH)], ref.at[:, pl.ds(saved * CH, 2 * CH)]))
-    copies.append((rates, rated))
-    return [
-        pltpu.make_async_copy(source, target, sems.at[i])
-        for i, (source, target) in enumerate(copies)
-    ]
-
-
-def edge_columns(side, taps, v, h, s, g, rate, rated, fields, start):
-    a = taps[0]
-    b = taps[1]
+def edge_jobs(side, taps, v, h, s, g, rate, rated, fields, start):
+    a = taps[0, :, : 3 * CH]
+    b = taps[1, :, : 3 * CH]
     jobs = []
     made = 0 if side == 0 else 2
-    for m in range(v.shape[0]):
-        vm, hm, sm, gm, rm, rdm = v.at[m], h.at[m], s.at[m], g.at[m], rate.at[m], rated.at[m]
+    for m in range(v.shape[1]):
+        vm, hm, sm, gm = v.at[side, m], h.at[side, m], s.at[side, m], g.at[side, m]
+        rm, rdm = rate.at[side, m], rated.at[m, pl.ds(2 * CH * side, 2 * CH)]
 
         def hidden(ref):
             def put(k, value):
@@ -228,53 +224,8 @@
         for level, (source, at, matrix, emit) in enumerate(stages):
             for k in (0, 2):
                 step = functools.partial(conv_pair, source, at + k, matrix, emit, k)
-                jobs.append(((level, m, k), step))
-    run_interleaved(jobs)
-
-
-def edge_scratch(members):
-    bf16, f32 = jnp.bfloat16, jnp.float32
-    return [
-        pltpu.VMEM((members, 8 * CH, 128), bf16),
-        pltpu.VMEM((members, 6 * CH, 128), bf16),
-        pltpu.VMEM((members, 6 * CH, 128), bf16),
-        pltpu.VMEM((members, 6 * CH, 128), bf16),
-        pltpu.VMEM((members, 2 * CH, 128), f32),
-        pltpu.VMEM((members, 2 * CH, 128), f32),
-        pltpu.VMEM((4, CH, 8, 128), bf16),
-        pltpu.SemaphoreType.DMA((members + 6,)),
-    ]
-
-
-def left_kernel(
-    chunk, taps, halo, own, halves, rates, out, v, h, s, g, rate, rated, cells16, sems, fields
-):
-    copies = edge_loads(0, halves, rates, own.at[:, pl.ds(0, 4 * CH)], halo, v, h, s, g, rated, sems)
-    for copy in copies:
-        copy.start()
-    for copy in copies:
-        copy.wait()
-    edge_columns(0, taps, v, h, s, g, rate, rated, fields, 0)
-    cells16[...] = fields[...].astype(jnp.bfloat16).reshape(cells16.shape)
-    last = pltpu.make_async_copy(cells16, out.at[pl.ds(8, 4)], sems.at[len(copies)])
-    last.start()
-    last.wait()
-
-
-def left_forecast(chunk, taps, halo, own, halves, rates):
-    members = own.shape[0]
-    return pl.pallas_call(
-        left_kernel,
-        in_specs=[anywhere(), vmem()] + [anywhere()] * 4,
-        out_specs=anywhere(),
-        out_shape=jax.ShapeDtypeStruct((12, CH, 8, 128), jnp.bfloat16),
-        scratch_shapes=edge_scratch(members) + [pltpu.VMEM((32 * CH, 128), jnp.float32)],
-        input_output_aliases={0: 0},
-        compiler_params=vmem_params(),
-        cost_estimate=pl.CostEstimate(
-            flops=5_000_000_000, bytes_accessed=4_000_000, transcendentals=1_000_000
-        ),
-    )(chunk, taps, halo, own, halves, rates)
+                jobs.append(((level, m, side, k), step))
+    return jobs
 
 
 def place_of(channel, lon, lat, part):
@@ -285,33 +236,42 @@
     return jnp.where(here, (column * CH + channel) * 8, 0), (slot - lat) & 127
 
 
-def right_kernel(
-    chunk, cells, first_taps, second_taps, left, right, halves, rates, out, picked,
-    v, h, s, g, rate, rated, cells16, sems, taps, fields, chunk16, lists, drawn, places, rows, turns, list_sems, place_sems,
+def edge_kernel(
+    inner, cells, left, right, wide16, wide32, out, picked,
+    taps, v, h, s, g, rate, rated, fields, inner16, lists, own_list, places, rows, turns,
+    sems, list_sems, place_sems,
 ):
-    members = v.shape[0]
-    digits = CH * HALO * members
-    copies = edge_loads(
-        1,
-        halves,
-        rates.at[:, pl.ds(0, 2 * CH)],
-        halves.at[:, pl.ds(6 * CH, 4 * CH)],
-        right, v, h, s, g, rated, sems,
+    members = v.shape[1]
+    halo = CH * HALO
+    digits = halo * members
+    early = begin([(there, here) for here, there in taps_moves(taps, wide16)], sems)
+    list_copies = begin(
+        [(left.at[pl.ds(digits, 32)], lists.at[0]), (right.at[pl.ds(digits, 32)], lists.at[1]), (cells, own_list)],
+        list_sems,
     )
-    list_copies = [
-        pltpu.make_async_copy(source.at[pl.ds(digits, 32)], lists.at[i], list_sems.at[i])
-        for i, source in enumerate((left, right))
-    ]
-    chunk_copy = pltpu.make_async_copy(chunk, chunk16, list_sems.at[2])
-    for copy in list_copies + copies + [chunk_copy]:
-        copy.start()
-    build_taps(first_taps, taps.at[0])
-    build_taps(second_taps, taps.at[1])
-    for copy in list_copies:
-        copy.wait()
+    columns = []
+    used = len(early)
+    for m in range(members):
+        moves = []
+        for side, source in enumerate((left, right)):
+            edge = v.at[side, m]
+            moves.append((source.at[pl.ds(halo * m, halo)], edge.at[pl.ds(4 * CH * side, 4 * CH)]))
+            source = wide16.at[m, pl.ds(OWN + 4 * CH * side, 4 * CH)]
+            moves.append((source, edge.at[pl.ds(4 * CH * (1 - side), 4 * CH)]))
+        columns.append(begin(moves, sems, used))
+        used += len(moves)
+    moves = []
+    for k, ref in enumerate((h, s, g)):
+        for side in range(2):
+            source = wide16.at[:, pl.ds(SAVED + 6 * CH * side + 2 * CH * k, 2 * CH)]
+            moves.append((source, ref.at[side, :, pl.ds(4 * CH * (1 - side), 2 * CH)]))
+    moves.append((wide32.at[:, pl.ds(0, 4 * CH)], rated))
+    later = begin(moves, sems, used)
+    inner_copy = begin([(inner, inner16)], list_sems, 3)
+    finish(list_copies)
     for k in range(3):
         if k == 1:
-            cell = cells[...]
+            cell = own_list[...]
             strip = cell >> 7
             channel = (strip * 43691) >> 21
             parts = (channel, strip - 48 * channel, cell & 127)
@@ -321,73 +281,77 @@
         row, turn = place_of(*parts, 2 - k)
         places[0, pl.ds(8 * k, 8), :] = row
         places[1, pl.ds(8 * k, 8), :] = turn
-    place_copies = [
-        pltpu.make_async_copy(places.at[0], rows, place_sems.at[0]),
-        pltpu.make_async_copy(places.at[1], turns, place_sems.at[1]),
-    ]
-    for copy in place_copies:
-        copy.start()
-    for copy in copies:
-        copy.wait()
-    edge_columns(1, taps, v, h, s, g, rate, rated, fields, 96 * CH)
-    cells16[...] = fields[pl.ds(96 * CH, 32 * CH), :].astype(jnp.bfloat16).reshape(cells16.shape)
-    out_copy = pltpu.make_async_copy(cells16, out, sems.at[len(copies)])
-    out_copy.start()
-    chunk_copy.wait()
-    fields[pl.ds(0, 96 * CH), :] = chunk16[...].astype(jnp.float32).reshape(96 * CH, 128)
-    for copy in place_copies:
-        copy.wait()
+    place_copies = begin([(places.at[0], rows), (places.at[1], turns)], place_sems)
+    finish(early)
+    jobs = []
+    for side in range(2):
+        jobs += edge_jobs(side, taps, v, h, s, g, rate, rated, fields, (64 + 32 * side) * CH)
+
+    for n in range(2):
+        for m in range(4 * n, 4 * n + 4):
+            jobs.append(((0, 4 * n, -1, 0), functools.partial(finish, columns[m])))
+    jobs.append(((1, -1, 0, 0), functools.partial(finish, later + inner_copy)))
+    run_interleaved(jobs)
+    fields[pl.ds(0, 64 * CH), :] = inner16[...].astype(jnp.float32).reshape(64 * CH, 128)
+    out[...] = fields[pl.ds(64 * CH, 64 * CH), :].astype(jnp.bfloat16).reshape(out.shape)
+    finish(place_copies)
     lane = lax.broadcasted_iota(jnp.int32, (8, 128), 1)
 
     def block(k, carry):
-        acc = jnp.zeros((8, 128), jnp.float32)
+        found = [jnp.zeros((8, 128), jnp.float32)] * 3
         for j in range(128):
-            cell = fields[pl.ds(pl.multiple_of(rows[k, j], 8), 8), :]
-            acc = jnp.where(lane == j, pltpu.roll(cell, turns[k, j], axis=1), acc)
-        drawn[k] = acc.astype(jnp.bfloat16)
+            for q in range(3):
+                cell = fields[pl.ds(pl.multiple_of(rows[8 * q + k, j], 8), 8), :]
+                cell = pltpu.roll(cell, turns[8 * q + k, j], axis=1)
+                found[q] = jnp.where(lane == j, cell, found[q])
+        for q in range(3):
+            picked[8 * q + k] = found[q].astype(jnp.bfloat16)
         return carry
 
-    lax.fori_loop(0, drawn.shape[0], block, 0)
-    drawn_copy = pltpu.make_async_copy(drawn, picked, place_sems.at[2])
-    drawn_copy.start()
-    drawn_copy.wait()
-    out_copy.wait()
-
-
-def right_forecast(chunk, cells, first_taps, second_taps, left, right, halves, rates):
+    lax.fori_loop(0, 8, block, 0)
+
+
+def edge_forecast(inner, cells, left, right, wide16, wide32):
     bf16, f32 = jnp.bfloat16, jnp.float32
-    members = halves.shape[0]
+    members = wide16.shape[0]
     return pl.pallas_call(
-        right_kernel,
-        in_specs=[anywhere()] + [vmem()] * 3 + [anywhere()] * 4,
-        out_specs=[anywhere()] * 2,
+        edge_kernel,
+        in_specs=[anywhere()] * 6,
+        out_specs=[vmem()] * 2,
         out_shape=[
-            jax.ShapeDtypeStruct((4, CH, 8, 128), bf16),
+            jax.ShapeDtypeStruct((8, CH, 8, 128), bf16),
             jax.ShapeDtypeStruct((24, 8, 128), bf16),
         ],
-        scratch_shapes=edge_scratch(members) + [
-            pltpu.VMEM((2, 3 * CH, 3 * CH), bf16),
+        scratch_shapes=[
+            pltpu.VMEM((2, 3 * CH, 256), bf16),
+            pltpu.VMEM((2, members, 8 * CH, 128), bf16),
+            pltpu.VMEM((2, members, 6 * CH, 128), bf16),
+            pltpu.VMEM((2, members, 6 * CH, 128), bf16),
+            pltpu.VMEM((2, members, 6 * CH, 128), bf16),
+            pltpu.VMEM((2, members, 2 * CH, 128), f32),
+            pltpu.VMEM((members, 4 * CH, 128), f32),
             pltpu.VMEM((128 * CH, 128), f32),
-            pltpu.VMEM((12, CH, 8, 128), bf16),
+            pltpu.VMEM((8, CH, 8, 128), bf16),
             pltpu.VMEM((2, 32, 128), bf16),
-            pltpu.VMEM((24, 8, 128), bf16),
+            pltpu.VMEM((8, 128), jnp.int32),
             pltpu.VMEM((2, 24, 128), jnp.int32),
             pltpu.SMEM((24, 128), jnp.int32),
             pltpu.SMEM((24, 128), jnp.int32),
-            pltpu.SemaphoreType.DMA((3,)),
-            pltpu.SemaphoreType.DMA((3,)),
+            pltpu.SemaphoreType.DMA((4 * members + 11,)),
+            pltpu.SemaphoreType.DMA((4,)),
+            pltpu.SemaphoreType.DMA((2,)),
         ],
         compiler_params=vmem_params(),
         cost_estimate=pl.CostEstimate(
-            flops=5_000_000_000, bytes_accessed=8_000_000, transcendentals=1_000_000
+            flops=9_000_000_000, bytes_accessed=8_000_000, transcendentals=2_000_000
         ),
-    )(chunk, cells, first_taps, second_taps, left, right, halves, rates)
+    )(inner, cells, left, right, wide16, wide32)
 
 
 def transform_kernel(parts, cells, numbers, observed, variance, out, values, stack, sem):
     f32 = jnp.float32
     exact = lax.Precision.HIGHEST
-    load = pltpu.make_async_copy(parts.at[:, pl.ds(40, 8)], values, sem)
+    load = pltpu.make_async_copy(parts.at[:, pl.ds(CH, 8)], values, sem)
     load.start()
     load.wait()
     for group in range(8):
@@ -478,15 +442,17 @@
 def mix_kernel(first, second, weights, out):
     w = weights[...]
 
-    def block(n, carry):
-        for k in range(5):
-            row = (5 * n + k) * 8
-            mix_rows(first, row, w, out, row)
-        return carry
-
-    lax.fori_loop(0, 3, block, 0)
-    for k in range(5):
-        mix_rows(second, 8 * k, w, out, 120 + 8 * k)
+    def half(parts, start):
+        def block(n, carry):
+            for k in range(5):
+                row = (5 * n + k) * 8
+                mix_rows(parts, row, w, out, start + row)
+            return carry
+
+        lax.fori_loop(0, 2, block, 0)
+
+    half(first, 0)
+    half(second, CH)
 
 
 def mix(first, second, weights):
@@ -508,17 +474,15 @@
 def order_kernel(cells, out, scratch, sems):
     to = lax.broadcasted_iota(jnp.int32, (128, 128), 0)
     at = lax.broadcasted_iota(jnp.int32, (128, 128), 1)
-    slot = at >> 3
-    column = jnp.where(slot < 8, slot + 4, jnp.where(slot < 12, slot - 8, slot))
+    source = at >> 4
+    side = (at >> 3) & 1
+    column = jnp.where(side == 0, source + 4, jnp.where(source < 4, source, source + 8))
     move = jnp.where(to == (at & 7) * 16 + column, 1.0, 0.0).astype(jnp.bfloat16)
 
-    def cell(i, c):
-        if i < 12:
-            return cells[(CH * i + c) // 120, (CH * i + c) % 120]
-        return cells[(CH * (i - 12) + c) // 40, 120 + (CH * (i - 12) + c) % 40]
-
     def rows(c):
-        return jnp.stack([cell(i, c) for i in range(16)]).reshape(128, 128)
+        return jnp.concatenate(
+            [cells[:, c][:, None], cells[:, CH + c][:, None]], axis=1
+        ).reshape(128, 128)
 
     depth = CH // CHUNKS
     copies = []
@@ -579,16 +543,9 @@
     left = ring(jnp.concatenate([tail, digits]), 1)
     right = ring(jnp.concatenate([head, digits]), -1)
 
-    chunk, left_halves, left_rates, right_halves, right_rates, taps = inner_forecast(
-        own, initial_kernel_taps, latter_kernel_taps
-    )
-    chunk = left_forecast(chunk, taps, left, own, left_halves, left_rates)
-    first_parts = lax.all_to_all(
-        chunk.reshape(8, 120, 8, 128), "mem", split_axis=0, concat_axis=0, tiled=True
-    )
-    edge, picked = right_forecast(
-        chunk, cells, initial_kernel_taps, latter_kernel_taps, left, right, right_halves, right_rates
-    )
+    inner, wide16, wide32 = inner_forecast(own, initial_kernel_taps, latter_kernel_taps)
+    first_parts = lax.all_to_all(inner, "mem", split_axis=0, concat_axis=0, tiled=True)
+    edge, picked = edge_forecast(inner, cells, left, right, wide16, wide32)
 
     picked = picked.reshape(3, 8, 8, 128)
     from_left = ring(picked[2], 1)
@@ -596,7 +553,7 @@
     part = (cells // 128 % 48 // 16).reshape(8, 1, 128)
     here = jnp.where(part == 0, from_left, jnp.where(part == 1, picked[1], from_right))
     message = jnp.concatenate(
-        [edge.reshape(8, 40, 8, 128), jnp.broadcast_to(here[None], (8, 8, 8, 128))], axis=1
+        [edge, jnp.broadcast_to(here[None], (8, 8, 8, 128))], axis=1
     )
     message, first_parts = lax.optimization_barrier((message, first_parts))
     second_parts = lax.all_to_all(message, "mem", split_axis=0, concat_axis=0, tiled=True)

time: 121 us -> 118 us (0.975)
  Pallas kernels: 37 us -> 31.2 us
  blocking collectives: 38.8 us -> 42.2 us
  starting transfers between devices: 16.3 us -> 19.5 us
  waiting for transfers between devices: 20.5 us -> 17.7 us
    all_to_all x1, waiting for transfers between devices: 6.25 us -> 0.01 us  [per_device(): lax.all_to_all(inner, 'mem', split_axis=0, concat_axis=0, tiled=True)]
    pallas_call x2 -> x1, Pallas kernels: 18.7 us -> 14 us  [edge_forecast(): pl.pallas_call(edge_kernel, in_specs=[anywhere()] * 6, out_specs=[vmem()]...]
    all_to_all x1, waiting for transfers between devices: 12.5 us -> 15.9 us  [per_device(): lax.all_to_all(message, 'mem', split_axis=0, concat_axis=0, tiled=True)]
    all_to_all x1, blocking collectives: 38.8 us -> 42.2 us  [per_device(): back = lax.all_to_all(mixed, 'mem', split_axis=0, concat_axis=0, tiled=True)]
    all_to_all x1, starting transfers between devices: 4.76 us -> 7.95 us  [per_device(): lax.all_to_all(message, 'mem', split_axis=0, concat_axis=0, tiled=True)]
  transfers between devices with their start and end apart: 6 -> 6, of which waited for: 4 -> 3; matrix products, arithmetic and copies ran while one was open for 1% -> 1% of each run, Pallas kernels for 25% -> 21%
where the time goes in v6:
time: 118 us; the launch traced here: 117 us
  blocking collectives  42.2 us (36%)
  Pallas kernels  31.2 us (26%)
  starting transfers between devices  19.5 us (17%)
  waiting for transfers between devices  17.7 us (15%)
  local copies, waits for them, and re-layouts  2.64 us (2%)
  other arithmetic  2.63 us (2%)
  between operations  1.59 us (1%)
    all_to_all x1, blocking collectives, per_device(): back = lax.all_to_all(mixed, 'mem', split_axis=0, concat_axis=0, tiled=True)  42.2 us
    all_to_all x1, waiting for transfers between devices, per_device(): lax.all_to_all(message, 'mem', split_axis=0, concat_axis=0, tiled=True)  15.9 us
    pallas_call x1, Pallas kernels, edge_forecast(): pl.pallas_call(edge_kernel, in_specs=[anywhere()] * 6, out_specs=[vmem()]...  14 us
    pallas_call x1, Pallas kernels, inner_forecast(): pl.pallas_call(inner_kernel, in_specs=[vmem()] * 3, out_specs=[anywhere()...  10.3 us
    all_to_all x1, starting transfers between devices, per_device(): lax.all_to_all(inner, 'mem', split_axis=0, concat_axis=0, tiled=True)  7.96 us
    all_to_all x1, starting transfers between devices, per_device(): lax.all_to_all(message, 'mem', split_axis=0, concat_axis=0, tiled=True)  7.95 us
    ppermute x4, starting transfers between devices, ring(): lax.ppermute(cells, 'space', [(i, (i + step) % count) for i in range(coun...  3.55 us
    pallas_call x1, Pallas kernels, transform_of(): pl.pallas_call(transform_kernel, in_specs=[anywhere(), vmem(), smem, vmem...  3.06 us
  transfers between devices with their start and end apart: 6, of which 3 were waited for; matrix products, arithmetic and copies ran while one was open for 1% of the time, Pallas kernels for 21%

profile of v6, /device:TPU:6, one launch (start us, length us, event | category | flops | bytes accessed | tf_op | source)
XLA Modules:
  0.0 117.4 jit_solution(14706820159703039164)
XLA Ops:
  0.0 2.4 %copy.9 = bf16[8,16,80,128]{3,2,1,0:T(8,128)(2,1)S(1)} copy(bf16[8,16,80,128]{3,1,2,0:T(8,128)(2,1)} %bitcast.13) | data formatting | bytes 5242880 | tf_op jit(solution)/shard_map/transpose | solution.py:537
  2.5 0.1 fusion.13
  2.6 0.0 copy-start.3
  2.6 0.0 copy-start.4
  2.6 0.1 pad.9.clone
  2.7 1.2 %fusion.1 = (bf16[2592,128]{1,0:T(8,128)(2,1)S(1)}, bf16[2592,128]{1,0:T(8,128)(2,1)}) fusion(bf16[24,128]{1,0:T(8,128)(2,1)S(1)} %maximum_bitcast_fusion, bf16[2560,128]{1,0:T(8,128)(2,1)S(1)} %bitcast.14, bf16[2592]{0:T(1024)(128)(2,1)S(1)} %pad.9.clone, bf16[2560,128]{1,0:T(8,128)(2,1)S(1)} %bitcast.15), kind=kLoop, calls=%fused_computation.4 | loop fusion | flops 3317760 | bytes 2649152 | tf_op jit(solution)/shard_map/concatenate | solution.py:544
  3.9 0.0 collective-permute-start
  3.9 1.7 %collective-permute-start.1 = (bf16[2592,128]{1,0:T(8,128)(2,1)S(1)}, bf16[2592,128]{1,0:T(8,128)(2,1)S(1)}, u32[]{:S(2)}, u32[]{:S(2)}) collective-permute-start(bf16[2592,128]{1,0:T(8,128)(2,1)S(1)} %get-tuple-element.25), channel_id=1, source_target_pairs={{0,120},{8,0},{16,8},{24,16},{32,24},{40,32},{48,40},{56,48},{64,5... | collective-permute-start | bytes 1990664 | tf_op jit(solution)/shard_map/ppermute | solution.py:522
  5.7 10.3 %shard_map.82 = (bf16[8,80,8,128]{3,2,1,0:T(8,128)(2,1)}, bf16[8,32768,128]{2,1,0:T(8,128)(2,1)}, f32[8,16384,128]{2,1,0:T(8,128)}) custom-call(bf16[8,1280,128]{2,1,0:T(8,128)(2,1)S(1)} %bitcast.9, bf16[9,80,80]{2,1,0:T(8,128)(2,1)S(1)} %copy-done.3, bf16[9,80,80]{2,1,0:T(8,128)(2,1)S(1)} %copy-done.4), custom_call_target="tpu_custom_call" | custom-call | flops 12000000000 | bytes 8000000 | tf_op jit(solution)/shard_map/pallas_call | solution.py:164
  16.0 8.0 %all-to-all-start = ((bf16[8,80,8,128]{3,2,1,0:T(8,128)(2,1)}), bf16[8,80,8,128]{3,2,1,0:T(8,128)(2,1)S(1)}, u32[]{:S(2)}, u32[]{:S(2)}) async-start(bf16[8,80,8,128]{3,2,1,0:T(8,128)(2,1)} %get-tuple-element.12.inner), calls=%async_computation | async-start | bytes 2621440 | tf_op jit(solution)/shard_map/all_to_all | solution.py:547
  24.0 14.0 %shard_map.83 = (bf16[8,80,8,128]{3,2,1,0:T(8,128)(2,1)S(1)}, bf16[24,8,128]{2,1,0:T(8,128)(2,1)S(1)}) custom-call(bf16[8,80,8,128]{3,2,1,0:T(8,128)(2,1)} %get-tuple-element.12.inner, s32[8,128]{1,0:T(8,128)S(1)} %bitcast.12, bf16[2592,128]{1,0:T(8,128)(2,1)S(1)} %collective-permute-done.left, bf16[2592,128]{1,0:T(8,128)(2,1)S(1)} %collective-permute-done.1.right, ...), custom_call_target="tpu_custom_call" | custom-call | flops 8999999488 | bytes 8000000 | tf_op jit(solution)/shard_map/pallas_call | solution.py:317
  38.0 0.1 collective-permute-start.2
  38.1 1.7 %collective-permute-start.3 = (bf16[8,8,128]{2,1,0:T(8,128)(2,1)S(1)}, bf16[8,8,128]{2,1,0:T(8,128)(2,1)S(1)}, u32[]{:S(2)}, u32[]{:S(2)}) collective-permute-start(bf16[8,8,128]{2,1,0:T(8,128)(2,1)S(1)} %get-tuple-element.23), channel_id=1, source_target_pairs={{0,120},{8,0},{16,8},{24,16},{32,24},{40,32},{48,40},{56,48},{64,5... | collective-permute-start | bytes 49160 | tf_op jit(solution)/shard_map/ppermute | solution.py:522
  39.9 1.4 %collective-permute-done.2 = bf16[8,8,128]{2,1,0:T(8,128)(2,1)S(1)} collective-permute-done((bf16[8,8,128]{2,1,0:T(8,128)(2,1)S(1)}, bf16[8,8,128]{2,1,0:T(8,128)(2,1)S(1)}, u32[]{:S(2)}, u32[]{:S(2)}) %collective-permute-start.2) | collective-permute-done | bytes 16416 | tf_op jit(solution)/shard_map/ppermute | solution.py:522
  41.3 0.3 collective-permute-done.3
  41.7 1.2 %pad_maximum_fusion = bf16[8,88,8,128]{3,2,1,0:T(8,128)(2,1)} fusion(bf16[8,8,8,128]{3,2,1,0:T(8,128)(2,1)S(1)} %broadcast_in_dim.25, bf16[8,80,8,128]{3,2,1,0:T(8,128)(2,1)S(1)} %get-tuple-element.15), kind=kLoop, calls=%fused_computation | loop fusion | flops 720896 | bytes 2883584 | tf_op jit(solution)/shard_map/concatenate | solution.py:555
  42.9 0.0 all-to-all-done.first
  42.9 7.9 %all-to-all-start.1 = ((bf16[8,88,8,128]{3,2,1,0:T(8,128)(2,1)}), bf16[8,88,8,128]{3,2,1,0:T(8,128)(2,1)S(1)}, u32[]{:S(2)}, u32[]{:S(2)}) async-start(bf16[8,88,8,128]{3,2,1,0:T(8,128)(2,1)} %pad_maximum_fusion), calls=%async_computation.1 | async-start | bytes 2883584 | tf_op jit(solution)/shard_map/all_to_all | solution.py:559
  52.1 0.1 pad_add_fusion.numbers
  52.2 15.9 %all-to-all-done.1.parts.second = bf16[8,88,8,128]{3,2,1,0:T(8,128)(2,1)S(1)} async-done(((bf16[8,88,8,128]{3,2,1,0:T(8,128)(2,1)}), bf16[8,88,8,128]{3,2,1,0:T(8,128)(2,1)S(1)}, u32[]{:S(2)}, u32[]{:S(2)}) %all-to-all-start.1) | async-done | bytes 1441824 | tf_op jit(solution)/shard_map/all_to_all | solution.py:559
  68.2 3.1 %shard_map.84.weights = bf16[256,256]{1,0:T(8,128)(2,1)S(1)} custom-call(bf16[8,88,8,128]{3,2,1,0:T(8,128)(2,1)S(1)} %all-to-all-done.1.parts.second, s32[1,1024]{1,0:T(1,128)S(1)} %copy-done, s32[2]{0:T(128)S(1)} %pad_add_fusion.numbers, f32[1,1024]{1,0:T(1,128)S(1)} %copy-done.1, f32[1,1024]{1,0:T(1,128)S(1)} %copy-done.2), custom_call_target="tpu_custom_call" | custom-call | flops 100000000 | bytes 500000 | tf_op jit(solution)/shard_map/pallas_call | solution.py:406
  71.2 2.0 %shard_map.85 = bf16[8,160,8,128]{3,2,1,0:T(8,128)(2,1)S(1)} custom-call(bf16[8,80,8,128]{3,2,1,0:T(8,128)(2,1)S(1)} %all-to-all-done.first, bf16[8,88,8,128]{3,2,1,0:T(8,128)(2,1)S(1)} %all-to-all-done.1.parts.second, bf16[256,256]{1,0:T(8,128)(2,1)S(1)} %shard_map.84.weights), custom_call_target="tpu_custom_call" | custom-call | flops 700000000 | bytes 5300000 | tf_op jit(solution)/shard_map/pallas_call | solution.py:459
  73.2 42.2 %all_to_all.15.cells = bf16[8,160,8,128]{3,2,1,0:T(8,128)(2,1)S(1)} all-to-all(bf16[8,160,8,128]{3,2,1,0:T(8,128)(2,1)S(1)} %shard_map.85), channel_id=1, replica_groups=mesh['space'=16,'mem'=8] {'mem'}, dimensions={0} | all-to-all | bytes 5242880 | tf_op jit(solution)/shard_map/all_to_all | solution.py:565
  115.4 1.8 %shard_map.86 = bf16[8,80,16,128]{3,2,1,0:T(8,128)(2,1)} custom-call(bf16[8,160,8,128]{3,2,1,0:T(8,128)(2,1)S(1)} %all_to_all.15.cells), custom_call_target="tpu_custom_call" | custom-call | flops 600000000 | bytes 5300000 | tf_op jit(solution)/shard_map/pallas_call | solution.py:504
  (18 shorter events, 0.1 us)
Async XLA Ops:
  0.0 2.4 %copy-start = (s32[1,1024]{1,0:T(1,128)S(1)}, s32[1,1024]{1,0:T(1,128)}, u32[]{:S(2)}) copy-start(s32[1,1024]{1,0:T(1,128)} %cells.1) | copy-start | bytes 12292
  2.6 3.1 %copy-start.3 = (bf16[9,80,80]{2,1,0:T(8,128)(2,1)S(1)}, bf16[9,80,80]{2,1,0:T(8,128)(2,1)}, u32[]{:S(2)}) copy-start(bf16[9,80,80]{2,1,0:T(8,128)(2,1)} %first_taps.1) | copy-start | bytes 345604
  2.6 3.1 %copy-start.4 = (bf16[9,80,80]{2,1,0:T(8,128)(2,1)S(1)}, bf16[9,80,80]{2,1,0:T(8,128)(2,1)}, u32[]{:S(2)}) copy-start(bf16[9,80,80]{2,1,0:T(8,128)(2,1)} %second_taps.1) | copy-start | bytes 345604
  3.9 20.1 %collective-permute-start = (bf16[2592,128]{1,0:T(8,128)(2,1)}, bf16[2592,128]{1,0:T(8,128)(2,1)S(1)}, u32[]{:S(2)}, u32[]{:S(2)}) collective-permute-start(bf16[2592,128]{1,0:T(8,128)(2,1)} %get-tuple-element.26), channel_id=1, source_target_pairs={{0,8},{8,16},{16,24},{24,32},{32,40},{40,48},{48,56},{56,64},{64,7... | collective-permute-start | bytes 1990664 | tf_op jit(solution)/shard_map/ppermute | solution.py:522
  3.9 20.1 %collective-permute-start.1 = (bf16[2592,128]{1,0:T(8,128)(2,1)S(1)}, bf16[2592,128]{1,0:T(8,128)(2,1)S(1)}, u32[]{:S(2)}, u32[]{:S(2)}) collective-permute-start(bf16[2592,128]{1,0:T(8,128)(2,1)S(1)} %get-tuple-element.25), channel_id=1, source_target_pairs={{0,120},{8,0},{16,8},{24,16},{32,24},{40,32},{48,40},{56,48},{64,5... | collective-permute-start | bytes 1990664 | tf_op jit(solution)/shard_map/ppermute | solution.py:522
  16.0 26.9 %all-to-all-start = ((bf16[8,80,8,128]{3,2,1,0:T(8,128)(2,1)}), bf16[8,80,8,128]{3,2,1,0:T(8,128)(2,1)S(1)}, u32[]{:S(2)}, u32[]{:S(2)}) async-start(bf16[8,80,8,128]{3,2,1,0:T(8,128)(2,1)} %get-tuple-element.12.inner), calls=%async_computation | async-start | bytes 2621440 | tf_op jit(solution)/shard_map/all_to_all | solution.py:547
  38.0 3.2 %collective-permute-start.2 = (bf16[8,8,128]{2,1,0:T(8,128)(2,1)S(1)}, bf16[8,8,128]{2,1,0:T(8,128)(2,1)S(1)}, u32[]{:S(2)}, u32[]{:S(2)}) collective-permute-start(bf16[8,8,128]{2,1,0:T(8,128)(2,1)S(1)} %get-tuple-element.24), channel_id=1, source_target_pairs={{0,8},{8,16},{16,24},{24,32},{32,40},{40,48},{48,56},{56,64},{64,7... | collective-permute-start | bytes 49160 | tf_op jit(solution)/shard_map/ppermute | solution.py:522
  38.1 3.5 %collective-permute-start.3 = (bf16[8,8,128]{2,1,0:T(8,128)(2,1)S(1)}, bf16[8,8,128]{2,1,0:T(8,128)(2,1)S(1)}, u32[]{:S(2)}, u32[]{:S(2)}) collective-permute-start(bf16[8,8,128]{2,1,0:T(8,128)(2,1)S(1)} %get-tuple-element.23), channel_id=1, source_target_pairs={{0,120},{8,0},{16,8},{24,16},{32,24},{40,32},{48,40},{56,48},{64,5... | collective-permute-start | bytes 49160 | tf_op jit(solution)/shard_map/ppermute | solution.py:522
  42.9 25.3 %copy-start.1 = (f32[1,1024]{1,0:T(1,128)S(1)}, f32[1,1024]{1,0:T(1,128)}, u32[]{:S(2)}) copy-start(f32[1,1024]{1,0:T(1,128)} %observed.1) | copy-start | bytes 12292
  42.9 25.3 %copy-start.2 = (f32[1,1024]{1,0:T(1,128)S(1)}, f32[1,1024]{1,0:T(1,128)}, u32[]{:S(2)}) copy-start(f32[1,1024]{1,0:T(1,128)} %variance.1) | copy-start | bytes 12292
  42.9 25.2 %all-to-all-start.1 = ((bf16[8,88,8,128]{3,2,1,0:T(8,128)(2,1)}), bf16[8,88,8,128]{3,2,1,0:T(8,128)(2,1)S(1)}, u32[]{:S(2)}, u32[]{:S(2)}) async-start(bf16[8,88,8,128]{3,2,1,0:T(8,128)(2,1)} %pad_maximum_fusion), calls=%async_computation.1 | async-start | bytes 2883584 | tf_op jit(solution)/shard_map/all_to_all | solution.py:559

commit v7 on v6

--- a/solution.py
+++ b/solution.py
@@ -348,15 +348,21 @@
     )(inner, cells, left, right, wide16, wide32)
 
 
-def transform_kernel(parts, cells, numbers, observed, variance, out, values, stack, sem):
+def transform_kernel(here, pair, ahead, across, behind, cells, numbers, observed, variance, out, stack):
     f32 = jnp.float32
-    exact = lax.Precision.HIGHEST
-    load = pltpu.make_async_copy(parts.at[:, pl.ds(CH, 8)], values, sem)
-    load.start()
-    load.wait()
-    for group in range(8):
-        for block in range(8):
-            stack[pl.ds(8 * group, 8), pl.ds(128 * block, 128)] = values[group, block].astype(f32)
+    exact = lax.Precision.HIGH
+    depth = numbers[2] & 3
+    half = numbers[2] >> 2
+    for step, ref in enumerate((None, ahead, across, behind)):
+        for other in range(2):
+            group = 4 * (half ^ other) + ((depth + step) & 3)
+            rows = pl.ds(pl.multiple_of(8 * group, 8), 8)
+            for block in range(8):
+                if ref is None:
+                    value = (here, pair)[other][block]
+                else:
+                    value = ref[other, block]
+                stack[rows, pl.ds(128 * block, 128)] = value.astype(f32)
     model_obs = stack[...]
     center = jnp.sum(model_obs, axis=0, keepdims=True) * (1.0 / 64.0)
     spread = model_obs - center
@@ -401,26 +407,22 @@
         out[pl.ds(64 * q, 64), :] = turned.astype(jnp.bfloat16)
 
 
-def transform_of(parts, cells, numbers, observed, variance):
+def transform_of(pieces, cells, numbers, observed, variance):
     smem = pl.BlockSpec(memory_space=pltpu.SMEM)
     return pl.pallas_call(
         transform_kernel,
-        in_specs=[anywhere(), vmem(), smem, vmem(), vmem()],
+        in_specs=[vmem()] * 6 + [smem, vmem(), vmem()],
         out_specs=vmem(),
         out_shape=jax.ShapeDtypeStruct((256, 256), jnp.bfloat16),
-        scratch_shapes=[
-            pltpu.VMEM((8, 8, 8, 128), jnp.bfloat16),
-            pltpu.VMEM((64, 1024), jnp.float32),
-            pltpu.SemaphoreType.DMA,
-        ],
+        scratch_shapes=[pltpu.VMEM((64, 1024), jnp.float32)],
         compiler_params=vmem_params(),
         cost_estimate=pl.CostEstimate(
             flops=100_000_000, bytes_accessed=500_000, transcendentals=1000
         ),
-    )(parts, cells, numbers, observed, variance)
-
-
-def mix_rows(parts, first, w, out, start):
+    )(*pieces, cells, numbers, observed, variance)
+
+
+def spread_rows(parts, first):
     centers = []
     halves = []
     for half in range(2):
@@ -431,7 +433,11 @@
             centers.append(center)
             stack.append((value.reshape(64, 128) - center).astype(jnp.bfloat16))
         halves.append(jnp.concatenate(stack, axis=0))
-    mixed = jnp.dot(w, jnp.concatenate(halves, axis=1), preferred_element_type=jnp.float32)
+    return jnp.concatenate(halves, axis=1), centers
+
+
+def mix_rows(spread, centers, w, out, start):
+    mixed = jnp.dot(w, spread, preferred_element_type=jnp.float32)
     for half in range(2):
         for q in range(4):
             value = mixed[64 * q : 64 * q + 64, 128 * half : 128 * half + 128]
@@ -446,7 +452,7 @@
         def block(n, carry):
             for k in range(5):
                 row = (5 * n + k) * 8
-                mix_rows(parts, row, w, out, start + row)
+                mix_rows(*spread_rows(parts, row), w, out, start + row)
             return carry
 
         lax.fori_loop(0, 2, block, 0)
@@ -520,6 +526,12 @@
 def ring(cells, step):
     count = lax.axis_size("space")
     return lax.ppermute(cells, "space", [(i, (i + step) % count) for i in range(count)])
+
+
+def depth_ring(cells, step):
+    return lax.ppermute(
+        cells, "mem", [(4 * y + (z + step) % 4, 4 * y + z) for y in range(2) for z in range(4)]
+    )
 
 
 def per_device(
@@ -552,15 +564,14 @@
     from_right = ring(picked[0], -1)
     part = (cells // 128 % 48 // 16).reshape(8, 1, 128)
     here = jnp.where(part == 0, from_left, jnp.where(part == 1, picked[1], from_right))
-    message = jnp.concatenate(
-        [edge, jnp.broadcast_to(here[None], (8, 8, 8, 128))], axis=1
-    )
-    message, first_parts = lax.optimization_barrier((message, first_parts))
-    second_parts = lax.all_to_all(message, "mem", split_axis=0, concat_axis=0, tiled=True)
-    numbers = jnp.stack([observed_count[0], local_radius[0]])
-    weights = transform_of(
-        second_parts, observed_cells, numbers, observed_value, error_variance
-    )
+    edge, first_parts = lax.optimization_barrier((edge, first_parts))
+    second_parts = lax.all_to_all(edge, "mem", split_axis=0, concat_axis=0, tiled=True)
+    pair = lax.ppermute(here, "mem", [(i, i ^ 4) for i in range(8)])
+    both = jnp.stack([here, pair])
+    pieces = (here, pair, depth_ring(both, 1), depth_ring(both, 2), depth_ring(both, 3))
+    group = lax.axis_index("mem").astype(jnp.int32)
+    numbers = jnp.stack([observed_count[0], local_radius[0], group])
+    weights = transform_of(pieces, observed_cells, numbers, observed_value, error_variance)
     mixed = mix(first_parts, second_parts, weights)
     back = lax.all_to_all(mixed, "mem", split_axis=0, concat_axis=0, tiled=True)
     return order(back)

time: 118 us -> 115 us (0.975)
  blocking collectives: 42.2 us -> 34.1 us
  starting transfers between devices: 19.5 us -> 24.7 us
  other arithmetic: 2.63 us -> 1.42 us
    all_to_all x1, waiting for transfers between devices: 15.9 us -> 0.01 us  [per_device(): lax.all_to_all(edge, 'mem', split_axis=0, concat_axis=0, tiled=True)]
    ppermute x0 -> x4, waiting for transfers between devices: none -> 13.9 us  [the longest x1 9.71 us: per_device(): pair = lax.ppermute(here, 'mem', [(i, i ^ 4) for i in range(8)])]
    ppermute x0 -> x4, starting transfers between devices: none -> 8.6 us  [the longest x3 4.39 us: depth_ring(): lax.ppermute(cells, 'mem', [(4 * y + (z + step) % 4, 4 * y + z) for y in...]
    all_to_all x1, blocking collectives: 42.2 us -> 34.1 us  [per_device(): back = lax.all_to_all(mixed, 'mem', split_axis=0, concat_axis=0, tiled=True)]
    all_to_all x1, starting transfers between devices: 7.95 us -> 4.6 us  [per_device(): lax.all_to_all(edge, 'mem', split_axis=0, concat_axis=0, tiled=True)]
    all_to_all x1, waiting for transfers between devices: 0.01 us -> 2.98 us  [per_device(): lax.all_to_all(inner, 'mem', split_axis=0, concat_axis=0, tiled=True)]
    concatenate x1 -> x0, other arithmetic: 1.23 us -> none  [per_device(): jnp.concatenate([edge, jnp.broadcast_to(here[None], (8, 8, 8, 128))], axi...]
  transfers between devices with their start and end apart: 6 -> 10, of which waited for: 3 -> 6; matrix products, arithmetic and copies ran while one was open for 1% -> 0% of each run, Pallas kernels for 21% -> 23%
where the time goes in v7:
time: 115 us; the launch traced here: 114 us
  blocking collectives  34.1 us (30%)
  Pallas kernels  30.4 us (26%)
  starting transfers between devices  24.7 us (21%)
  waiting for transfers between devices  18.4 us (16%)
  local copies, waits for them, and re-layouts  3.67 us (3%)
  between operations  1.58 us (1%)
  other arithmetic  1.42 us (1%)
    all_to_all x1, blocking collectives, per_device(): back = lax.all_to_all(mixed, 'mem', split_axis=0, concat_axis=0, tiled=True)  34.1 us
    pallas_call x1, Pallas kernels, edge_forecast(): pl.pallas_call(edge_kernel, in_specs=[anywhere()] * 6, out_specs=[vmem()]...  14 us
    pallas_call x1, Pallas kernels, inner_forecast(): pl.pallas_call(inner_kernel, in_specs=[vmem()] * 3, out_specs=[anywhere()...  10.1 us
    ppermute x1, waiting for transfers between devices, per_device(): pair = lax.ppermute(here, 'mem', [(i, i ^ 4) for i in range(8)])  9.71 us
    all_to_all x1, starting transfers between devices, per_device(): lax.all_to_all(inner, 'mem', split_axis=0, concat_axis=0, tiled=True)  7.96 us
    all_to_all x1, starting transfers between devices, per_device(): lax.all_to_all(edge, 'mem', split_axis=0, concat_axis=0, tiled=True)  4.6 us
    ppermute x3, starting transfers between devices, depth_ring(): lax.ppermute(cells, 'mem', [(4 * y + (z + step) % 4, 4 * y + z) for y in...  4.39 us
    ppermute x1, starting transfers between devices, per_device(): pair = lax.ppermute(here, 'mem', [(i, i ^ 4) for i in range(8)])  4.21 us
  transfers between devices with their start and end apart: 10, of which 6 were waited for; matrix products, arithmetic and copies ran while one was open for 0% of the time, Pallas kernels for 23%

profile of v7, /device:TPU:6, one launch (start us, length us, event | category | flops | bytes accessed | tf_op | source)
XLA Modules:
  0.0 114.3 jit_solution(16576573317519685467)
XLA Ops:
  0.0 2.4 %copy.9 = bf16[8,16,80,128]{3,2,1,0:T(8,128)(2,1)S(1)} copy(bf16[8,16,80,128]{3,1,2,0:T(8,128)(2,1)} %bitcast.18) | data formatting | bytes 5242880 | tf_op jit(solution)/shard_map/transpose | solution.py:549
  2.5 0.1 fusion.13
  2.7 1.3 %fusion.1 = (bf16[2592,128]{1,0:T(8,128)(2,1)S(1)}, bf16[2592,128]{1,0:T(8,128)(2,1)}) fusion(bf16[24,128]{1,0:T(8,128)(2,1)S(1)} %maximum_bitcast_fusion, bf16[2560,128]{1,0:T(8,128)(2,1)S(1)} %bitcast.19, bf16[2592]{0:T(1024)(128)(2,1)S(1)} %pad.10.clone, bf16[2560,128]{1,0:T(8,128)(2,1)S(1)} %bitcast.20), kind=kLoop, calls=%fused_computation.3 | loop fusion | flops 3317760 | bytes 2649152 | tf_op jit(solution)/shard_map/concatenate | solution.py:556
  3.9 1.7 %collective-permute-start.1 = (bf16[2592,128]{1,0:T(8,128)(2,1)S(1)}, bf16[2592,128]{1,0:T(8,128)(2,1)S(1)}, u32[]{:S(2)}, u32[]{:S(2)}) collective-permute-start(bf16[2592,128]{1,0:T(8,128)(2,1)S(1)} %get-tuple-element.25), channel_id=1, source_target_pairs={{0,120},{8,0},{16,8},{24,16},{32,24},{40,32},{48,40},{56,48},{64,5... | collective-permute-start | bytes 1990664 | tf_op jit(solution)/shard_map/ppermute | solution.py:528
  5.7 10.1 %shard_map.82 = (bf16[8,80,8,128]{3,2,1,0:T(8,128)(2,1)}, bf16[8,32768,128]{2,1,0:T(8,128)(2,1)}, f32[8,16384,128]{2,1,0:T(8,128)}) custom-call(bf16[8,1280,128]{2,1,0:T(8,128)(2,1)S(1)} %bitcast.12, bf16[9,80,80]{2,1,0:T(8,128)(2,1)S(1)} %copy-done.2, bf16[9,80,80]{2,1,0:T(8,128)(2,1)S(1)} %copy-done.3), custom_call_target="tpu_custom_call" | custom-call | flops 12000000000 | bytes 8000000 | tf_op jit(solution)/shard_map/pallas_call | solution.py:164
  15.8 8.0 %all-to-all-start = ((bf16[8,80,8,128]{3,2,1,0:T(8,128)(2,1)}), bf16[8,80,8,128]{3,2,1,0:T(8,128)(2,1)S(1)}, u32[]{:S(2)}, u32[]{:S(2)}) async-start(bf16[8,80,8,128]{3,2,1,0:T(8,128)(2,1)} %get-tuple-element.12.inner), calls=%async_computation | async-start | bytes 2621440 | tf_op jit(solution)/shard_map/all_to_all | solution.py:559
  23.8 14.0 %shard_map.83 = (bf16[8,80,8,128]{3,2,1,0:T(8,128)(2,1)S(1)}, bf16[24,8,128]{2,1,0:T(8,128)(2,1)S(1)}) custom-call(bf16[8,80,8,128]{3,2,1,0:T(8,128)(2,1)} %get-tuple-element.12.inner, s32[8,128]{1,0:T(8,128)S(1)} %bitcast.15, bf16[2592,128]{1,0:T(8,128)(2,1)S(1)} %collective-permute-done.left, bf16[2592,128]{1,0:T(8,128)(2,1)S(1)} %collective-permute-done.1.right, ...), custom_call_target="tpu_custom_call" | custom-call | flops 8999999488 | bytes 8000000 | tf_op jit(solution)/shard_map/pallas_call | solution.py:317
  37.7 1.1 copy-done
  38.8 3.0 %all-to-all-done.first = bf16[8,80,8,128]{3,2,1,0:T(8,128)(2,1)S(1)} async-done(((bf16[8,80,8,128]{3,2,1,0:T(8,128)(2,1)}), bf16[8,80,8,128]{3,2,1,0:T(8,128)(2,1)S(1)}, u32[]{:S(2)}, u32[]{:S(2)}) %all-to-all-start) | async-done | bytes 1310752 | tf_op jit(solution)/shard_map/all_to_all | solution.py:559
  41.8 4.6 %all-to-all-start.1 = ((bf16[8,80,8,128]{3,2,1,0:T(8,128)(2,1)}), bf16[8,80,8,128]{3,2,1,0:T(8,128)(2,1)S(1)}, u32[]{:S(2)}, u32[]{:S(2)}) async-start(bf16[8,80,8,128]{3,2,1,0:T(8,128)(2,1)} %copy-done), calls=%async_computation.1 | async-start | bytes 2621440 | tf_op jit(solution)/shard_map/all_to_all | solution.py:568
  46.5 1.7 %collective-permute-start.3 = (bf16[8,8,128]{2,1,0:T(8,128)(2,1)S(1)}, bf16[8,8,128]{2,1,0:T(8,128)(2,1)S(1)}, u32[]{:S(2)}, u32[]{:S(2)}) collective-permute-start(bf16[8,8,128]{2,1,0:T(8,128)(2,1)S(1)} %get-tuple-element.23), channel_id=1, source_target_pairs={{0,120},{8,0},{16,8},{24,16},{32,24},{40,32},{48,40},{56,48},{64,5... | collective-permute-start | bytes 49160 | tf_op jit(solution)/shard_map/ppermute | solution.py:528
  48.2 1.4 %collective-permute-done.2 = bf16[8,8,128]{2,1,0:T(8,128)(2,1)S(1)} collective-permute-done((bf16[8,8,128]{2,1,0:T(8,128)(2,1)S(1)}, bf16[8,8,128]{2,1,0:T(8,128)(2,1)S(1)}, u32[]{:S(2)}, u32[]{:S(2)}) %collective-permute-start.2) | collective-permute-done | bytes 16416 | tf_op jit(solution)/shard_map/ppermute | solution.py:528
  49.6 0.1 collective-permute-done.3
  49.8 4.2 %collective-permute-start.4 = (bf16[8,8,128]{2,1,0:T(8,128)(2,1)S(1)}, bf16[8,8,128]{2,1,0:T(8,128)(2,1)S(1)}, u32[]{:S(2)}, u32[]{:S(2)}) collective-permute-start(bf16[8,8,128]{2,1,0:T(8,128)(2,1)S(1)} %select_select_fusion.here), channel_id=1, source_target_pairs={{0,4},{1,5},{2,6},{3,7},{4,0},{5,1},{6,2},{7,3},{8,12},{9,13},{10,... | collective-permute-start | bytes 49160 | tf_op jit(solution)/shard_map/ppermute | solution.py:569
  55.3 9.7 %collective-permute-done.4.pair = bf16[8,8,128]{2,1,0:T(8,128)(2,1)S(1)} collective-permute-done((bf16[8,8,128]{2,1,0:T(8,128)(2,1)S(1)}, bf16[8,8,128]{2,1,0:T(8,128)(2,1)S(1)}, u32[]{:S(2)}, u32[]{:S(2)}) %collective-permute-start.4) | collective-permute-done | bytes 16416 | tf_op jit(solution)/shard_map/ppermute | solution.py:569
  65.0 2.7 %collective-permute-start.5 = (bf16[2,8,8,128]{3,2,1,0:T(8,128)(2,1)S(1)}, bf16[2,8,8,128]{3,2,1,0:T(8,128)(2,1)S(1)}, u32[]{:S(2)}, u32[]{:S(2)}) collective-permute-start(bf16[2,8,8,128]{3,2,1,0:T(8,128)(2,1)S(1)} %pad_maximum_fusion.2), channel_id=1, source_target_pairs={{1,0},{2,1},{3,2},{0,3},{5,4},{6,5},{7,6},{4,7},{9,8},{10,9},{11,1... | collective-permute-start | bytes 98312 | tf_op jit(solution)/shard_map/ppermute | solution.py:532
  67.7 0.9 collective-permute-start.6
  68.5 0.9 collective-permute-start.7
  69.5 3.6 %collective-permute-done.6.across = bf16[2,8,8,128]{3,2,1,0:T(8,128)(2,1)S(1)} collective-permute-done((bf16[2,8,8,128]{3,2,1,0:T(8,128)(2,1)S(1)}, bf16[2,8,8,128]{3,2,1,0:T(8,128)(2,1)S(1)}, u32[]{:S(2)}, u32[]{:S(2)}) %collective-permute-start.6) | collective-permute-done | bytes 32800 | tf_op jit(solution)/shard_map/ppermute | solution.py:532
  73.1 0.6 collective-permute-done.7.behind
  73.6 2.5 %shard_map.84.weights = bf16[256,256]{1,0:T(8,128)(2,1)S(1)} custom-call(bf16[8,8,128]{2,1,0:T(8,128)(2,1)S(1)} %select_select_fusion.here, bf16[8,8,128]{2,1,0:T(8,128)(2,1)S(1)} %collective-permute-done.4.pair, bf16[2,8,8,128]{3,2,1,0:T(8,128)(2,1)S(1)} %collective-permute-done.5.ahead, bf16[2,8,8,128]{3,2,1,0:T(8,128)(2,1)S(1)} %collective-permute-done.6.across, ...), custom_call_target="tpu_custom_call" | custom-call | flops 100000000 | bytes 500000 | tf_op jit(solution)/shard_map/pallas_call | solution.py:412
  76.2 2.0 %shard_map.85 = bf16[8,160,8,128]{3,2,1,0:T(8,128)(2,1)S(1)} custom-call(bf16[8,80,8,128]{3,2,1,0:T(8,128)(2,1)S(1)} %all-to-all-done.first, bf16[8,80,8,128]{3,2,1,0:T(8,128)(2,1)S(1)} %all-to-all-done.1.second, bf16[256,256]{1,0:T(8,128)(2,1)S(1)} %shard_map.84.weights), custom_call_target="tpu_custom_call" | custom-call | flops 700000000 | bytes 5300000 | tf_op jit(solution)/shard_map/pallas_call | solution.py:465
  78.2 34.1 %all_to_all.15.cells = bf16[8,160,8,128]{3,2,1,0:T(8,128)(2,1)S(1)} all-to-all(bf16[8,160,8,128]{3,2,1,0:T(8,128)(2,1)S(1)} %shard_map.85), channel_id=1, replica_groups=mesh['space'=16,'mem'=8] {'mem'}, dimensions={0} | all-to-all | bytes 5242880 | tf_op jit(solution)/shard_map/all_to_all | solution.py:576
  112.3 1.8 %shard_map.86 = bf16[8,80,16,128]{3,2,1,0:T(8,128)(2,1)} custom-call(bf16[8,160,8,128]{3,2,1,0:T(8,128)(2,1)S(1)} %all_to_all.15.cells), custom_call_target="tpu_custom_call" | custom-call | flops 600000000 | bytes 5300000 | tf_op jit(solution)/shard_map/pallas_call | solution.py:510
  (27 shorter events, 0.3 us)
Async XLA Ops:
  0.0 2.4 %copy-start.1 = (s32[1,1024]{1,0:T(1,128)S(1)}, s32[1,1024]{1,0:T(1,128)}, u32[]{:S(2)}) copy-start(s32[1,1024]{1,0:T(1,128)} %cells.1) | copy-start | bytes 12292
  2.7 3.0 %copy-start.2 = (bf16[9,80,80]{2,1,0:T(8,128)(2,1)S(1)}, bf16[9,80,80]{2,1,0:T(8,128)(2,1)}, u32[]{:S(2)}) copy-start(bf16[9,80,80]{2,1,0:T(8,128)(2,1)} %first_taps.1) | copy-start | bytes 345604
  2.7 3.0 %copy-start.3 = (bf16[9,80,80]{2,1,0:T(8,128)(2,1)S(1)}, bf16[9,80,80]{2,1,0:T(8,128)(2,1)}, u32[]{:S(2)}) copy-start(bf16[9,80,80]{2,1,0:T(8,128)(2,1)} %second_taps.1) | copy-start | bytes 345604
  3.9 19.8 %collective-permute-start = (bf16[2592,128]{1,0:T(8,128)(2,1)}, bf16[2592,128]{1,0:T(8,128)(2,1)S(1)}, u32[]{:S(2)}, u32[]{:S(2)}) collective-permute-start(bf16[2592,128]{1,0:T(8,128)(2,1)} %get-tuple-element.26), channel_id=1, source_target_pairs={{0,8},{8,16},{16,24},{24,32},{32,40},{40,48},{48,56},{56,64},{64,7... | collective-permute-start | bytes 1990664 | tf_op jit(solution)/shard_map/ppermute | solution.py:528
  3.9 19.8 %collective-permute-start.1 = (bf16[2592,128]{1,0:T(8,128)(2,1)S(1)}, bf16[2592,128]{1,0:T(8,128)(2,1)S(1)}, u32[]{:S(2)}, u32[]{:S(2)}) collective-permute-start(bf16[2592,128]{1,0:T(8,128)(2,1)S(1)} %get-tuple-element.25), channel_id=1, source_target_pairs={{0,120},{8,0},{16,8},{24,16},{32,24},{40,32},{48,40},{56,48},{64,5... | collective-permute-start | bytes 1990664 | tf_op jit(solution)/shard_map/ppermute | solution.py:528
  15.8 26.0 %all-to-all-start = ((bf16[8,80,8,128]{3,2,1,0:T(8,128)(2,1)}), bf16[8,80,8,128]{3,2,1,0:T(8,128)(2,1)S(1)}, u32[]{:S(2)}, u32[]{:S(2)}) async-start(bf16[8,80,8,128]{3,2,1,0:T(8,128)(2,1)} %get-tuple-element.12.inner), calls=%async_computation | async-start | bytes 2621440 | tf_op jit(solution)/shard_map/all_to_all | solution.py:559
  37.7 1.1 copy-start
  41.8 31.9 %copy-start.4 = (f32[1,1024]{1,0:T(1,128)S(1)}, f32[1,1024]{1,0:T(1,128)}, u32[]{:S(2)}) copy-start(f32[1,1024]{1,0:T(1,128)} %observed.1) | copy-start | bytes 12292
  41.8 31.9 %copy-start.5 = (f32[1,1024]{1,0:T(1,128)S(1)}, f32[1,1024]{1,0:T(1,128)}, u32[]{:S(2)}) copy-start(f32[1,1024]{1,0:T(1,128)} %variance.1) | copy-start | bytes 12292
  41.8 34.4 %all-to-all-start.1 = ((bf16[8,80,8,128]{3,2,1,0:T(8,128)(2,1)}), bf16[8,80,8,128]{3,2,1,0:T(8,128)(2,1)S(1)}, u32[]{:S(2)}, u32[]{:S(2)}) async-start(bf16[8,80,8,128]{3,2,1,0:T(8,128)(2,1)} %copy-done), calls=%async_computation.1 | async-start | bytes 2621440 | tf_op jit(solution)/shard_map/all_to_all | solution.py:568
  46.4 3.2 %collective-permute-start.2 = (bf16[8,8,128]{2,1,0:T(8,128)(2,1)S(1)}, bf16[8,8,128]{2,1,0:T(8,128)(2,1)S(1)}, u32[]{:S(2)}, u32[]{:S(2)}) collective-permute-start(bf16[8,8,128]{2,1,0:T(8,128)(2,1)S(1)} %get-tuple-element.24), channel_id=1, source_target_pairs={{0,8},{8,16},{16,24},{24,32},{32,40},{40,48},{48,56},{56,64},{64,7... | collective-permute-start | bytes 49160 | tf_op jit(solution)/shard_map/ppermute | solution.py:528
  46.5 3.2 %collective-permute-start.3 = (bf16[8,8,128]{2,1,0:T(8,128)(2,1)S(1)}, bf16[8,8,128]{2,1,0:T(8,128)(2,1)S(1)}, u32[]{:S(2)}, u32[]{:S(2)}) collective-permute-start(bf16[8,8,128]{2,1,0:T(8,128)(2,1)S(1)} %get-tuple-element.23), channel_id=1, source_target_pairs={{0,120},{8,0},{16,8},{24,16},{32,24},{40,32},{48,40},{56,48},{64,5... | collective-permute-start | bytes 49160 | tf_op jit(solution)/shard_map/ppermute | solution.py:528
  49.8 15.2 %collective-permute-start.4 = (bf16[8,8,128]{2,1,0:T(8,128)(2,1)S(1)}, bf16[8,8,128]{2,1,0:T(8,128)(2,1)S(1)}, u32[]{:S(2)}, u32[]{:S(2)}) collective-permute-start(bf16[8,8,128]{2,1,0:T(8,128)(2,1)S(1)} %select_select_fusion.here), channel_id=1, source_target_pairs={{0,4},{1,5},{2,6},{3,7},{4,0},{5,1},{6,2},{7,3},{8,12},{9,13},{10,... | collective-permute-start | bytes 49160 | tf_op jit(solution)/shard_map/ppermute | solution.py:569
  65.0 4.5 %collective-permute-start.5 = (bf16[2,8,8,128]{3,2,1,0:T(8,128)(2,1)S(1)}, bf16[2,8,8,128]{3,2,1,0:T(8,128)(2,1)S(1)}, u32[]{:S(2)}, u32[]{:S(2)}) collective-permute-start(bf16[2,8,8,128]{3,2,1,0:T(8,128)(2,1)S(1)} %pad_maximum_fusion.2), channel_id=1, source_target_pairs={{1,0},{2,1},{3,2},{0,3},{5,4},{6,5},{7,6},{4,7},{9,8},{10,9},{11,1... | collective-permute-start | bytes 98312 | tf_op jit(solution)/shard_map/ppermute | solution.py:532
  67.7 5.4 %collective-permute-start.6 = (bf16[2,8,8,128]{3,2,1,0:T(8,128)(2,1)S(1)}, bf16[2,8,8,128]{3,2,1,0:T(8,128)(2,1)S(1)}, u32[]{:S(2)}, u32[]{:S(2)}) collective-permute-start(bf16[2,8,8,128]{3,2,1,0:T(8,128)(2,1)S(1)} %pad_maximum_fusion.2), channel_id=1, source_target_pairs={{2,0},{3,1},{0,2},{1,3},{6,4},{7,5},{4,6},{5,7},{10,8},{11,9},{8,1... | collective-permute-start | bytes 98312 | tf_op jit(solution)/shard_map/ppermute | solution.py:532
  68.5 5.1 %collective-permute-start.7 = (bf16[2,8,8,128]{3,2,1,0:T(8,128)(2,1)S(1)}, bf16[2,8,8,128]{3,2,1,0:T(8,128)(2,1)S(1)}, u32[]{:S(2)}, u32[]{:S(2)}) collective-permute-start(bf16[2,8,8,128]{3,2,1,0:T(8,128)(2,1)S(1)} %pad_maximum_fusion.2), channel_id=1, source_target_pairs={{3,0},{0,1},{1,2},{2,3},{7,4},{4,5},{5,6},{6,7},{11,8},{8,9},{9,10... | collective-permute-start | bytes 98312 | tf_op jit(solution)/shard_map/ppermute | solution.py:532

commit v8 on v7

--- a/solution.py
+++ b/solution.py
@@ -11,8 +11,7 @@
 STEP_SIZE = 0.5
 HALO = 4
 CH = 80
-PAIR_A = 8
-LAG = 3
+LAG = 4
 
 
 def vmem_params():
@@ -105,57 +104,58 @@
     ]
     early = begin(early + taps_moves(taps, wide16), sems)
 
-    def group(n, carry):
-        jobs = []
-        for i in range(PAIR_A):
-            m = n * PAIR_A + i
-            v, hm, sm, gm, rm = own.at[m], h.at[m], s.at[m], g.at[m], rate.at[m]
-
-            def put_first(k, value, hm=hm):
-                hm[pl.ds(CH * k, CH), :] = gelu(value).astype(jnp.bfloat16)
-
-            def put_section(k, value, v=v, sm=sm, rm=rm):
-                base = v[pl.ds(CH * (k + 2), CH), :].astype(jnp.float32)
-                sm[pl.ds(CH * k, CH), :] = (base + STEP_SIZE * value).astype(jnp.bfloat16)
-                rm[pl.ds(CH * k, CH), :] = base + 0.5 * STEP_SIZE * value
-
-            def put_second(k, value, gm=gm):
-                gm[pl.ds(CH * k, CH), :] = gelu(value).astype(jnp.bfloat16)
-
-            def put_forecast(k, value, rm=rm, m=m):
-                cells = rm[pl.ds(CH * (k + 2), CH), :] + 0.5 * STEP_SIZE * value
-                fields[pl.ds(8 * CH * k + m, CH, stride=8), :] = cells
-
-            stages = (
-                (v, a, 14, put_first),
-                (hm, b, 12, put_section),
-                (sm, a, 10, put_second),
-                (gm, b, 8, put_forecast),
-            )
-            for level, (source, matrix, columns, emit) in enumerate(stages):
-                for k in range(0, columns, 2):
-                    step = functools.partial(conv_pair, source, k, matrix, emit, k)
-                    jobs.append(((k // 2 + LAG * level, i, level), step))
-        run_interleaved(jobs)
-        return carry
-
-    lax.fori_loop(0, members // PAIR_A, group, 0)
-    late = []
+    sent = []
+
+    def save(source, target):
+        sent.extend(begin([(source, target)], sems, len(early) + len(sent)))
+
+    def send(x):
+        for column in (x, x + 1):
+            cells = fields[pl.ds(8 * CH * column, 8 * CH), :].astype(jnp.bfloat16)
+            cells16[column] = cells.reshape(CH, 8, 128)
+        save(cells16.at[pl.ds(x, 2)], out.at[pl.ds(x, 2)])
+
+    jobs = []
     for side in range(2):
-        for k, (ref, right) in enumerate(((h, 12), (s, 10), (g, 8))):
-            target = wide16.at[:, pl.ds(SAVED + 6 * CH * side + 2 * CH * k, 2 * CH)]
-            late.append((ref.at[:, pl.ds(CH * right * side, 2 * CH)], target))
+        for level, ref, right, ready in ((0, h, 12, 6), (1, s, 10, 5 + LAG), (2, g, 8, 4 + 2 * LAG)):
+            source = ref.at[:, pl.ds(CH * right * side, 2 * CH)]
+            target = wide16.at[:, pl.ds(SAVED + 6 * CH * side + 2 * CH * level, 2 * CH)]
+            jobs.append(((ready, members, side), functools.partial(save, source, target)))
+        source = rate.at[:, pl.ds(10 * CH * side, 2 * CH)]
         target = wide32.at[:, pl.ds(2 * CH * side, 2 * CH)]
-        late.append((rate.at[:, pl.ds(10 * CH * side, 2 * CH)], target))
-    late = begin(late, sems, len(early))
-    last = []
-    for x in range(8):
-        column = fields[pl.ds(8 * CH * x, 8 * CH), :].astype(jnp.bfloat16)
-        cells16[x] = column.reshape(CH, 8, 128)
-        if x % 2:
-            pair = pl.ds(x - 1, 2)
-            last += begin([(cells16.at[pair], out.at[pair])], sems, len(early) + len(late) + x // 2)
-    finish(early + late + last)
+        jobs.append(((5 + LAG, members, 2 + side), functools.partial(save, source, target)))
+    for k in range(0, 8, 2):
+        jobs.append(((k // 2 + 3 * LAG, members, 4), functools.partial(send, k)))
+    for m in range(members):
+        v, hm, sm, gm, rm = own.at[m], h.at[m], s.at[m], g.at[m], rate.at[m]
+
+        def put_first(k, value, hm=hm):
+            hm[pl.ds(CH * k, CH), :] = gelu(value).astype(jnp.bfloat16)
+
+        def put_section(k, value, v=v, sm=sm, rm=rm):
+            base = v[pl.ds(CH * (k + 2), CH), :].astype(jnp.float32)
+            sm[pl.ds(CH * k, CH), :] = (base + STEP_SIZE * value).astype(jnp.bfloat16)
+            rm[pl.ds(CH * k, CH), :] = base + 0.5 * STEP_SIZE * value
+
+        def put_second(k, value, gm=gm):
+            gm[pl.ds(CH * k, CH), :] = gelu(value).astype(jnp.bfloat16)
+
+        def put_forecast(k, value, rm=rm, m=m):
+            cells = rm[pl.ds(CH * (k + 2), CH), :] + 0.5 * STEP_SIZE * value
+            fields[pl.ds(8 * CH * k + m, CH, stride=8), :] = cells
+
+        stages = (
+            (v, a, 14, put_first),
+            (hm, b, 12, put_section),
+            (sm, a, 10, put_second),
+            (gm, b, 8, put_forecast),
+        )
+        for level, (source, matrix, columns, emit) in enumerate(stages):
+            for k in range(0, columns, 2):
+                step = functools.partial(conv_pair, source, k, matrix, emit, k)
+                jobs.append(((k // 2 + LAG * level, m, level), step))
+    run_interleaved(jobs)
+    finish(early + sent)
 
 
 def inner_forecast(own, first_taps, second_taps):
@@ -238,7 +238,7 @@
 
 def edge_kernel(
     inner, cells, left, right, wide16, wide32, out, picked,
-    taps, v, h, s, g, rate, rated, fields, inner16, lists, own_list, places, rows, turns,
+    taps, v, h, s, g, rate, rated, fields, inner16, cells16, lists, own_list, places, rows, turns,
     sems, list_sems, place_sems,
 ):
     members = v.shape[1]
@@ -292,8 +292,9 @@
             jobs.append(((0, 4 * n, -1, 0), functools.partial(finish, columns[m])))
     jobs.append(((1, -1, 0, 0), functools.partial(finish, later + inner_copy)))
     run_interleaved(jobs)
+    cells16[...] = fields[pl.ds(64 * CH, 64 * CH), :].astype(jnp.bfloat16).reshape(cells16.shape)
+    out_copy = begin([(cells16, out)], sems, 0)
     fields[pl.ds(0, 64 * CH), :] = inner16[...].astype(jnp.float32).reshape(64 * CH, 128)
-    out[...] = fields[pl.ds(64 * CH, 64 * CH), :].astype(jnp.bfloat16).reshape(out.shape)
     finish(place_copies)
     lane = lax.broadcasted_iota(jnp.int32, (8, 128), 1)
 
@@ -309,6 +310,7 @@
         return carry
 
     lax.fori_loop(0, 8, block, 0)
+    finish(out_copy)
 
 
 def edge_forecast(inner, cells, left, right, wide16, wide32):
@@ -317,7 +319,7 @@
     return pl.pallas_call(
         edge_kernel,
         in_specs=[anywhere()] * 6,
-        out_specs=[vmem()] * 2,
+        out_specs=[anywhere(), vmem()],
         out_shape=[
             jax.ShapeDtypeStruct((8, CH, 8, 128), bf16),
             jax.ShapeDtypeStruct((24, 8, 128), bf16),
@@ -331,6 +333,7 @@
             pltpu.VMEM((2, members, 2 * CH, 128), f32),
             pltpu.VMEM((members, 4 * CH, 128), f32),
             pltpu.VMEM((128 * CH, 128), f32),
+            pltpu.VMEM((8, CH, 8, 128), bf16),
             pltpu.VMEM((8, CH, 8, 128), bf16),
             pltpu.VMEM((2, 32, 128), bf16),
             pltpu.VMEM((8, 128), jnp.int32),
@@ -348,7 +351,10 @@
     )(inner, cells, left, right, wide16, wide32)
 
 
-def transform_kernel(here, pair, ahead, across, behind, cells, numbers, observed, variance, out, stack):
+def transform_kernel(
+    here, pair, ahead, across, behind, cells, numbers, observed, variance, edge, out, stack
+):
+    del edge
     f32 = jnp.float32
     exact = lax.Precision.HIGH
     depth = numbers[2] & 3
@@ -407,11 +413,11 @@
         out[pl.ds(64 * q, 64), :] = turned.astype(jnp.bfloat16)
 
 
-def transform_of(pieces, cells, numbers, observed, variance):
+def transform_of(pieces, cells, numbers, observed, variance, edge):
     smem = pl.BlockSpec(memory_space=pltpu.SMEM)
     return pl.pallas_call(
         transform_kernel,
-        in_specs=[vmem()] * 6 + [smem, vmem(), vmem()],
+        in_specs=[vmem()] * 6 + [smem, vmem(), vmem(), anywhere()],
         out_specs=vmem(),
         out_shape=jax.ShapeDtypeStruct((256, 256), jnp.bfloat16),
         scratch_shapes=[pltpu.VMEM((64, 1024), jnp.float32)],
@@ -419,7 +425,7 @@
         cost_estimate=pl.CostEstimate(
             flops=100_000_000, bytes_accessed=500_000, transcendentals=1000
         ),
-    )(*pieces, cells, numbers, observed, variance)
+    )(*pieces, cells, numbers, observed, variance, edge)
 
 
 def spread_rows(parts, first):
@@ -571,7 +577,9 @@
     pieces = (here, pair, depth_ring(both, 1), depth_ring(both, 2), depth_ring(both, 3))
     group = lax.axis_index("mem").astype(jnp.int32)
     numbers = jnp.stack([observed_count[0], local_radius[0], group])
-    weights = transform_of(pieces, observed_cells, numbers, observed_value, error_variance)
+    weights = transform_of(
+        pieces, observed_cells, numbers, observed_value, error_variance, edge
+    )
     mixed = mix(first_parts, second_parts, weights)
     back = lax.all_to_all(mixed, "mem", split_axis=0, concat_axis=0, tiled=True)
     return order(back)

time: 115 us -> 114 us (level)
  waiting for transfers between devices: 18.4 us -> 20.1 us
  transfers between devices with their start and end apart: 10 -> 10, of which waited for: 6 -> 5; matrix products, arithmetic and copies ran while one was open for 0% -> 0% of each run, Pallas kernels for 23% -> 23%
where the time goes in v8:
time: 114 us
  blocking collectives  34.1 us (30%)
  Pallas kernels  30.1 us (26%)
  starting transfers between devices  24.1 us (21%)
  waiting for transfers between devices  20.1 us (18%)
  local copies, waits for them, and re-layouts  2.62 us (2%)
  between operations  1.57 us (1%)
  other arithmetic  1.43 us (1%)
    all_to_all x1, blocking collectives, per_device(): back = lax.all_to_all(mixed, 'mem', split_axis=0, concat_axis=0, tiled=True)  34.1 us
    pallas_call x1, Pallas kernels, edge_forecast(): pl.pallas_call(edge_kernel, in_specs=[anywhere()] * 6, out_specs=[anywher...  14 us
    ppermute x1, waiting for transfers between devices, per_device(): pair = lax.ppermute(here, 'mem', [(i, i ^ 4) for i in range(8)])  10.4 us
    pallas_call x1, Pallas kernels, inner_forecast(): pl.pallas_call(inner_kernel, in_specs=[vmem()] * 3, out_specs=[anywhere()...  9.8 us
    all_to_all x1, starting transfers between devices, per_device(): lax.all_to_all(inner, 'mem', split_axis=0, concat_axis=0, tiled=True)  7.96 us
    all_to_all x1, starting transfers between devices, per_device(): lax.all_to_all(edge, 'mem', split_axis=0, concat_axis=0, tiled=True)  4.6 us
    ppermute x3, starting transfers between devices, depth_ring(): lax.ppermute(cells, 'mem', [(4 * y + (z + step) % 4, 4 * y + z) for y in...  4.39 us
    ppermute x3, waiting for transfers between devices, depth_ring(): lax.ppermute(cells, 'mem', [(4 * y + (z + step) % 4, 4 * y + z) for y in...  4.19 us
  transfers between devices with their start and end apart: 10, of which 5 were waited for; matrix products, arithmetic and copies ran while one was open for 0% of the time, Pallas kernels for 23%

profile of v8, /device:TPU:6, one launch (start us, length us, event | category | flops | bytes accessed | tf_op | source)
XLA Modules:
  0.0 114.0 jit_solution(14390894602229851237)
XLA Ops:
  0.0 2.4 %copy.9 = bf16[8,16,80,128]{3,2,1,0:T(8,128)(2,1)S(1)} copy(bf16[8,16,80,128]{3,1,2,0:T(8,128)(2,1)} %bitcast.18) | data formatting | bytes 5242880 | tf_op jit(solution)/shard_map/transpose | solution.py:555
  2.5 0.1 fusion.13
  2.6 0.1 pad.10.clone
  2.7 1.3 %fusion.1 = (bf16[2592,128]{1,0:T(8,128)(2,1)S(1)}, bf16[2592,128]{1,0:T(8,128)(2,1)}) fusion(bf16[24,128]{1,0:T(8,128)(2,1)S(1)} %maximum_bitcast_fusion, bf16[2560,128]{1,0:T(8,128)(2,1)S(1)} %bitcast.19, bf16[2592]{0:T(1024)(128)(2,1)S(1)} %pad.10.clone, bf16[2560,128]{1,0:T(8,128)(2,1)S(1)} %bitcast.20), kind=kLoop, calls=%fused_computation.3 | loop fusion | flops 3317760 | bytes 2649152 | tf_op jit(solution)/shard_map/concatenate | solution.py:562
  3.9 1.7 %collective-permute-start.1 = (bf16[2592,128]{1,0:T(8,128)(2,1)S(1)}, bf16[2592,128]{1,0:T(8,128)(2,1)S(1)}, u32[]{:S(2)}, u32[]{:S(2)}) collective-permute-start(bf16[2592,128]{1,0:T(8,128)(2,1)S(1)} %get-tuple-element.25), channel_id=1, source_target_pairs={{0,120},{8,0},{16,8},{24,16},{32,24},{40,32},{48,40},{56,48},{64,5... | collective-permute-start | bytes 1990664 | tf_op jit(solution)/shard_map/ppermute | solution.py:534
  5.7 9.8 %shard_map.82 = (bf16[8,80,8,128]{3,2,1,0:T(8,128)(2,1)}, bf16[8,32768,128]{2,1,0:T(8,128)(2,1)}, f32[8,16384,128]{2,1,0:T(8,128)}) custom-call(bf16[8,1280,128]{2,1,0:T(8,128)(2,1)S(1)} %bitcast.12, bf16[9,80,80]{2,1,0:T(8,128)(2,1)S(1)} %copy-done.3, bf16[9,80,80]{2,1,0:T(8,128)(2,1)S(1)} %copy-done.4), custom_call_target="tpu_custom_call" | custom-call | flops 12000000000 | bytes 8000000 | tf_op jit(solution)/shard_map/pallas_call | solution.py:164
  15.5 8.0 %all-to-all-start = ((bf16[8,80,8,128]{3,2,1,0:T(8,128)(2,1)}), bf16[8,80,8,128]{3,2,1,0:T(8,128)(2,1)S(1)}, u32[]{:S(2)}, u32[]{:S(2)}) async-start(bf16[8,80,8,128]{3,2,1,0:T(8,128)(2,1)} %get-tuple-element.12.inner), calls=%async_computation | async-start | bytes 2621440 | tf_op jit(solution)/shard_map/all_to_all | solution.py:565
  23.5 14.0 %shard_map.83 = (bf16[8,80,8,128]{3,2,1,0:T(8,128)(2,1)}, bf16[24,8,128]{2,1,0:T(8,128)(2,1)S(1)}) custom-call(bf16[8,80,8,128]{3,2,1,0:T(8,128)(2,1)} %get-tuple-element.12.inner, s32[8,128]{1,0:T(8,128)S(1)} %bitcast.15, bf16[2592,128]{1,0:T(8,128)(2,1)S(1)} %collective-permute-done.left, bf16[2592,128]{1,0:T(8,128)(2,1)S(1)} %collective-permute-done.1.right, ...), custom_call_target="tpu_custom_call" | custom-call | flops 8999999488 | bytes 8000000 | tf_op jit(solution)/shard_map/pallas_call | solution.py:319
  37.4 4.0 %all-to-all-done.first = bf16[8,80,8,128]{3,2,1,0:T(8,128)(2,1)S(1)} async-done(((bf16[8,80,8,128]{3,2,1,0:T(8,128)(2,1)}), bf16[8,80,8,128]{3,2,1,0:T(8,128)(2,1)S(1)}, u32[]{:S(2)}, u32[]{:S(2)}) %all-to-all-start) | async-done | bytes 1310752 | tf_op jit(solution)/shard_map/all_to_all | solution.py:565
  41.5 4.6 %all-to-all-start.1 = ((bf16[8,80,8,128]{3,2,1,0:T(8,128)(2,1)}), bf16[8,80,8,128]{3,2,1,0:T(8,128)(2,1)S(1)}, u32[]{:S(2)}, u32[]{:S(2)}) async-start(bf16[8,80,8,128]{3,2,1,0:T(8,128)(2,1)} %get-tuple-element.17.edge), calls=%async_computation.1 | async-start | bytes 2621440 | tf_op jit(solution)/shard_map/all_to_all | solution.py:574
  46.2 1.7 %collective-permute-start.3 = (bf16[8,8,128]{2,1,0:T(8,128)(2,1)S(1)}, bf16[8,8,128]{2,1,0:T(8,128)(2,1)S(1)}, u32[]{:S(2)}, u32[]{:S(2)}) collective-permute-start(bf16[8,8,128]{2,1,0:T(8,128)(2,1)S(1)} %get-tuple-element.23), channel_id=1, source_target_pairs={{0,120},{8,0},{16,8},{24,16},{32,24},{40,32},{48,40},{56,48},{64,5... | collective-permute-start | bytes 49160 | tf_op jit(solution)/shard_map/ppermute | solution.py:534
  47.9 1.4 %collective-permute-done.2 = bf16[8,8,128]{2,1,0:T(8,128)(2,1)S(1)} collective-permute-done((bf16[8,8,128]{2,1,0:T(8,128)(2,1)S(1)}, bf16[8,8,128]{2,1,0:T(8,128)(2,1)S(1)}, u32[]{:S(2)}, u32[]{:S(2)}) %collective-permute-start.2) | collective-permute-done | bytes 16416 | tf_op jit(solution)/shard_map/ppermute | solution.py:534
  49.4 3.6 %collective-permute-start.4 = (bf16[8,8,128]{2,1,0:T(8,128)(2,1)S(1)}, bf16[8,8,128]{2,1,0:T(8,128)(2,1)S(1)}, u32[]{:S(2)}, u32[]{:S(2)}) collective-permute-start(bf16[8,8,128]{2,1,0:T(8,128)(2,1)S(1)} %select_select_fusion.here), channel_id=1, source_target_pairs={{0,4},{1,5},{2,6},{3,7},{4,0},{5,1},{6,2},{7,3},{8,12},{9,13},{10,... | collective-permute-start | bytes 49160 | tf_op jit(solution)/shard_map/ppermute | solution.py:575
  54.3 10.4 %collective-permute-done.4.pair = bf16[8,8,128]{2,1,0:T(8,128)(2,1)S(1)} collective-permute-done((bf16[8,8,128]{2,1,0:T(8,128)(2,1)S(1)}, bf16[8,8,128]{2,1,0:T(8,128)(2,1)S(1)}, u32[]{:S(2)}, u32[]{:S(2)}) %collective-permute-start.4) | collective-permute-done | bytes 16416 | tf_op jit(solution)/shard_map/ppermute | solution.py:575
  64.7 2.7 %collective-permute-start.5 = (bf16[2,8,8,128]{3,2,1,0:T(8,128)(2,1)S(1)}, bf16[2,8,8,128]{3,2,1,0:T(8,128)(2,1)S(1)}, u32[]{:S(2)}, u32[]{:S(2)}) collective-permute-start(bf16[2,8,8,128]{3,2,1,0:T(8,128)(2,1)S(1)} %pad_maximum_fusion.2), channel_id=1, source_target_pairs={{1,0},{2,1},{3,2},{0,3},{5,4},{6,5},{7,6},{4,7},{9,8},{10,9},{11,1... | collective-permute-start | bytes 98312 | tf_op jit(solution)/shard_map/ppermute | solution.py:538
  67.4 0.9 collective-permute-start.6
  68.2 0.9 collective-permute-start.7
  69.1 0.1 pad_add_fusion.numbers
  69.2 3.6 %collective-permute-done.6.across = bf16[2,8,8,128]{3,2,1,0:T(8,128)(2,1)S(1)} collective-permute-done((bf16[2,8,8,128]{3,2,1,0:T(8,128)(2,1)S(1)}, bf16[2,8,8,128]{3,2,1,0:T(8,128)(2,1)S(1)}, u32[]{:S(2)}, u32[]{:S(2)}) %collective-permute-start.6) | collective-permute-done | bytes 32800 | tf_op jit(solution)/shard_map/ppermute | solution.py:538
  72.8 0.6 collective-permute-done.7.behind
  73.4 2.5 %shard_map.84.weights = bf16[256,256]{1,0:T(8,128)(2,1)S(1)} custom-call(bf16[8,8,128]{2,1,0:T(8,128)(2,1)S(1)} %select_select_fusion.here, bf16[8,8,128]{2,1,0:T(8,128)(2,1)S(1)} %collective-permute-done.4.pair, bf16[2,8,8,128]{3,2,1,0:T(8,128)(2,1)S(1)} %collective-permute-done.5.ahead, bf16[2,8,8,128]{3,2,1,0:T(8,128)(2,1)S(1)} %collective-permute-done.6.across, ...), custom_call_target="tpu_custom_call" | custom-call | flops 100000000 | bytes 500000 | tf_op jit(solution)/shard_map/pallas_call | solution.py:418
  75.9 2.0 %shard_map.85 = bf16[8,160,8,128]{3,2,1,0:T(8,128)(2,1)S(1)} custom-call(bf16[8,80,8,128]{3,2,1,0:T(8,128)(2,1)S(1)} %all-to-all-done.first, bf16[8,80,8,128]{3,2,1,0:T(8,128)(2,1)S(1)} %all-to-all-done.1.second, bf16[256,256]{1,0:T(8,128)(2,1)S(1)} %shard_map.84.weights), custom_call_target="tpu_custom_call" | custom-call | flops 700000000 | bytes 5300000 | tf_op jit(solution)/shard_map/pallas_call | solution.py:471
  77.9 34.1 %all_to_all.15.cells = bf16[8,160,8,128]{3,2,1,0:T(8,128)(2,1)S(1)} all-to-all(bf16[8,160,8,128]{3,2,1,0:T(8,128)(2,1)S(1)} %shard_map.85), channel_id=1, replica_groups=mesh['space'=16,'mem'=8] {'mem'}, dimensions={0} | all-to-all | bytes 5242880 | tf_op jit(solution)/shard_map/all_to_all | solution.py:584
  112.0 1.8 %shard_map.86 = bf16[8,80,16,128]{3,2,1,0:T(8,128)(2,1)} custom-call(bf16[8,160,8,128]{3,2,1,0:T(8,128)(2,1)S(1)} %all_to_all.15.cells), custom_call_target="tpu_custom_call" | custom-call | flops 600000000 | bytes 5300000 | tf_op jit(solution)/shard_map/pallas_call | solution.py:516
  (25 shorter events, 0.2 us)
Async XLA Ops:
  0.0 2.4 %copy-start = (s32[1,1024]{1,0:T(1,128)S(1)}, s32[1,1024]{1,0:T(1,128)}, u32[]{:S(2)}) copy-start(s32[1,1024]{1,0:T(1,128)} %cells.1) | copy-start | bytes 12292
  2.7 3.0 %copy-start.3 = (bf16[9,80,80]{2,1,0:T(8,128)(2,1)S(1)}, bf16[9,80,80]{2,1,0:T(8,128)(2,1)}, u32[]{:S(2)}) copy-start(bf16[9,80,80]{2,1,0:T(8,128)(2,1)} %first_taps.1) | copy-start | bytes 345604
  2.7 3.0 %copy-start.4 = (bf16[9,80,80]{2,1,0:T(8,128)(2,1)S(1)}, bf16[9,80,80]{2,1,0:T(8,128)(2,1)}, u32[]{:S(2)}) copy-start(bf16[9,80,80]{2,1,0:T(8,128)(2,1)} %second_taps.1) | copy-start | bytes 345604
  3.9 19.5 %collective-permute-start = (bf16[2592,128]{1,0:T(8,128)(2,1)}, bf16[2592,128]{1,0:T(8,128)(2,1)S(1)}, u32[]{:S(2)}, u32[]{:S(2)}) collective-permute-start(bf16[2592,128]{1,0:T(8,128)(2,1)} %get-tuple-element.26), channel_id=1, source_target_pairs={{0,8},{8,16},{16,24},{24,32},{32,40},{40,48},{48,56},{56,64},{64,7... | collective-permute-start | bytes 1990664 | tf_op jit(solution)/shard_map/ppermute | solution.py:534
  3.9 19.5 %collective-permute-start.1 = (bf16[2592,128]{1,0:T(8,128)(2,1)S(1)}, bf16[2592,128]{1,0:T(8,128)(2,1)S(1)}, u32[]{:S(2)}, u32[]{:S(2)}) collective-permute-start(bf16[2592,128]{1,0:T(8,128)(2,1)S(1)} %get-tuple-element.25), channel_id=1, source_target_pairs={{0,120},{8,0},{16,8},{24,16},{32,24},{40,32},{48,40},{56,48},{64,5... | collective-permute-start | bytes 1990664 | tf_op jit(solution)/shard_map/ppermute | solution.py:534
  15.5 26.0 %all-to-all-start = ((bf16[8,80,8,128]{3,2,1,0:T(8,128)(2,1)}), bf16[8,80,8,128]{3,2,1,0:T(8,128)(2,1)S(1)}, u32[]{:S(2)}, u32[]{:S(2)}) async-start(bf16[8,80,8,128]{3,2,1,0:T(8,128)(2,1)} %get-tuple-element.12.inner), calls=%async_computation | async-start | bytes 2621440 | tf_op jit(solution)/shard_map/all_to_all | solution.py:565
  41.5 31.9 %copy-start.1 = (f32[1,1024]{1,0:T(1,128)S(1)}, f32[1,1024]{1,0:T(1,128)}, u32[]{:S(2)}) copy-start(f32[1,1024]{1,0:T(1,128)} %observed.1) | copy-start | bytes 12292
  41.5 31.9 %copy-start.2 = (f32[1,1024]{1,0:T(1,128)S(1)}, f32[1,1024]{1,0:T(1,128)}, u32[]{:S(2)}) copy-start(f32[1,1024]{1,0:T(1,128)} %variance.1) | copy-start | bytes 12292
  41.5 34.4 %all-to-all-start.1 = ((bf16[8,80,8,128]{3,2,1,0:T(8,128)(2,1)}), bf16[8,80,8,128]{3,2,1,0:T(8,128)(2,1)S(1)}, u32[]{:S(2)}, u32[]{:S(2)}) async-start(bf16[8,80,8,128]{3,2,1,0:T(8,128)(2,1)} %get-tuple-element.17.edge), calls=%async_computation.1 | async-start | bytes 2621440 | tf_op jit(solution)/shard_map/all_to_all | solution.py:574
  46.1 3.2 %collective-permute-start.2 = (bf16[8,8,128]{2,1,0:T(8,128)(2,1)S(1)}, bf16[8,8,128]{2,1,0:T(8,128)(2,1)S(1)}, u32[]{:S(2)}, u32[]{:S(2)}) collective-permute-start(bf16[8,8,128]{2,1,0:T(8,128)(2,1)S(1)} %get-tuple-element.24), channel_id=1, source_target_pairs={{0,8},{8,16},{16,24},{24,32},{32,40},{40,48},{48,56},{56,64},{64,7... | collective-permute-start | bytes 49160 | tf_op jit(solution)/shard_map/ppermute | solution.py:534
  46.2 3.2 %collective-permute-start.3 = (bf16[8,8,128]{2,1,0:T(8,128)(2,1)S(1)}, bf16[8,8,128]{2,1,0:T(8,128)(2,1)S(1)}, u32[]{:S(2)}, u32[]{:S(2)}) collective-permute-start(bf16[8,8,128]{2,1,0:T(8,128)(2,1)S(1)} %get-tuple-element.23), channel_id=1, source_target_pairs={{0,120},{8,0},{16,8},{24,16},{32,24},{40,32},{48,40},{56,48},{64,5... | collective-permute-start | bytes 49160 | tf_op jit(solution)/shard_map/ppermute | solution.py:534
  49.4 15.3 %collective-permute-start.4 = (bf16[8,8,128]{2,1,0:T(8,128)(2,1)S(1)}, bf16[8,8,128]{2,1,0:T(8,128)(2,1)S(1)}, u32[]{:S(2)}, u32[]{:S(2)}) collective-permute-start(bf16[8,8,128]{2,1,0:T(8,128)(2,1)S(1)} %select_select_fusion.here), channel_id=1, source_target_pairs={{0,4},{1,5},{2,6},{3,7},{4,0},{5,1},{6,2},{7,3},{8,12},{9,13},{10,... | collective-permute-start | bytes 49160 | tf_op jit(solution)/shard_map/ppermute | solution.py:575
  64.7 4.5 %collective-permute-start.5 = (bf16[2,8,8,128]{3,2,1,0:T(8,128)(2,1)S(1)}, bf16[2,8,8,128]{3,2,1,0:T(8,128)(2,1)S(1)}, u32[]{:S(2)}, u32[]{:S(2)}) collective-permute-start(bf16[2,8,8,128]{3,2,1,0:T(8,128)(2,1)S(1)} %pad_maximum_fusion.2), channel_id=1, source_target_pairs={{1,0},{2,1},{3,2},{0,3},{5,4},{6,5},{7,6},{4,7},{9,8},{10,9},{11,1... | collective-permute-start | bytes 98312 | tf_op jit(solution)/shard_map/ppermute | solution.py:538
  67.4 5.4 %collective-permute-start.6 = (bf16[2,8,8,128]{3,2,1,0:T(8,128)(2,1)S(1)}, bf16[2,8,8,128]{3,2,1,0:T(8,128)(2,1)S(1)}, u32[]{:S(2)}, u32[]{:S(2)}) collective-permute-start(bf16[2,8,8,128]{3,2,1,0:T(8,128)(2,1)S(1)} %pad_maximum_fusion.2), channel_id=1, source_target_pairs={{2,0},{3,1},{0,2},{1,3},{6,4},{7,5},{4,6},{5,7},{10,8},{11,9},{8,1... | collective-permute-start | bytes 98312 | tf_op jit(solution)/shard_map/ppermute | solution.py:538
  68.2 5.1 %collective-permute-start.7 = (bf16[2,8,8,128]{3,2,1,0:T(8,128)(2,1)S(1)}, bf16[2,8,8,128]{3,2,1,0:T(8,128)(2,1)S(1)}, u32[]{:S(2)}, u32[]{:S(2)}) collective-permute-start(bf16[2,8,8,128]{3,2,1,0:T(8,128)(2,1)S(1)} %pad_maximum_fusion.2), channel_id=1, source_target_pairs={{3,0},{0,1},{1,2},{2,3},{7,4},{4,5},{5,6},{6,7},{11,8},{8,9},{9,10... | collective-permute-start | bytes 98312 | tf_op jit(solution)/shard_map/ppermute | solution.py:538
